TPU v7x, 32 devices: a whole 2x2x4 slice. The times are simulated.
32 devices in a mesh: dp: 2 (over x), ctx: 4 (over y, core), expert: 4 (over z).
Axes of the slice: x: 2, y: 2, z: 4, core: 2. Of those that a mesh axis runs over, the one named last changes fastest.
Arguments:
- inputs: bfloat16 [2, 8, 512, 2048], P(None, ('dp', 'expert'), 'ctx'), may hold values from -6 to 6
- cotangent: bfloat16 [2, 8, 512, 2048], P(None, ('dp', 'expert'), 'ctx'), may hold values from -6 to 6
- lengths: int32 [2, 8, 3], P(None, ('dp', 'expert')), may hold values from 1 to 448, 512 in all within a row
- block_order: int32 [2, 8, 4], P(None, ('dp', 'expert')), may hold values from 0 to 3, each once within a row
- routes: int32 [2, 8, 512, 8], P(None, ('dp', 'expert'), 'ctx'), may hold values from 0 to 15, all different within a row; in each aligned block of 128 rows (0 to 127, 128 to 255, ..., all dimensions but the last counted through in order) at most 74 rows name the same one
- query_weight: bfloat16 [2048, 2048], P(('dp', 'ctx', 'expert')), may hold values from -0.125 to 0.125
- key_weight: bfloat16 [2048, 2048], P(('dp', 'ctx', 'expert')), may hold values from -0.125 to 0.125
- value_weight: bfloat16 [2048, 2048], P(('dp', 'ctx', 'expert')), may hold values from -0.125 to 0.125
- output_weight: bfloat16 [2048, 2048], P(('dp', 'ctx', 'expert')), may hold values from -1.5 to 1.5
- attention_gain: bfloat16 [2048], P(('dp', 'ctx', 'expert')), may hold values from 0.099609375 to 1.8984375
- mixture_gain: bfloat16 [2048], P(('dp', 'ctx', 'expert')), may hold values from 0.099609375 to 1.8984375
- query_key_gain: bfloat16 [256], P(('dp', 'ctx', 'expert')), may hold values from 0.099609375 to 1.8984375
- router: bfloat16 [2048, 16], P(('dp', 'ctx', 'expert')), may hold values from -0.0625 to 0.0625
- expert_gate: bfloat16 [16, 2048, 1024], P(('ctx', 'expert'), 'dp'), may hold values from -0.125 to 0.125
- expert_up: bfloat16 [16, 2048, 1024], P(('ctx', 'expert'), 'dp'), may hold values from -0.125 to 0.125
- expert_down: bfloat16 [16, 1024, 2048], P(('ctx', 'expert'), 'dp'), may hold values from -1 to 1
Outputs:
- output: bfloat16 [2, 8, 512, 2048], P(None, ('dp', 'expert'), 'ctx')
- input_grad: float32 [2, 8, 512, 2048], P(None, ('dp', 'expert'), 'ctx')
- query_grad: float32 [2048, 2048], P(('dp', 'ctx', 'expert'))
- key_grad: float32 [2048, 2048], P(('dp', 'ctx', 'expert'))
- value_grad: float32 [2048, 2048], P(('dp', 'ctx', 'expert'))
- output_grad: float32 [2048, 2048], P(('dp', 'ctx', 'expert'))
- attention_gain_grad: float32 [2048], P(('dp', 'ctx', 'expert'))
- mixture_gain_grad: float32 [2048], P(('dp', 'ctx', 'expert'))
- query_key_grad: float32 [256], P(('dp', 'ctx', 'expert'))
- router_grad: float32 [2048, 16], P(('dp', 'ctx', 'expert'))
- gate_grad: float32 [16, 2048, 1024], P(('ctx', 'expert'), 'dp')
- up_grad: float32 [16, 2048, 1024], P(('ctx', 'expert'), 'dp')
- down_grad: float32 [16, 1024, 2048], P(('ctx', 'expert'), 'dp')
Inputs may be any that keep to these rules, and one draw needn't show every extreme that they name: The 3 lengths of a group in one micro-batch sum to 512; the longest is 448. `block_order`: in each micro-batch and group a permutation of the 4 blocks. `routes`: each token names 8 different experts; among the tokens of one device in one micro-batch no expert is named more than 74 times, a bound that some block reaches.
All inputs are finite; a program needn't handle non-finite values.
Results may differ from a plain program's by a relative error of at most 0.02.
Values may be sent and summed in bfloat16 or wider, within the bound.
No kernel may reach another device: no remote copies, remote signals or barrier semaphores. Data moves between devices by JAX's collectives and lax.ppermute only.
A program may use at most 320 MiB of HBM per device.

v0:
```python
import jax
import jax.numpy as jnp
from jax import lax
from jax.sharding import PartitionSpec as P

HEADS = 16
DH = 128
BLOCK = 128
HALVES = 2
SMALL = 128

EPSILON = 1e-06
NEGATIVE = -1e30
THETA_BASE = 50000.0
F32 = jnp.float32
BF16 = jnp.bfloat16


def matmul(left_side, right_side):
    return jnp.dot(left_side, right_side, preferred_element_type=F32)


def matmul_t(left_side, right_side):
    return lax.dot_general(
        left_side, right_side, (((1,), (1,)), ((), ())), preferred_element_type=F32
    )


def inner_rows(left_side, right_side):
    return lax.dot_general(
        left_side, right_side, (((0,), (0,)), ((), ())), preferred_element_type=F32
    )


def swap(value, axis, bit):
    return lax.ppermute(value, axis, [(i, i ^ bit) for i in range(4)])


MIDDLE = [(1, 2), (2, 1)]
OUTWARD = [(1, 0), (2, 3)]
INWARD = [(0, 1), (3, 2)]


def gather_ctx(own):
    across = swap(own, "ctx", 2)
    beside = swap(own, "ctx", 1)
    corner = swap(across, "ctx", 1)
    return [own, beside, across, corner]


def scatter_ctx(slots):
    far = slots[2].astype(F32) + swap(slots[3], "ctx", 1).astype(F32)
    near = slots[0].astype(F32) + swap(slots[1], "ctx", 1).astype(F32)
    return near + swap(far.astype(BF16), "ctx", 2).astype(F32)


def gather_line(own):
    pair = swap(own, "expert", 1)
    third_mid = lax.ppermute(own, "expert", MIDDLE)
    second_mid = lax.ppermute(pair, "expert", MIDDLE)
    second_end = lax.ppermute(third_mid, "expert", OUTWARD)
    third_end = lax.ppermute(second_mid, "expert", OUTWARD)
    place = lax.axis_index("expert")
    middle = (place == 1) | (place == 2)
    return [
        own,
        pair,
        jnp.where(middle, second_mid, second_end),
        jnp.where(middle, third_mid, third_end),
    ]


def scatter_line(slots):
    three = lax.ppermute(slots[3].astype(BF16), "expert", INWARD)
    second = slots[2] + three.astype(F32)
    second_low = second.astype(BF16)
    over = lax.ppermute(second_low, "expert", MIDDLE)
    inward = lax.ppermute(second_low, "expert", INWARD)
    first = slots[1] + over.astype(F32)
    third = slots[3] + inward.astype(F32)
    home = lax.ppermute(third.astype(BF16), "expert", MIDDLE)
    pair = swap(first.astype(BF16), "expert", 1)
    return slots[0] + pair.astype(F32) + home.astype(F32)


def gather_both(own):
    line = gather_line(own)
    here = jnp.stack(line + [swap(piece, "ctx", 2) for piece in line])
    return here, swap(here, "ctx", 1)


def scatter_both(here, there):
    received = [swap(there[s], "ctx", 1) for s in range(8)]
    chip = [here[s].astype(F32) + received[s].astype(F32) for s in range(8)]
    across = [swap(chip[4 + s].astype(BF16), "ctx", 2) for s in range(4)]
    return scatter_line([chip[s] + across[s].astype(F32) for s in range(4)])


def places(index, lengths, block_order):
    blocks = jnp.arange(block_order.shape[0], dtype=jnp.int32)
    holder = (index // BLOCK)[:, None] == blocks[None, :]
    logical = (
        jnp.sum(jnp.where(holder, block_order[None, :], 0), axis=1) * BLOCK + index % BLOCK
    )
    seq_ends = jnp.cumsum(lengths)
    segment = jnp.sum((logical[:, None] >= seq_ends[None, :]).astype(jnp.int32), axis=1)
    starts = seq_ends - lengths
    member = segment[:, None] == jnp.arange(lengths.shape[0], dtype=jnp.int32)[None, :]
    seq_first = jnp.sum(jnp.where(member, starts[None, :], 0), axis=1)
    return (segment, (logical - seq_first).astype(F32))


def rotary_tables(positions, half_size):
    frequency = THETA_BASE ** (-(jnp.arange(half_size, dtype=F32) / half_size))
    angles = positions[:, None] * frequency[None, :]
    return (jnp.cos(angles), jnp.sin(angles))


def rotate(values, cosine, sine_table):
    half_size = values.shape[-1] // 2
    first_half = values[..., :half_size]
    second = values[..., half_size:]
    cosine_b = cosine[:, None, :]
    sine_b = sine_table[:, None, :]
    return jnp.concatenate(
        [first_half * cosine_b - second * sine_b, second * cosine_b + first_half * sine_b], axis=-1
    )


def unrotate(values, cosine, sine_table):
    half_size = values.shape[-1] // 2
    first_half = values[..., :half_size]
    second = values[..., half_size:]
    cosine_b = cosine[:, None, :]
    sine_b = sine_table[:, None, :]
    return jnp.concatenate(
        [first_half * cosine_b + second * sine_b, second * cosine_b - first_half * sine_b], axis=-1
    )


def norm_back(upstream, unit_rows, scaling, gain_vector):
    weighted = upstream * gain_vector
    return scaling * (weighted - unit_rows * jnp.mean(weighted * unit_rows, axis=-1, keepdims=True))


def row_scale(rows):
    return lax.rsqrt(jnp.mean(rows * rows, axis=-1, keepdims=True) + EPSILON)


def gather_weights(query_weight, key_weight, value_weight, output_weight, attention_gain, mixture_gain, query_key_gain, router):
    rows, width = query_weight.shape
    ctx_size = lax.axis_size("ctx")
    share = width // (HALVES * ctx_size)
    stacked = jnp.stack([query_weight, key_weight, value_weight], axis=1)
    stacked = stacked.reshape(rows, 3, HALVES, ctx_size, share).transpose(3, 0, 1, 2, 4)
    stacked = stacked.reshape(ctx_size, rows, 3 * HALVES * share)
    few = query_key_gain.shape[0]
    small = jnp.concatenate(
        [
            attention_gain[:, None],
            mixture_gain[:, None],
            jnp.pad(query_key_gain, (0, rows - few))[:, None],
            router,
        ],
        axis=1,
    )
    small = jnp.pad(small, ((0, 0), (0, SMALL - small.shape[1])))
    payload = jnp.concatenate(
        [stacked, jnp.broadcast_to(small[None], (ctx_size, rows, SMALL))], axis=2
    )
    payload = lax.all_to_all(payload, "ctx", split_axis=0, concat_axis=0, tiled=True)
    whole = lax.all_gather(payload, ("dp", "expert"), axis=0, tiled=False)
    dp_size, line = lax.axis_size("dp"), lax.axis_size("expert")
    whole = whole.reshape(dp_size, line, ctx_size, rows, payload.shape[2])
    whole = whole.transpose(0, 2, 1, 3, 4).reshape(-1, payload.shape[2])
    projections = whole[:, : 3 * HALVES * share]
    small = whole[:, 3 * HALVES * share :].astype(F32)
    pair = small[:, 2].reshape(-1, rows)[:, :few].reshape(-1)
    router_all = whole[:, 3 * HALVES * share + 3 : 3 * HALVES * share + 3 + router.shape[1]]
    if whole_heads(dp_size, rows * line, share):
        out_rows = lax.all_gather(output_weight, ("dp", "expert"), axis=0, tiled=True)
    else:
        out_rows = lax.all_gather(output_weight, ("dp", "ctx", "expert"), axis=0, tiled=True)
        out_rows = out_rows.reshape(HALVES, ctx_size, share, -1)
        out_rows = lax.dynamic_index_in_dim(out_rows, lax.axis_index("ctx"), 1, keepdims=False)
        out_rows = out_rows.reshape(HALVES * share, -1)
    return projections, out_rows, small[:, 0], small[:, 1], pair[:DH], pair[DH:], router_all


def whole_heads(dp_size, line_rows, share):
    return dp_size == HALVES and line_rows == share


def scatter_grads(projections, small_columns, out_rows, rows, few):
    ctx_size, dp_size, line = lax.axis_size("ctx"), lax.axis_size("dp"), lax.axis_size("expert")
    width = projections.shape[0]
    share = out_rows.shape[0] // HALVES
    small = jnp.pad(small_columns, ((0, 0), (0, SMALL - small_columns.shape[1])))
    payload = jnp.concatenate([projections, small], axis=1).astype(BF16)
    columns = payload.shape[1]
    payload = payload.reshape(dp_size, ctx_size, line, rows, columns).transpose(0, 2, 1, 3, 4)
    payload = payload.reshape(dp_size * line * ctx_size, rows, columns)
    payload = lax.psum_scatter(payload, ("dp", "expert"), scatter_dimension=0, tiled=True)
    payload = lax.all_to_all(payload, "ctx", split_axis=0, concat_axis=0, tiled=True)
    parts = payload[:, :, : 3 * HALVES * share].reshape(ctx_size, rows, 3, HALVES, share)
    parts = parts.transpose(2, 1, 3, 0, 4).reshape(3, rows, width).astype(F32)
    small = jnp.sum(payload[:, :, 3 * HALVES * share :].astype(F32), axis=0)
    if whole_heads(dp_size, rows * line, share):
        out_part = lax.psum_scatter(
            out_rows.astype(BF16), ("dp", "expert"), scatter_dimension=0, tiled=True
        )
    else:
        place = lax.axis_index("ctx")
        spread = jnp.zeros((HALVES, ctx_size, share, width), BF16)
        spread = lax.dynamic_update_slice_in_dim(
            spread, out_rows.astype(BF16).reshape(HALVES, 1, share, width), place, 1
        )
        out_part = lax.psum_scatter(
            spread.reshape(-1, width), ("dp", "ctx", "expert"), scatter_dimension=0, tiled=True
        )
    return parts[0], parts[1], parts[2], out_part.astype(F32), small[:, 0], small[:, 1], small[:few, 2], small[:, 3:]


def attention_forward(stream, weights, tables):
    projections, _, attention_gain, _, query_gain, key_gain, _ = weights
    segment, cosine, sine_table = tables
    tokens = stream.shape[0]
    heads = projections.shape[1] // (3 * DH)
    unit = stream * row_scale(stream)
    normed = (unit * attention_gain).astype(BF16)
    joined = matmul(normed, projections).reshape(tokens, 3, heads, DH)
    query_rows, key_rows = joined[:, 0], joined[:, 1]
    valued = joined[:, 2].astype(BF16)
    query_scale = row_scale(query_rows)
    key_scale = row_scale(key_rows)
    query_unit = query_rows * query_scale
    key_unit = key_rows * key_scale
    query_rot = rotate(query_unit * query_gain, cosine, sine_table).astype(BF16)
    key_rot = rotate(key_unit * key_gain, cosine, sine_table).astype(BF16)
    scores = jnp.einsum("qhd,khd->hqk", query_rot, key_rot, preferred_element_type=F32) * DH ** (-0.5)
    scores = jnp.where((segment[:, None] == segment[None, :])[None], scores, NEGATIVE)
    powers = jnp.exp(scores - jnp.max(scores, axis=-1, keepdims=True))
    probs = powers / jnp.sum(powers, axis=-1, keepdims=True)
    attended = jnp.einsum("hqk,khd->qhd", probs.astype(BF16), valued, preferred_element_type=F32)
    attended = attended.reshape(tokens, heads * DH).astype(BF16)
    return attended, (normed, unit, query_scale, query_unit, key_scale, key_unit, query_rot, key_rot, valued, probs)


def attention_backward(branch_grad, saved, weights, tables):
    projections, out_rows, _, _, query_gain, key_gain, _ = weights
    _, cosine, sine_table = tables
    normed, unit, query_scale, query_unit, key_scale, key_unit, query_rot, key_rot, valued, probs = saved
    tokens, heads = query_rot.shape[0], query_rot.shape[1]
    attended_grad = matmul_t(branch_grad, out_rows).astype(BF16).reshape(tokens, heads, DH)
    prob_grad = jnp.einsum("qhd,khd->hqk", attended_grad, valued, preferred_element_type=F32)
    score_grad = (
        probs * (prob_grad - jnp.sum(probs * prob_grad, axis=-1, keepdims=True))
    ).astype(BF16)
    query_rot_grad = jnp.einsum("hqk,khd->qhd", score_grad, key_rot, preferred_element_type=F32)
    key_rot_grad = jnp.einsum("hqk,qhd->khd", score_grad, query_rot, preferred_element_type=F32)
    value_grad = jnp.einsum(
        "hqk,qhd->khd", probs.astype(BF16), attended_grad, preferred_element_type=F32
    ).astype(BF16)
    query_rot_grad = (query_rot_grad * DH ** (-0.5)).astype(BF16).astype(F32)
    key_rot_grad = (key_rot_grad * DH ** (-0.5)).astype(BF16).astype(F32)
    query_norm_grad = unrotate(query_rot_grad, cosine, sine_table)
    key_norm_grad = unrotate(key_rot_grad, cosine, sine_table)
    gain_pair = jnp.concatenate(
        [
            jnp.sum(query_norm_grad * query_unit, axis=(0, 1)),
            jnp.sum(key_norm_grad * key_unit, axis=(0, 1)),
        ]
    )
    query_grad = norm_back(query_norm_grad, query_unit, query_scale, query_gain)
    key_grad = norm_back(key_norm_grad, key_unit, key_scale, key_gain)
    joined = jnp.concatenate(
        [
            query_grad.astype(BF16).reshape(tokens, -1),
            key_grad.astype(BF16).reshape(tokens, -1),
            value_grad.reshape(tokens, -1),
        ],
        axis=1,
    )
    normed_grad = matmul_t(joined, projections)
    attention_gain_grad = jnp.sum(normed_grad * unit, axis=0)
    return joined, normed_grad.astype(BF16), attention_gain_grad, gain_pair


def chosen_gates(normed, router, chosen):
    logits = jnp.where(chosen, matmul(normed, router), NEGATIVE)
    powers = jnp.where(chosen, jnp.exp(logits - jnp.max(logits, axis=1, keepdims=True)), 0.0)
    return powers / jnp.sum(powers, axis=1, keepdims=True)


def pick_rows(onehot, blocks):
    return jnp.einsum("bsj,bjd->bsd", onehot, blocks, preferred_element_type=F32).astype(BF16)


def place_rows(onehot, rows):
    return jnp.einsum("bsj,bsd->bjd", onehot, rows, preferred_element_type=F32).astype(BF16)


def expert_pass(normed, upstream, chosen, router, gate_full, up_full, down_full, expert, capacity):
    blocks, tokens, width = normed.shape
    gates = chosen_gates(
        normed.reshape(-1, width), router, chosen.reshape(blocks * tokens, -1)
    ).reshape(blocks, tokens, -1)
    mine = jnp.arange(gates.shape[2], dtype=jnp.int32) == expert
    gate_here = jnp.sum(jnp.where(mine, gates, 0.0), axis=2)
    here = jnp.any(chosen & mine, axis=2)
    slot = jnp.cumsum(here.astype(jnp.int32), axis=1) - 1
    onehot = (
        slot[:, None, :] == jnp.arange(capacity, dtype=jnp.int32)[None, :, None]
    ) & here[:, None, :]
    gate_rows = jnp.sum(jnp.where(onehot, gate_here[:, None, :], 0.0), axis=2)
    gate_rows = gate_rows.reshape(-1, 1)
    onehot = onehot.astype(BF16)
    rows_in = pick_rows(onehot, normed).reshape(-1, width)
    rows_up = pick_rows(onehot, upstream).reshape(-1, width)
    gate_pre = matmul(rows_in, gate_full)
    up_pre = matmul(rows_in, up_full)
    sigma = jax.nn.sigmoid(gate_pre)
    hidden = (gate_pre * sigma * up_pre).astype(BF16)
    produced = matmul(hidden, down_full).astype(BF16).astype(F32)
    gate_grad = jnp.sum(produced * rows_up.astype(F32), axis=1).reshape(blocks, capacity)
    gate_grad = jnp.einsum("bsj,bs->bj", onehot.astype(F32), gate_grad, precision=lax.Precision.HIGHEST)
    shared = place_rows(onehot, (gate_rows * produced).astype(BF16).reshape(blocks, capacity, width))
    out_grad = (gate_rows * rows_up.astype(F32)).astype(BF16)
    hidden_grad = matmul_t(out_grad, down_full)
    gate_pre_grad = (hidden_grad * up_pre * sigma * (1.0 + gate_pre * (1.0 - sigma))).astype(BF16)
    up_pre_grad = (hidden_grad * gate_pre * sigma).astype(BF16)
    rows_grad = (matmul_t(gate_pre_grad, gate_full) + matmul_t(up_pre_grad, up_full)).astype(BF16)
    back = place_rows(onehot, rows_grad.reshape(blocks, capacity, width))
    return shared, back, gate_grad, (rows_in, hidden, out_grad, gate_pre_grad, up_pre_grad)


def body(
    inputs,
    cotangent,
    lengths,
    block_order,
    routes,
    query_weight,
    key_weight,
    value_weight,
    output_weight,
    attention_gain,
    mixture_gain,
    query_key_gain,
    router,
    expert_gate,
    expert_up,
    expert_down,
):
    micro_count, _, tokens, width = inputs.shape
    top = routes.shape[3]
    expert_count = router.shape[1]
    most = tokens * top * 9 // (8 * expert_count) + 2
    capacity = -(-most // 16) * 16
    place, line = lax.axis_index("ctx"), lax.axis_index("expert")
    line_size = lax.axis_size("expert")
    ctx_size = lax.axis_size("ctx")
    few = query_key_gain.shape[0]
    weights = gather_weights(
        query_weight, key_weight, value_weight, output_weight, attention_gain, mixture_gain, query_key_gain, router
    )
    projections, out_rows, _, mixture_all, _, _, router_all = weights
    gate_full = lax.all_gather(expert_gate[0], "dp", axis=0, tiled=True)
    up_full = lax.all_gather(expert_up[0], "dp", axis=0, tiled=True)
    down_full = lax.all_gather(expert_down[0], "dp", axis=0, tiled=True)

    routes_all = lax.all_gather(routes[:, 0], ("ctx", "expert"), axis=0, tiled=False)
    routes_all = routes_all.reshape(ctx_size, line_size, micro_count, tokens, top)
    ctx_order = [place ^ s for s in (0, 2, 1, 3)]
    line_order = [line ^ s for s in range(4)]
    ordered = jnp.stack([routes_all[a, b] for a in ctx_order for b in line_order])
    chosen_all = jnp.any(
        ordered[..., None] == jnp.arange(expert_count, dtype=jnp.int32), axis=3
    )
    chosen_own = jnp.any(
        routes[:, 0][..., None] == jnp.arange(expert_count, dtype=jnp.int32), axis=2
    )

    index = jnp.concatenate(
        [(place ^ s) * tokens + jnp.arange(tokens, dtype=jnp.int32) for s in range(4)]
    )
    stream_all = jnp.concatenate(gather_ctx(inputs[:, 0]), axis=1).astype(F32)
    upstream_all = [gather_both(cotangent[m, 0]) for m in range(micro_count)]

    outputs, residual_grads, attention_saved, expert_saved = [], [], [], []
    out_terms = jnp.zeros_like(out_rows, F32)
    mixture_gain_grad = jnp.zeros((width,), F32)
    router_grad = jnp.zeros((width, expert_count), F32)
    tables_list = []
    for m in range(micro_count):
        segment, position = places(index, lengths[m, 0], block_order[m, 0])
        tables = (segment,) + rotary_tables(position, DH // 2)
        tables_list.append(tables)
        attended, saved = attention_forward(stream_all[m], weights, tables)
        attention_saved.append((attended, saved))
        terms = matmul(attended, out_rows).astype(BF16).reshape(4, tokens, width)
        residual = inputs[m, 0].astype(F32) + scatter_ctx([terms[s] for s in range(4)])
        scale_two = row_scale(residual)
        unit_two = residual * scale_two
        normed_two = (unit_two * mixture_all).astype(BF16)
        here, there = gather_both(normed_two)
        normed_all = jnp.concatenate([here, there])
        shared, back, gate_grad, kept = expert_pass(
            normed_all,
            jnp.concatenate(upstream_all[m]),
            chosen_all[:, m],
            router_all,
            gate_full,
            up_full,
            down_full,
            place * line_size + line,
            capacity,
        )
        expert_saved.append(kept)
        half = shared.shape[0] // 2
        outputs.append((residual + scatter_both(shared[:half], shared[half:])).astype(BF16))
        ordered_grad = gate_grad.reshape(ctx_size, line_size, tokens)
        ordered_grad = jnp.stack(
            [ordered_grad[((a ^ place) >> 1) + 2 * ((a ^ place) & 1)] for a in range(4)]
        )
        ordered_grad = jnp.stack([ordered_grad[:, b ^ line] for b in range(4)], axis=1)
        gate_value_grad = lax.all_to_all(
            ordered_grad.reshape(-1, tokens), ("ctx", "expert"), split_axis=0, concat_axis=0, tiled=True
        ).T
        gates = chosen_gates(normed_two, router_all, chosen_own[m])
        select_grad = gates * (
            gate_value_grad - jnp.sum(gates * gate_value_grad, axis=1, keepdims=True)
        )
        logit_grad = select_grad.astype(BF16)
        router_grad = router_grad + inner_rows(normed_two, logit_grad)
        normed_grad = scatter_both(back[:half], back[half:]) + matmul_t(logit_grad, router_all)
        mixture_gain_grad = mixture_gain_grad + jnp.sum(normed_grad * unit_two, axis=0)
        residual_grads.append(
            cotangent[m, 0].astype(F32) + norm_back(normed_grad, unit_two, scale_two, mixture_all)
        )

    joined_list, normed_list, input_grads = [], [], []
    attention_gain_grad = jnp.zeros((width,), F32)
    gain_pair = jnp.zeros((2 * DH,), F32)
    for m in range(micro_count):
        branch_grad = jnp.concatenate(gather_ctx(residual_grads[m].astype(BF16)))
        attended, saved = attention_saved[m]
        out_terms = out_terms + inner_rows(attended, branch_grad)
        joined, normed_grad, gain_part, pair_part = attention_backward(
            branch_grad, saved, weights, tables_list[m]
        )
        joined_list.append(joined)
        normed_list.append(saved[0])
        attention_gain_grad = attention_gain_grad + gain_part
        gain_pair = gain_pair + pair_part
        terms = normed_grad.reshape(4, tokens, width)
        normed_grad = scatter_ctx([terms[s] for s in range(4)])
        stream = inputs[m, 0].astype(F32)
        scale_one = row_scale(stream)
        input_grads.append(
            residual_grads[m] + norm_back(normed_grad, stream * scale_one, scale_one, weights[2])
        )

    projection_grad = inner_rows(jnp.concatenate(normed_list), jnp.concatenate(joined_list))
    rows = query_weight.shape[0]
    pair_column = jnp.pad(gain_pair.reshape(-1, few), ((0, 0), (0, rows - few))).reshape(-1)
    small_columns = jnp.concatenate(
        [attention_gain_grad[:, None], mixture_gain_grad[:, None], pair_column[:, None], router_grad], axis=1
    )
    reduced = scatter_grads(projection_grad, small_columns, out_terms, rows, few)

    rows_in, hidden, out_grad, gate_pre_grad, up_pre_grad = [
        jnp.concatenate(parts) for parts in zip(*expert_saved)
    ]
    gate_sum, up_sum, down_sum = [
        lax.psum_scatter(
            inner_rows(a, b).astype(BF16), "dp", scatter_dimension=0, tiled=True
        ).astype(F32)[None]
        for a, b in ((rows_in, gate_pre_grad), (rows_in, up_pre_grad), (hidden, out_grad))
    ]
    return (
        jnp.stack(outputs)[:, None],
        jnp.stack(input_grads)[:, None],
        reduced[0],
        reduced[1],
        reduced[2],
        reduced[3],
        reduced[4],
        reduced[5],
        reduced[6],
        reduced[7][:, :expert_count],
        gate_sum,
        up_sum,
        down_sum,
    )


def solution(mesh):
    tokens_4 = P(None, ("dp", "expert"), "ctx", None)
    group = P(None, ("dp", "expert"), None)
    matrix = P(("dp", "ctx", "expert"), None)
    vector = P(("dp", "ctx", "expert"))
    experts = P(("ctx", "expert"), "dp", None)
    return jax.shard_map(
        body,
        mesh=mesh,
        in_specs=(tokens_4, tokens_4, group, group, tokens_4)
        + (matrix,) * 4
        + (vector,) * 3
        + (matrix,)
        + (experts,) * 3,
        out_specs=(tokens_4, tokens_4)
        + (matrix,) * 4
        + (vector,) * 3
        + (matrix,)
        + (experts,) * 3,
        check_vma=False,
    )
```

profile of v0, /device:TPU:0, one launch (start us, length us, event | category | flops | bytes accessed | tf_op | source)
XLA Modules:
  0.0 1343.4 jit_solution(13217520407268565653)
XLA Ops:
  13.2 16.6 %all_to_all.34 = bf16[4,64,1664]{2,1,0:T(8,128)(2,1)} all-to-all(bf16[4,64,1664]{2,1,0:T(8,128)(2,1)S(1)} %pad_maximum_fusion.14), channel_id=1, replica_groups=mesh['dp'=2,'ctx'=4,'expert'=4] {'ctx'}, dimensions={0} | all-to-all | bytes 1703936 | tf_op jit(solution)/shard_map/all_to_all | solution.py:171
  42.1 74.2 %all-gather.1 = s32[32,1,128,8]{2,3,1,0:T(8,128)S(1)} all-gather(s32[2,1,128,8]{2,3,1,0:T(8,128)S(1)} %copy-done.113), channel_id=3, replica_groups=mesh['dp'=2,'ctx'=4,'expert'=4] {'ctx','expert'}, dimensions={0}, use_global_device_ids=true | all-gather | bytes 139264 | tf_op jit(solution)/shard_map/all_gather | solution.py:372
  133.9 26.5 %collective-permute-done.99 = bf16[128,2048]{1,0:T(8,128)(2,1)S(1)} collective-permute-done((bf16[128,2048]{1,0:T(8,128)(2,1)}, bf16[128,2048]{1,0:T(8,128)(2,1)S(1)}, u32[]{:S(2)}, u32[]{:S(2)}) %collective-permute-start.99) | collective-permute-done | bytes 524320 | tf_op jit(solution)/shard_map/ppermute | solution.py:61
  164.8 23.0 %collective-permute-done.66 = bf16[128,2048]{1,0:T(8,128)(2,1)S(1)} collective-permute-done((bf16[128,2048]{1,0:T(8,128)(2,1)}, bf16[128,2048]{1,0:T(8,128)(2,1)S(1)}, u32[]{:S(2)}, u32[]{:S(2)}) %collective-permute-start.66) | collective-permute-done | bytes 524320 | tf_op jit(solution)/shard_map/ppermute | solution.py:61
  192.3 16.0 %collective-permute-done.100 = bf16[128,2048]{1,0:T(8,128)(2,1)S(1)} collective-permute-done((bf16[128,2048]{1,0:T(8,128)(2,1)S(1)}, bf16[128,2048]{1,0:T(8,128)(2,1)S(1)}, u32[]{:S(2)}, u32[]{:S(2)}) %collective-permute-start.100) | collective-permute-done | bytes 524320 | tf_op jit(solution)/shard_map/ppermute | solution.py:62
  209.6 16.1 %collective-permute-done.67 = bf16[128,2048]{1,0:T(8,128)(2,1)S(1)} collective-permute-done((bf16[128,2048]{1,0:T(8,128)(2,1)S(1)}, bf16[128,2048]{1,0:T(8,128)(2,1)S(1)}, u32[]{:S(2)}, u32[]{:S(2)}) %collective-permute-start.67) | collective-permute-done | bytes 524320 | tf_op jit(solution)/shard_map/ppermute | solution.py:62
  233.0 7.7 collective-permute-done.102
  243.9 8.0 collective-permute-done.103
  279.8 8.8 copy.192
  288.7 7.8 fusion.81
  352.6 8.4 collective-permute-done.35
  361.0 10.4 collective-permute-done.5
  380.7 8.6 collective-permute-done.36
  392.2 8.4 collective-permute-done.6
  413.7 16.5 %collective-permute-done.9 = bf16[128,2048]{1,0:T(8,128)(2,1)S(1)} collective-permute-done((bf16[128,2048]{1,0:T(8,128)(2,1)S(1)}, bf16[128,2048]{1,0:T(8,128)(2,1)S(1)}, u32[]{:S(2)}, u32[]{:S(2)}) %collective-permute-start.9) | collective-permute-done | bytes 524320 | tf_op jit(solution)/shard_map/ppermute | solution.py:61
  432.9 9.0 collective-permute-done.40
  455.3 10.9 collective-permute-done.42
  468.3 9.2 collective-permute-done.43
  490.8 20.4 %collective-permute-done.44 = bf16[128,2048]{1,0:T(8,128)(2,1)S(1)} collective-permute-done((bf16[128,2048]{1,0:T(8,128)(2,1)S(1)}, bf16[128,2048]{1,0:T(8,128)(2,1)S(1)}, u32[]{:S(2)}, u32[]{:S(2)}) %collective-permute-start.44) | collective-permute-done | bytes 524320 | tf_op jit(solution)/shard_map/ppermute | solution.py:36
  569.8 10.3 fusion.39
  580.1 10.3 fusion.47
  596.1 13.7 %multiply_convert_fusion = (bf16[1280,1024]{1,0:T(8,128)(2,1)S(1)}, bf16[1280,1024]{1,0:T(8,128)(2,1)S(1)}, bf16[1280,1024]{1,0:T(8,128)(2,1)S(1)}) fusion(f32[1280,1024]{1,0:T(8,128)} %fusion.47, f32[1280,1024]{1,0:T(8,128)} %fusion.39, bf16[1280,2048]{1,0:T(8,128)(2,1)} %fusion.6, bf16[1,1024,2048]{2,1,0:T(8,128)(2,1)} %all-gather.19.cloned.1.call-done), kind=kOutput, calls=%fused_computation.40 | convolution fusion | flops 5389680640 | bytes 27787264 | tf_op jit(solution)/shard_map/dot_general | solution.py:24
  609.8 10.5 fusion.7
  629.0 8.3 fusion.43
  637.3 8.6 add_convert_fusion
  655.2 9.9 fusion.41
  672.5 12.7 multiply_convert_fusion.2
  685.2 11.0 fusion.45
  696.2 8.7 add_convert_fusion.1
  716.0 11.0 fusion.5
  751.3 8.5 collective-permute-done.117
  763.1 7.8 collective-permute-done.57
  826.0 8.3 collective-permute-done.88
  858.0 10.3 collective-permute-done.78
  925.1 14.4 %fusion.55 = bf16[2048,1024]{1,0:T(8,128)(2,1)} fusion(bf16[1280,1024]{1,0:T(8,128)(2,1)} %copy-done.177, bf16[1280,1024]{1,0:T(8,128)(2,1)} %get-tuple-element.160, bf16[1280,2048]{1,0:T(8,128)(2,1)S(1)} %bitcast.851, bf16[1280,2048]{1,0:T(8,128)(2,1)S(1)} %bitcast.859), kind=kOutput, calls=%fused_computation.103 | convolution fusion | flops 10770972672 | bytes 19922944 | tf_op jit(solution)/shard_map/dot_general | solution.py:30
  941.9 12.4 collective-permute-done.91
  983.1 10.6 multiply_convert_fusion.7
  995.1 9.8 convolution_convert_fusion
  1009.1 17.0 %fusion.52 = bf16[2048,1024]{1,0:T(8,128)(2,1)} fusion(bf16[1280,1024]{1,0:T(8,128)(2,1)} %copy-done.182, bf16[1280,1024]{1,0:T(8,128)(2,1)} %get-tuple-element.161, bf16[1280,2048]{1,0:T(8,128)(2,1)} %bitcast.848, bf16[1280,2048]{1,0:T(8,128)(2,1)} %bitcast.852), kind=kOutput, calls=%fused_computation.102 | convolution fusion | flops 10770972672 | bytes 19922944 | tf_op jit(solution)/shard_map/dot_general | solution.py:30
  1046.2 15.1 %fusion.58 = bf16[1024,2048]{1,0:T(8,128)(2,1)} fusion(bf16[1280,2048]{1,0:T(8,128)(2,1)S(1)} %bitcast.873, bf16[1280,2048]{1,0:T(8,128)(2,1)} %copy-done.32, bf16[1280,1024]{1,0:T(8,128)(2,1)S(1)} %copy-done.180, bf16[1280,1024]{1,0:T(8,128)(2,1)S(1)} %copy-done.181), kind=kOutput, calls=%fused_computation.104 | convolution fusion | flops 10770972672 | bytes 19922944 | tf_op jit(solution)/shard_map/dot_general | solution.py:30
  1090.0 9.7 collective-permute-done.31
  1106.1 11.0 collective-permute-done.21
  1120.3 8.0 collective-permute-done.128
  1130.9 8.8 collective-permute-done.95
  1140.5 8.4 collective-permute-done.18
  1162.3 34.9 %reduce-scatter.10.cloned.1.call-done = bf16[1024,1024]{1,0:T(8,128)(2,1)} async-done(((bf16[2048,1024]{1,0:T(8,128)(2,1)}), bf16[1024,1024]{1,0:T(8,128)(2,1)}) %reduce-scatter.10.cloned.1.call-update) | async-done | bytes 2097168 | tf_op jit(solution)/shard_map/reduce_scatter | solution.py:476
  1201.2 67.3 %reduce-scatter.8.cloned.1.call-done = bf16[64,2048]{1,0:T(8,128)(2,1)} async-done(((bf16[512,2048]{1,0:T(8,128)(2,1)}), bf16[64,2048]{1,0:T(8,128)(2,1)}) %reduce-scatter.8.cloned.1.call-update) | async-done | bytes 262160 | tf_op jit(solution)/shard_map/reduce_scatter | solution.py:209
  1270.3 53.7 %reduce-scatter.14.cloned.1.call-done = bf16[512,2048]{1,0:T(8,128)(2,1)} async-done(((bf16[1024,2048]{1,0:T(8,128)(2,1)}), bf16[512,2048]{1,0:T(8,128)(2,1)}) %reduce-scatter.14.cloned.1.call-update) | async-done | bytes 2097168 | tf_op jit(solution)/shard_map/reduce_scatter | solution.py:476
  (960 shorter events, 587.6 us)
Async XLA Ops:
  7.2 262.7 %all-gather.13.cloned.1.call-start = ((), (), s32[]{:S(2)}) async-start(), calls=%async_computation.15 | async-start | bytes 7667712 | tf_op jit(solution)/shard_map/all_gather | solution.py:172
  29.9 296.6 %all-gather.11.cloned.1.call-start = ((), (), s32[]{:S(2)}) async-start(), calls=%async_computation.9 | async-start | bytes 2359296 | tf_op jit(solution)/shard_map/all_gather | solution.py:181
  30.7 539.1 %all-gather.17.cloned.1.call-start = ((), (), s32[]{:S(2)}) async-start(), calls=%async_computation.17 | async-start | bytes 6291456 | tf_op jit(solution)/shard_map/all_gather | solution.py:369
  31.4 548.7 %all-gather.15.cloned.1.call-start = ((), (), s32[]{:S(2)}) async-start(), calls=%async_computation.16 | async-start | bytes 6291456 | tf_op jit(solution)/shard_map/all_gather | solution.py:368
  32.0 564.1 %all-gather.19.cloned.1.call-start = ((), (), s32[]{:S(2)}) async-start(), calls=%async_computation.18 | async-start | bytes 6291456 | tf_op jit(solution)/shard_map/all_gather | solution.py:370
  33.1 93.0 %collective-permute-start.96 = (bf16[128,2048]{1,0:T(8,128)(2,1)}, bf16[128,2048]{1,0:T(8,128)(2,1)}, u32[]{:S(2)}, u32[]{:S(2)}) collective-permute-start(bf16[128,2048]{1,0:T(8,128)(2,1)} %get-tuple-element.281), channel_id=1, source_target_pairs={{0,1},{1,0},{2,3},{3,2},{4,5},{5,4},{6,7},{7,6},{8,9},{9,8},{10,11... | collective-permute-start | bytes 1572872 | tf_op jit(solution)/shard_map/ppermute | solution.py:36
  35.1 91.7 %collective-permute-start.98 = (bf16[128,2048]{1,0:T(8,128)(2,1)}, bf16[128,2048]{1,0:T(8,128)(2,1)}, u32[]{:S(2)}, u32[]{:S(2)}) collective-permute-start(bf16[128,2048]{1,0:T(8,128)(2,1)} %get-tuple-element.281), channel_id=1, source_target_pairs={{1,2},{2,1},{5,6},{6,5},{9,10},{10,9},{13,14},{14,13},{17,18},{18,... | collective-permute-start | bytes 1572872 | tf_op jit(solution)/shard_map/ppermute | solution.py:59
  36.5 192.9 %collective-permute-start.101 = (bf16[128,2048]{1,0:T(8,128)(2,1)}, bf16[128,2048]{1,0:T(8,128)(2,1)}, u32[]{:S(2)}, u32[]{:S(2)}) collective-permute-start(bf16[128,2048]{1,0:T(8,128)(2,1)} %get-tuple-element.281), channel_id=1, source_target_pairs={{0,8},{4,12},{8,0},{12,4},{1,9},{5,13},{9,1},{13,5},{2,10},{6,14},... | collective-permute-start | bytes 1572872 | tf_op jit(solution)/shard_map/ppermute | solution.py:36
  36.9 93.3 %collective-permute-start.63 = (bf16[128,2048]{1,0:T(8,128)(2,1)}, bf16[128,2048]{1,0:T(8,128)(2,1)S(1)}, u32[]{:S(2)}, u32[]{:S(2)}) collective-permute-start(bf16[128,2048]{1,0:T(8,128)(2,1)} %get-tuple-element.280), channel_id=1, source_target_pairs={{0,1},{1,0},{2,3},{3,2},{4,5},{5,4},{6,7},{7,6},{8,9},{9,8},{10,11... | collective-permute-start | bytes 1572872 | tf_op jit(solution)/shard_map/ppermute | solution.py:36
  40.6 92.6 %collective-permute-start.65 = (bf16[128,2048]{1,0:T(8,128)(2,1)}, bf16[128,2048]{1,0:T(8,128)(2,1)}, u32[]{:S(2)}, u32[]{:S(2)}) collective-permute-start(bf16[128,2048]{1,0:T(8,128)(2,1)} %get-tuple-element.280), channel_id=1, source_target_pairs={{1,2},{2,1},{5,6},{6,5},{9,10},{10,9},{13,14},{14,13},{17,18},{18,... | collective-permute-start | bytes 1572872 | tf_op jit(solution)/shard_map/ppermute | solution.py:59
  126.7 33.7 %collective-permute-start.99 = (bf16[128,2048]{1,0:T(8,128)(2,1)}, bf16[128,2048]{1,0:T(8,128)(2,1)S(1)}, u32[]{:S(2)}, u32[]{:S(2)}) collective-permute-start(bf16[128,2048]{1,0:T(8,128)(2,1)} %collective-permute-done.98), channel_id=1, source_target_pairs={{1,0},{2,3},{5,4},{6,7},{9,8},{10,11},{13,12},{14,15},{17,16},{18,... | collective-permute-start | bytes 1572872 | tf_op jit(solution)/shard_map/ppermute | solution.py:61
  131.0 111.5 %collective-permute-start.1 = (bf16[2,128,2048]{2,1,0:T(8,128)(2,1)S(1)}, bf16[2,128,2048]{2,1,0:T(8,128)(2,1)S(1)}, u32[]{:S(2)}, u32[]{:S(2)}) collective-permute-start(bf16[2,128,2048]{2,1,0:T(8,128)(2,1)S(1)} %bitcast.860), channel_id=1, source_target_pairs={{0,8},{4,12},{8,0},{12,4},{1,9},{5,13},{9,1},{13,5},{2,10},{6,14},... | collective-permute-start | bytes 3145736 | tf_op jit(solution)/shard_map/ppermute | solution.py:36
  133.2 131.8 %collective-permute-start = (bf16[2,128,2048]{2,1,0:T(8,128)(2,1)S(1)}, bf16[2,128,2048]{2,1,0:T(8,128)(2,1)S(1)}, u32[]{:S(2)}, u32[]{:S(2)}) collective-permute-start(bf16[2,128,2048]{2,1,0:T(8,128)(2,1)S(1)} %bitcast.861), channel_id=1, source_target_pairs={{0,4},{4,0},{8,12},{12,8},{1,5},{5,1},{9,13},{13,9},{2,6},{6,2},{1... | collective-permute-start | bytes 3145736 | tf_op jit(solution)/shard_map/ppermute | solution.py:36
  133.2 30.3 %collective-permute-start.64 = (bf16[128,2048]{1,0:T(8,128)(2,1)}, bf16[128,2048]{1,0:T(8,128)(2,1)S(1)}, u32[]{:S(2)}, u32[]{:S(2)}) collective-permute-start(bf16[128,2048]{1,0:T(8,128)(2,1)} %copy-done.66), channel_id=1, source_target_pairs={{1,2},{2,1},{5,6},{6,5},{9,10},{10,9},{13,14},{14,13},{17,18},{18,... | collective-permute-start | bytes 1572872 | tf_op jit(solution)/shard_map/ppermute | solution.py:60
  163.5 44.8 %collective-permute-start.100 = (bf16[128,2048]{1,0:T(8,128)(2,1)S(1)}, bf16[128,2048]{1,0:T(8,128)(2,1)S(1)}, u32[]{:S(2)}, u32[]{:S(2)}) collective-permute-start(bf16[128,2048]{1,0:T(8,128)(2,1)S(1)} %collective-permute-done.97), channel_id=1, source_target_pairs={{1,0},{2,3},{5,4},{6,7},{9,8},{10,11},{13,12},{14,15},{17,16},{18,... | collective-permute-start | bytes 1572872 | tf_op jit(solution)/shard_map/ppermute | solution.py:62
  187.8 37.9 %collective-permute-start.67 = (bf16[128,2048]{1,0:T(8,128)(2,1)S(1)}, bf16[128,2048]{1,0:T(8,128)(2,1)S(1)}, u32[]{:S(2)}, u32[]{:S(2)}) collective-permute-start(bf16[128,2048]{1,0:T(8,128)(2,1)S(1)} %collective-permute-done.64), channel_id=1, source_target_pairs={{1,0},{2,3},{5,4},{6,7},{9,8},{10,11},{13,12},{14,15},{17,16},{18,... | collective-permute-start | bytes 1572872 | tf_op jit(solution)/shard_map/ppermute | solution.py:62
  208.4 46.6 %collective-permute-start.68 = (bf16[128,2048]{1,0:T(8,128)(2,1)}, bf16[128,2048]{1,0:T(8,128)(2,1)S(1)}, u32[]{:S(2)}, u32[]{:S(2)}) collective-permute-start(bf16[128,2048]{1,0:T(8,128)(2,1)} %get-tuple-element.280), channel_id=1, source_target_pairs={{0,8},{4,12},{8,0},{12,4},{1,9},{5,13},{9,1},{13,5},{2,10},{6,14},... | collective-permute-start | bytes 1572872 | tf_op jit(solution)/shard_map/ppermute | solution.py:36
  242.5 99.5 %collective-permute-start.70 = (bf16[128,2048]{1,0:T(8,128)(2,1)}, bf16[128,2048]{1,0:T(8,128)(2,1)}, u32[]{:S(2)}, u32[]{:S(2)}) collective-permute-start(bf16[128,2048]{1,0:T(8,128)(2,1)} %get-tuple-element.139), channel_id=1, source_target_pairs={{0,8},{4,12},{8,0},{12,4},{1,9},{5,13},{9,1},{13,5},{2,10},{6,14},... | collective-permute-start | bytes 1572872 | tf_op jit(solution)/shard_map/ppermute | solution.py:36
  255.0 92.9 %collective-permute-start.104 = (bf16[128,2048]{1,0:T(8,128)(2,1)}, bf16[128,2048]{1,0:T(8,128)(2,1)}, u32[]{:S(2)}, u32[]{:S(2)}) collective-permute-start(bf16[128,2048]{1,0:T(8,128)(2,1)} %get-tuple-element.141), channel_id=1, source_target_pairs={{0,8},{4,12},{8,0},{12,4},{1,9},{5,13},{9,1},{13,5},{2,10},{6,14},... | collective-permute-start | bytes 1572872 | tf_op jit(solution)/shard_map/ppermute | solution.py:36
  263.2 87.2 %collective-permute-start.71 = (bf16[128,2048]{1,0:T(8,128)(2,1)}, bf16[128,2048]{1,0:T(8,128)(2,1)}, u32[]{:S(2)}, u32[]{:S(2)}) collective-permute-start(bf16[128,2048]{1,0:T(8,128)(2,1)} %get-tuple-element.137), channel_id=1, source_target_pairs={{0,8},{4,12},{8,0},{12,4},{1,9},{5,13},{9,1},{13,5},{2,10},{6,14},... | collective-permute-start | bytes 1572872 | tf_op jit(solution)/shard_map/ppermute | solution.py:36
  350.4 170.1 %collective-permute-start.105 = (bf16[8,128,2048]{2,1,0:T(8,128)(2,1)S(1)}, bf16[8,128,2048]{2,1,0:T(8,128)(2,1)}, u32[]{:S(2)}, u32[]{:S(2)}) collective-permute-start(bf16[8,128,2048]{2,1,0:T(8,128)(2,1)S(1)} %get-tuple-element.292), channel_id=1, source_target_pairs={{0,4},{4,0},{8,12},{12,8},{1,5},{5,1},{9,13},{13,9},{2,6},{6,2},{1... | collective-permute-start | bytes 12582920 | tf_op jit(solution)/shard_map/ppermute | solution.py:36
  400.6 125.0 %collective-permute-start.72 = (bf16[8,128,2048]{2,1,0:T(8,128)(2,1)}, bf16[8,128,2048]{2,1,0:T(8,128)(2,1)}, u32[]{:S(2)}, u32[]{:S(2)}) collective-permute-start(bf16[8,128,2048]{2,1,0:T(8,128)(2,1)} %get-tuple-element.282), channel_id=1, source_target_pairs={{0,4},{4,0},{8,12},{12,8},{1,5},{5,1},{9,13},{13,9},{2,6},{6,2},{1... | collective-permute-start | bytes 12582920 | tf_op jit(solution)/shard_map/ppermute | solution.py:36
  401.5 52.1 %collective-permute-start.41 = (bf16[128,2048]{1,0:T(8,128)(2,1)S(1)}, bf16[128,2048]{1,0:T(8,128)(2,1)S(1)}, u32[]{:S(2)}, u32[]{:S(2)}) collective-permute-start(bf16[128,2048]{1,0:T(8,128)(2,1)S(1)} %get-tuple-element.354), channel_id=1, source_target_pairs={{0,8},{4,12},{8,0},{12,4},{1,9},{5,13},{9,1},{13,5},{2,10},{6,14},... | collective-permute-start | bytes 1572872 | tf_op jit(solution)/shard_map/ppermute | solution.py:36
  412.4 29.6 %collective-permute-start.40 = (bf16[128,2048]{1,0:T(8,128)(2,1)S(1)}, bf16[128,2048]{1,0:T(8,128)(2,1)S(1)}, u32[]{:S(2)}, u32[]{:S(2)}) collective-permute-start(bf16[128,2048]{1,0:T(8,128)(2,1)S(1)} %collective-permute-done.37), channel_id=1, source_target_pairs={{1,0},{2,3},{5,4},{6,7},{9,8},{10,11},{13,12},{14,15},{17,16},{18,... | collective-permute-start | bytes 1572872 | tf_op jit(solution)/shard_map/ppermute | solution.py:62
  442.0 37.6 %collective-permute-start.11 = (bf16[128,2048]{1,0:T(8,128)(2,1)S(1)}, bf16[128,2048]{1,0:T(8,128)(2,1)S(1)}, u32[]{:S(2)}, u32[]{:S(2)}) collective-permute-start(bf16[128,2048]{1,0:T(8,128)(2,1)S(1)} %get-tuple-element.149), channel_id=1, source_target_pairs={{0,8},{4,12},{8,0},{12,4},{1,9},{5,13},{9,1},{13,5},{2,10},{6,14},... | collective-permute-start | bytes 1572872 | tf_op jit(solution)/shard_map/ppermute | solution.py:36
  477.5 34.6 %collective-permute-start.13 = (bf16[128,2048]{1,0:T(8,128)(2,1)S(1)}, bf16[128,2048]{1,0:T(8,128)(2,1)S(1)}, u32[]{:S(2)}, u32[]{:S(2)}) collective-permute-start(bf16[128,2048]{1,0:T(8,128)(2,1)S(1)} %get-tuple-element.147), channel_id=1, source_target_pairs={{0,8},{4,12},{8,0},{12,4},{1,9},{5,13},{9,1},{13,5},{2,10},{6,14},... | collective-permute-start | bytes 1572872 | tf_op jit(solution)/shard_map/ppermute | solution.py:36
  479.6 31.5 %collective-permute-start.44 = (bf16[128,2048]{1,0:T(8,128)(2,1)S(1)}, bf16[128,2048]{1,0:T(8,128)(2,1)S(1)}, u32[]{:S(2)}, u32[]{:S(2)}) collective-permute-start(bf16[128,2048]{1,0:T(8,128)(2,1)S(1)} %get-tuple-element.153), channel_id=1, source_target_pairs={{0,8},{4,12},{8,0},{12,4},{1,9},{5,13},{9,1},{13,5},{2,10},{6,14},... | collective-permute-start | bytes 1572872 | tf_op jit(solution)/shard_map/ppermute | solution.py:36
  488.7 30.9 %collective-permute-start.14 = (bf16[128,2048]{1,0:T(8,128)(2,1)S(1)}, bf16[128,2048]{1,0:T(8,128)(2,1)S(1)}, u32[]{:S(2)}, u32[]{:S(2)}) collective-permute-start(bf16[128,2048]{1,0:T(8,128)(2,1)S(1)} %get-tuple-element.145), channel_id=1, source_target_pairs={{0,8},{4,12},{8,0},{12,4},{1,9},{5,13},{9,1},{13,5},{2,10},{6,14},... | collective-permute-start | bytes 1572872 | tf_op jit(solution)/shard_map/ppermute | solution.py:36
  512.1 36.9 %collective-permute-start.45 = (bf16[8,128,2048]{2,1,0:T(8,128)(2,1)}, bf16[8,128,2048]{2,1,0:T(8,128)(2,1)}, u32[]{:S(2)}, u32[]{:S(2)}) collective-permute-start(bf16[8,128,2048]{2,1,0:T(8,128)(2,1)} %get-tuple-element.312), channel_id=1, source_target_pairs={{0,4},{4,0},{8,12},{12,8},{1,5},{5,1},{9,13},{13,9},{2,6},{6,2},{1... | collective-permute-start | bytes 12582920 | tf_op jit(solution)/shard_map/ppermute | solution.py:36
  520.5 34.8 %collective-permute-start.15 = (bf16[8,128,2048]{2,1,0:T(8,128)(2,1)}, bf16[8,128,2048]{2,1,0:T(8,128)(2,1)}, u32[]{:S(2)}, u32[]{:S(2)}) collective-permute-start(bf16[8,128,2048]{2,1,0:T(8,128)(2,1)} %get-tuple-element.302), channel_id=1, source_target_pairs={{0,4},{4,0},{8,12},{12,8},{1,5},{5,1},{9,13},{13,9},{2,6},{6,2},{1... | collective-permute-start | bytes 12582920 | tf_op jit(solution)/shard_map/ppermute | solution.py:36
  628.0 116.8 %collective-permute-start.53 = (bf16[128,2048]{1,0:T(8,128)(2,1)}, bf16[128,2048]{1,0:T(8,128)(2,1)}, u32[]{:S(2)}, u32[]{:S(2)}) collective-permute-start(bf16[128,2048]{1,0:T(8,128)(2,1)} %get-tuple-element.212), channel_id=1, source_target_pairs={{0,4},{4,0},{8,12},{12,8},{1,5},{5,1},{9,13},{13,9},{2,6},{6,2},{1... | collective-permute-start | bytes 1572872 | tf_op jit(solution)/shard_map/ppermute | solution.py:36
  628.5 116.5 %collective-permute-start.56 = (bf16[128,2048]{1,0:T(8,128)(2,1)}, bf16[128,2048]{1,0:T(8,128)(2,1)}, u32[]{:S(2)}, u32[]{:S(2)}) collective-permute-start(bf16[128,2048]{1,0:T(8,128)(2,1)} %get-tuple-element.210), channel_id=1, source_target_pairs={{0,4},{4,0},{8,12},{12,8},{1,5},{5,1},{9,13},{13,9},{2,6},{6,2},{1... | collective-permute-start | bytes 1572872 | tf_op jit(solution)/shard_map/ppermute | solution.py:36
  628.5 122.2 %collective-permute-start.55 = (bf16[128,2048]{1,0:T(8,128)(2,1)}, bf16[128,2048]{1,0:T(8,128)(2,1)S(1)}, u32[]{:S(2)}, u32[]{:S(2)}) collective-permute-start(bf16[128,2048]{1,0:T(8,128)(2,1)} %get-tuple-element.211), channel_id=1, source_target_pairs={{0,4},{4,0},{8,12},{12,8},{1,5},{5,1},{9,13},{13,9},{2,6},{6,2},{1... | collective-permute-start | bytes 1572872 | tf_op jit(solution)/shard_map/ppermute | solution.py:36
  652.5 89.7 %collective-permute-start.113 = (bf16[128,2048]{1,0:T(8,128)(2,1)}, bf16[128,2048]{1,0:T(8,128)(2,1)}, u32[]{:S(2)}, u32[]{:S(2)}) collective-permute-start(bf16[128,2048]{1,0:T(8,128)(2,1)} %get-tuple-element.186), channel_id=1, source_target_pairs={{0,4},{4,0},{8,12},{12,8},{1,5},{5,1},{9,13},{13,9},{2,6},{6,2},{1... | collective-permute-start | bytes 1572872 | tf_op jit(solution)/shard_map/ppermute | solution.py:36
  652.6 89.8 %collective-permute-start.116 = (bf16[128,2048]{1,0:T(8,128)(2,1)}, bf16[128,2048]{1,0:T(8,128)(2,1)}, u32[]{:S(2)}, u32[]{:S(2)}) collective-permute-start(bf16[128,2048]{1,0:T(8,128)(2,1)} %get-tuple-element.184), channel_id=1, source_target_pairs={{0,4},{4,0},{8,12},{12,8},{1,5},{5,1},{9,13},{13,9},{2,6},{6,2},{1... | collective-permute-start | bytes 1572872 | tf_op jit(solution)/shard_map/ppermute | solution.py:36
  734.3 420.5 %reduce-scatter.12.cloned.1.call-start = ((), (), s32[]{:S(2)}) async-start(), calls=%async_computation.13 | async-start | bytes 6291456 | tf_op jit(solution)/shard_map/reduce_scatter | solution.py:476
  761.6 31.8 %collective-permute-start.114 = (bf16[128,2048]{1,0:T(8,128)(2,1)S(1)}, bf16[128,2048]{1,0:T(8,128)(2,1)S(1)}, u32[]{:S(2)}, u32[]{:S(2)}) collective-permute-start(bf16[128,2048]{1,0:T(8,128)(2,1)S(1)} %get-tuple-element.194), channel_id=1, source_target_pairs={{0,8},{4,12},{8,0},{12,4},{1,9},{5,13},{9,1},{13,5},{2,10},{6,14},... | collective-permute-start | bytes 1572872 | tf_op jit(solution)/shard_map/ppermute | solution.py:36
  774.7 30.0 %collective-permute-start.54 = (bf16[128,2048]{1,0:T(8,128)(2,1)S(1)}, bf16[128,2048]{1,0:T(8,128)(2,1)S(1)}, u32[]{:S(2)}, u32[]{:S(2)}) collective-permute-start(bf16[128,2048]{1,0:T(8,128)(2,1)S(1)} %get-tuple-element.220), channel_id=1, source_target_pairs={{0,8},{4,12},{8,0},{12,4},{1,9},{5,13},{9,1},{13,5},{2,10},{6,14},... | collective-permute-start | bytes 1572872 | tf_op jit(solution)/shard_map/ppermute | solution.py:36
  873.1 28.5 %collective-permute-start.75 = (bf16[128,2048]{1,0:T(8,128)(2,1)S(1)}, bf16[128,2048]{1,0:T(8,128)(2,1)S(1)}, u32[]{:S(2)}, u32[]{:S(2)}) collective-permute-start(bf16[128,2048]{1,0:T(8,128)(2,1)S(1)} %get-tuple-element.178), channel_id=1, source_target_pairs={{0,8},{4,12},{8,0},{12,4},{1,9},{5,13},{9,1},{13,5},{2,10},{6,14},... | collective-permute-start | bytes 1572872 | tf_op jit(solution)/shard_map/ppermute | solution.py:36
  939.6 219.3 %reduce-scatter.6.cloned.1.call-start = ((), (), s32[]{:S(2)}) async-start(), calls=%async_computation.10 | async-start | bytes 7667712 | tf_op jit(solution)/shard_map/reduce_scatter | solution.py:203
  1009.1 188.1 %reduce-scatter.10.cloned.1.call-start = ((), (), s32[]{:S(2)}) async-start(), calls=%async_computation.12 | async-start | bytes 6291456 | tf_op jit(solution)/shard_map/reduce_scatter | solution.py:476
  1026.2 242.4 %reduce-scatter.8.cloned.1.call-start = ((), (), s32[]{:S(2)}) async-start(), calls=%async_computation.11 | async-start | bytes 2359296 | tf_op jit(solution)/shard_map/reduce_scatter | solution.py:209
  1032.7 291.3 %reduce-scatter.14.cloned.1.call-start = ((), (), s32[]{:S(2)}) async-start(), calls=%async_computation.14 | async-start | bytes 6291456 | tf_op jit(solution)/shard_map/reduce_scatter | solution.py:476
  1068.5 35.5 %collective-permute-start.19 = (bf16[128,2048]{1,0:T(8,128)(2,1)S(1)}, bf16[128,2048]{1,0:T(8,128)(2,1)S(1)}, u32[]{:S(2)}, u32[]{:S(2)}) collective-permute-start(bf16[128,2048]{1,0:T(8,128)(2,1)S(1)} %copy-done.84), channel_id=1, source_target_pairs={{0,4},{4,0},{8,12},{12,8},{1,5},{5,1},{9,13},{13,9},{2,6},{6,2},{1... | collective-permute-start | bytes 1572872 | tf_op jit(solution)/shard_map/ppermute | solution.py:36
  1105.3 34.3 %collective-permute-start.95 = (bf16[128,2048]{1,0:T(8,128)(2,1)S(1)}, bf16[128,2048]{1,0:T(8,128)(2,1)S(1)}, u32[]{:S(2)}, u32[]{:S(2)}) collective-permute-start(bf16[128,2048]{1,0:T(8,128)(2,1)S(1)} %add_convert_fusion.5), channel_id=1, source_target_pairs={{0,8},{4,12},{8,0},{12,4},{1,9},{5,13},{9,1},{13,5},{2,10},{6,14},... | collective-permute-start | bytes 1572872 | tf_op jit(solution)/shard_map/ppermute | solution.py:36
  1118.5 30.3 %collective-permute-start.18 = (bf16[128,2048]{1,0:T(8,128)(2,1)S(1)}, bf16[128,2048]{1,0:T(8,128)(2,1)S(1)}, u32[]{:S(2)}, u32[]{:S(2)}) collective-permute-start(bf16[128,2048]{1,0:T(8,128)(2,1)S(1)} %get-tuple-element.204), channel_id=1, source_target_pairs={{0,8},{4,12},{8,0},{12,4},{1,9},{5,13},{9,1},{13,5},{2,10},{6,14},... | collective-permute-start | bytes 1572872 | tf_op jit(solution)/shard_map/ppermute | solution.py:36
  1119.4 29.5 %collective-permute-start.32 = (bf16[128,2048]{1,0:T(8,128)(2,1)S(1)}, bf16[128,2048]{1,0:T(8,128)(2,1)S(1)}, u32[]{:S(2)}, u32[]{:S(2)}) collective-permute-start(bf16[128,2048]{1,0:T(8,128)(2,1)S(1)} %get-tuple-element.205), channel_id=1, source_target_pairs={{1,2},{2,1},{5,6},{6,5},{9,10},{10,9},{13,14},{14,13},{17,18},{18,... | collective-permute-start | bytes 1572872 | tf_op jit(solution)/shard_map/ppermute | solution.py:81
  1158.8 169.4 %all-to-all-start.3 = ((bf16[4,64,1664]{2,1,0:T(8,128)(2,1)}), bf16[4,64,1664]{2,1,0:T(8,128)(2,1)S(1)}, u32[]{:S(2)}, u32[]{:S(2)}) async-start(bf16[4,64,1664]{2,1,0:T(8,128)(2,1)} %reduce-scatter.6.cloned.1.call-done), calls=%async_computation.4 | async-start | bytes 1703936 | tf_op jit(solution)/shard_map/all_to_all | solution.py:204
  (291 other events, 5530.2 us)
Sparse Core Ops, SparseCore 0:
  30.0 132.8 all-gather.12
  165.0 55.9 all-gather.10
  222.5 56.6 all-gather.16
  280.6 56.7 all-gather.14
  338.8 56.7 all-gather.18
  939.7 53.9 reduce-scatter.11
  1009.2 131.1 reduce-scatter.5
  1143.4 53.7 reduce-scatter.9
  1200.7 67.7 reduce-scatter.7
  1270.7 53.3 reduce-scatter.13
where the time goes:
time: 1350 us; the launch traced here: 1340 us
  waiting for transfers between devices  559 us (41%)
  matrix products  296 us (22%)
  starting transfers between devices  146 us (11%)
  local copies, waits for them, and re-layouts  126 us (9%)
  other arithmetic  108 us (8%)
  blocking collectives  90.8 us (7%)
  between operations  18.2 us (1%)
    ppermute x97, waiting for transfers between devices, swap(): return lax.ppermute(value, axis, [(i, i ^ bit) for i in range(4)])  246 us
    dot_general x14, matrix products, matmul(): return jnp.dot(left_side, right_side, preferred_element_type=F32)  89.3 us
    reduce_scatter x3, waiting for transfers between devices, body(): lax.psum_scatter(inner_rows(a, b).astype(BF16), 'dp', scatter_dimension=0...  88.6 us
    dot_general x12, matrix products, matmul_t(): lax.dot_general(left_side, right_side, (((1,), (1,)), ((), ())), preferre...  86.3 us
    ppermute x97, starting transfers between devices, swap(): return lax.ppermute(value, axis, [(i, i ^ bit) for i in range(4)])  80.4 us
    all_gather x1, blocking collectives, body(): lax.all_gather(routes[:, 0], ('ctx', 'expert'), axis=0, tiled=False)  74.2 us
    ppermute x4, waiting for transfers between devices, gather_line(): second_end = lax.ppermute(third_mid, 'expert', OUTWARD)  72.4 us
    reduce_scatter x1, waiting for transfers between devices, scatter_grads(): lax.psum_scatter(out_rows.astype(BF16), ('dp', 'expert'), scatter_dimensi...  67.3 us
  transfers between devices with their start and end apart: 142, of which 50 were waited for; matrix products, arithmetic and copies ran while one was open for 35% of the time, Pallas kernels for 0%

commit v1 on v0

v1 whole, which is shorter than its diff:
```python
import functools

import jax
import jax.numpy as jnp
from jax import lax
from jax.experimental import pallas as pl
from jax.experimental.pallas import tpu as pltpu
from jax.sharding import PartitionSpec as P

HEADS = 16
DH = 128
BLOCK = 128
HALVES = 2
SMALL = 128
TAIL = 16

EPSILON = 1e-06
NEGATIVE = -1e30
THETA_BASE = 50000.0
QUICK = pl.CostEstimate(flops=1000, bytes_accessed=1000, transcendentals=0)
F32 = jnp.float32
BF16 = jnp.bfloat16


def dot(a, b):
    return jnp.dot(a, b, preferred_element_type=F32)
def dot_t(a, b):
    return lax.dot_general(a, b, (((1,), (1,)), ((), ())), preferred_element_type=F32)
def dot_l(a, b):
    return lax.dot_general(a, b, (((0,), (0,)), ((), ())), preferred_element_type=F32)

def expert_kernel(
    capacity, tile_f, tile_d, tokens, extra, order_ref, norm_ref, up_ref,
    wg_col, wu_col, wd_row, wd_col, wg_row, wu_row, *refs
):
    shared_ref, back_ref, rows_ref, dy_ref, h_ref, dhg_ref, dhu_ref = refs[extra : extra + 7]
    ru_ref, gate_rows_ref, sums_ref, slot_ref = refs[extra + 7 :]
    group, width = norm_ref.shape[0], norm_ref.shape[2]
    first_steps = h_ref.shape[1] // tile_f
    tiles = width // tile_d
    step = pl.program_id(0)
    expert = order_ref[0]
    tail = pl.ds(tokens, TAIL)

    def chosen(b):
        slots = lax.broadcasted_iota(jnp.int32, (capacity, tokens), 0).astype(F32)
        return slots == slot_ref[b : b + 1, :]

    @pl.when(step == 0)
    def _():
        lanes = pl.ds(pl.multiple_of(expert * tokens, tokens), tokens)
        gates = jnp.concatenate(
            [
                jnp.sum(norm_ref[b, tail, lanes].astype(F32), axis=0, keepdims=True)
                for b in range(group)
            ],
            axis=0,
        )
        here = gates > 0.0
        shape = (tokens, tokens)
        below = lax.broadcasted_iota(jnp.int32, shape, 0) <= lax.broadcasted_iota(jnp.int32, shape, 1)
        ones = jnp.where(here, 1.0, 0.0)
        counts = dot(
            jnp.concatenate([ones, jnp.zeros((16 - group, tokens), F32)], axis=0).astype(BF16),
            jnp.where(below, 1.0, 0.0).astype(BF16),
        )[:group]
        slot_ref[...] = jnp.where(here, counts - 1.0, -1.0)
        for b in range(group):
            mine = chosen(b)
            hot = jnp.where(mine, 1.0, 0.0).astype(BF16)
            gate_rows = jnp.sum(jnp.where(mine, gates[b : b + 1], 0.0), axis=1, keepdims=True)
            at = pl.ds(b * capacity, capacity)
            rows_ref[at, :] = dot(hot, norm_ref[b, :tokens, :]).astype(BF16)
            up = dot(hot, up_ref[b, 0])
            ru_ref[at, :] = up.astype(BF16)
            dy_ref[at, :] = (gate_rows * up).astype(BF16)
            gate_rows_ref[at, :] = gate_rows
        sums_ref[...] = jnp.zeros_like(sums_ref)

    @pl.when(step < first_steps)
    def _():
        at = pl.ds(pl.multiple_of(step * tile_f, tile_f), tile_f)
        hg = dot(rows_ref[...], wg_col[...])
        hu = dot(rows_ref[...], wu_col[...])
        dh = dot_t(dy_ref[...], wd_row[...])
        sig = jax.nn.sigmoid(hg)
        act = hg * sig
        h_ref[:, at] = (act * hu).astype(BF16)
        dhg_ref[:, at] = (dh * hu * sig * (1.0 + hg * (1.0 - sig))).astype(BF16)
        dhu_ref[:, at] = (dh * act).astype(BF16)

    @pl.when(step >= first_steps)
    def _():
        tile = (step - first_steps + order_ref[1] + 1) % tiles
        at = pl.ds(pl.multiple_of(tile * tile_d, tile_d), tile_d)
        y = dot(h_ref[...], wd_col[...]).astype(BF16).astype(F32)
        sums_ref[...] += jnp.sum(y * ru_ref[:, at].astype(F32), axis=1, keepdims=True)
        gy = (gate_rows_ref[...] * y).astype(BF16)
        dx = (dot_t(dhg_ref[...], wg_row[...]) + dot_t(dhu_ref[...], wu_row[...])).astype(BF16)
        for b in range(group):
            hot = jnp.where(chosen(b), 1.0, 0.0).astype(BF16)
            lo = b * capacity
            shared_ref[0, b] = dot_l(hot, gy[lo : lo + capacity]).astype(BF16)
            back_ref[b, :tokens, :] = dot_l(hot, dx[lo : lo + capacity]).astype(BF16)
            back_ref[b, tail, :] = jnp.zeros((TAIL, tile_d), BF16)

    @pl.when(step == pl.num_programs(0) - 1)
    def _():
        start = (expert % (tile_d // tokens)) * tokens
        lanes = pl.ds(pl.multiple_of(start, tokens), tokens)
        row = lax.broadcasted_iota(jnp.int32, (TAIL, tokens), 0)
        for b in range(group):
            part = sums_ref[pl.ds(b * capacity, capacity), :]
            grad = jnp.sum(jnp.where(chosen(b), part, 0.0), axis=0, keepdims=True)
            high = grad.astype(BF16).astype(F32)
            low = (grad - high).astype(BF16).astype(F32)
            rest = grad - high - low
            packed = jnp.where(row == 0, high, jnp.where(row == 1, low, jnp.where(row == 2, rest, 0.0)))
            back_ref[b, tail, lanes] = packed.astype(BF16)


def expert_call(order, norm, up, tokens, weights, kept, part, parts, shared, capacity, deps, tile_f=512, tile_d=512):
    wg, wu, wd = weights
    group, width = norm.shape[0], norm.shape[2]
    hidden = wg.shape[1]
    rows = group * capacity
    first_steps = hidden // tile_f
    tiles = width // tile_d
    anywhere = pl.BlockSpec(memory_space=pl.ANY)

    def early(i, o):
        return jnp.minimum(i, first_steps - 1)

    def late(i, o):
        return (jnp.maximum(i - first_steps, 0) + o[1] + 1) % tiles

    def fixed(shape, index=0):
        return pl.BlockSpec(shape, lambda i, o: (index,) + (0,) * (len(shape) - 1))

    def column(shape, place):
        return pl.BlockSpec(shape, lambda i, o: (0,) * (len(shape) - 1) + (place(i, o),))

    def row(shape, place):
        return pl.BlockSpec(shape, lambda i, o: (place(i, o), 0))

    micro, shared_in = shared
    shared_in = [] if shared_in is None else [shared_in]
    kept_in = [] if kept is None else list(kept)
    extra = len(deps) + len(shared_in) + len(kept_in)
    sizes = (width, width, hidden, hidden, hidden)
    struct = jax.ShapeDtypeStruct
    results = pl.pallas_call(
        functools.partial(expert_kernel, capacity, tile_f, tile_d, tokens, extra),
        grid_spec=pltpu.PrefetchScalarGridSpec(
            num_scalar_prefetch=1,
            grid=(first_steps + tiles,),
            in_specs=[
                fixed(norm.shape),
                pl.BlockSpec((group, 1, tokens, width), lambda i, o: (0, micro, 0, 0)),
                column((width, tile_f), early),
                column((width, tile_f), early),
                row((tile_f, width), early),
                column((hidden, tile_d), late),
                row((tile_d, hidden), late),
                row((tile_d, hidden), late),
            ]
            + [anywhere] * extra,
            out_specs=[
                pl.BlockSpec((1, group, tokens, tile_d), lambda i, o: (micro, 0, 0, late(i, o))),
                column((group, tokens + TAIL, tile_d), late),
            ]
            + [fixed((rows, size), part) for size in sizes],
            scratch_shapes=[
                pltpu.VMEM((rows, width), BF16),
                pltpu.VMEM((rows, 1), F32),
                pltpu.VMEM((rows, 1), F32),
                pltpu.VMEM((group, tokens), F32),
            ],
        ),
        out_shape=[struct((2, group, tokens, width), BF16), struct((group, tokens + TAIL, width), BF16)]
        + [struct((parts * rows, size), BF16) for size in sizes],
        input_output_aliases={9 + len(deps) + i: i for i in range(len(shared_in))}
        | {9 + len(deps) + len(shared_in) + i: 2 + i for i in range(len(kept_in))},
        compiler_params=pltpu.CompilerParams(vmem_limit_bytes=56 * 2**20),
        cost_estimate=QUICK,
    )(order, norm, up, wg, wu, wd, wd, wg, wu, *deps, *shared_in, *kept_in)
    return results[0], results[1], results[2:]


def product_kernel(left_ref, right_ref, *refs):
    refs[-1][...] = dot_l(left_ref[...], right_ref[...]).astype(BF16)


def product_call(left, right, deps, tile=512):
    depth, rows = left.shape
    columns = right.shape[1]
    wide = min(columns, 1024)
    return pl.pallas_call(
        product_kernel,
        grid=(columns // wide, rows // tile),
        in_specs=[
            pl.BlockSpec((depth, tile), lambda j, i: (0, i)),
            pl.BlockSpec((depth, wide), lambda j, i: (0, j)),
        ]
        + [pl.BlockSpec(memory_space=pl.ANY)] * len(deps),
        out_specs=pl.BlockSpec((tile, wide), lambda j, i: (i, j)),
        out_shape=jax.ShapeDtypeStruct((rows, columns), BF16),
        compiler_params=pltpu.CompilerParams(vmem_limit_bytes=56 * 2**20),
        cost_estimate=QUICK,
    )(left, right, *deps)


def pair_product_kernel(_, left_a, right_a, left_b, right_b, small_ref, *refs):
    out_ref = refs[-1]
    columns, few = right_a.shape[1], small_ref.shape[1]
    total = dot_l(left_a[...], right_a[...]) + dot_l(left_b[...], right_b[...])
    out_ref[:, :columns] = total.astype(BF16)
    out_ref[:, columns : columns + few] = small_ref[...]
    if out_ref.shape[1] > columns + few:
        attended_a, branch_a, attended_b, branch_b = refs[:4]
        wide = out_ref.shape[1] - columns - few
        tall = attended_a.shape[1]
        for j in range(out_ref.shape[0] // tall):
            at = slice(j * wide, (j + 1) * wide)
            total = dot_l(attended_a[...], branch_a[:, at]) + dot_l(attended_b[...], branch_b[:, at])
            out_ref[j * tall : (j + 1) * tall, columns + few :] = total.astype(BF16)


def pair_product_call(part, parts, lefts, rights, small, others, deps, tile=512):
    depth, rows = lefts[0].shape
    columns, few = rights[0].shape[1], small.shape[1]
    steps = rows // tile // parts

    def place(i, o):
        return o[0] * steps + i

    left = pl.BlockSpec((depth, tile), lambda i, o: (0, place(i, o)))
    right = pl.BlockSpec((depth, columns), lambda i, o: (0, 0))
    other_specs, wide = [], 0
    if others:
        wide = others[1].shape[1] // 4
        other_specs = [
            pl.BlockSpec((depth, tile // 2), lambda i, o: (0, place(i, o) // 2)),
            pl.BlockSpec((depth, 2 * wide), lambda i, o: (0, place(i, o) % 2)),
        ] * 2
    return pl.pallas_call(
        pair_product_kernel,
        grid_spec=pltpu.PrefetchScalarGridSpec(
            num_scalar_prefetch=1,
            grid=(steps,),
            in_specs=[left, right, left, right]
            + [pl.BlockSpec((tile, few), lambda i, o: (place(i, o), 0))]
            + other_specs
            + [pl.BlockSpec(memory_space=pl.ANY)] * len(deps),
            out_specs=pl.BlockSpec((tile, columns + few + wide), lambda i, o: (i, 0)),
        ),
        out_shape=jax.ShapeDtypeStruct((rows // parts, columns + few + wide), BF16),
        compiler_params=pltpu.CompilerParams(vmem_limit_bytes=48 * 2**20),
        cost_estimate=QUICK,
    )(part.reshape(1), lefts[0], rights[0], lefts[1], rights[1], small, *others, *deps)


def unpack_kernel(payload_ref, out_rows_ref, query_ref, key_ref, value_ref, output_ref, small_ref):
    ctx_size, _, columns = payload_ref.shape
    heads = (columns - SMALL) // (3 * DH)
    half = heads // HALVES
    for c in range(ctx_size):
        for head in range(heads):
            to = ((head // half) * ctx_size + c) * half + head % half
            for t, ref in enumerate((query_ref, key_ref, value_ref)):
                at = (3 * head + t) * DH
                ref[:, to * DH : (to + 1) * DH] = payload_ref[c, :, at : at + DH].astype(F32)
        wide = out_rows_ref.shape[2]
        output_ref[:, c * wide : (c + 1) * wide] = out_rows_ref[c]
    small_ref[...] = sum(
        payload_ref[c, :, columns - SMALL :].astype(F32) for c in range(ctx_size)
    )


def unpack_call(payload, out_rows):
    rows = payload.shape[1]
    width = out_rows.shape[0] * out_rows.shape[2]
    struct = jax.ShapeDtypeStruct
    return pl.pallas_call(
        unpack_kernel,
        out_shape=[struct((rows, width), F32)] * 4 + [struct((rows, SMALL), F32)],
    )(payload, out_rows)


def nothing_kernel(*refs):
    pass


def meet(values, *deps):
    anywhere = pl.BlockSpec(memory_space=pl.ANY)
    return pl.pallas_call(
        nothing_kernel,
        in_specs=[anywhere] * (len(values) + len(deps)),
        out_specs=[anywhere] * len(values),
        out_shape=[jax.ShapeDtypeStruct(value.shape, value.dtype) for value in values],
        input_output_aliases={i: i for i in range(len(values))},
    )(*values, *deps)


class Flow:
    def __init__(self, steps):
        self.steps = steps
        self.going = next(steps)


def idle():
    while True:
        yield []


def turn(flows, *deps, values=()):
    going = [value for flow in flows for value in flow.going] + list(values)
    deps = [value for value in deps if value is not None]
    met = meet(going, *deps) if going else deps
    token = met[0] if met else None
    for flow in flows:
        count = len(flow.going)
        flow.going = flow.steps.send(list(met[:count]))
        met = met[count:]
    return (token, list(met)) if values else token


def copy_kernel(value_ref, *refs):
    refs[-1][...] = value_ref[...]


def copy_after(value, *deps, tile=256):
    deps = [value for value in deps if value is not None]
    block = pl.BlockSpec((tile, value.shape[1]), lambda i: (i, 0))
    return pl.pallas_call(
        copy_kernel,
        grid=(value.shape[0] // tile,),
        in_specs=[block] + [pl.BlockSpec(memory_space=pl.ANY)] * len(deps),
        out_specs=block,
        out_shape=jax.ShapeDtypeStruct(value.shape, value.dtype),
        cost_estimate=QUICK,
    )(value, *deps)


def head_parts(joined, cos, sin, gain_q, gain_k, dh):
    q = joined[:, :dh]; k = joined[:, dh:2 * dh]
    rq = lax.rsqrt(jnp.mean(q * q, axis=-1, keepdims=True) + EPSILON)
    rk = lax.rsqrt(jnp.mean(k * k, axis=-1, keepdims=True) + EPSILON)
    uq = q * rq; uk = k * rk
    def turn(w):
        return (w * cos + pltpu.roll(w, dh // 2, 1) * sin).astype(BF16)
    return rq, uq, rk, uk, turn(uq * gain_q), turn(uk * gain_k), joined[:, 2 * dh:].astype(BF16)

def probabilities(qr, kr, row_ref, col_ref, dh):
    s = dot_t(qr, kr) * dh ** (-0.5)
    s = jnp.where(row_ref[...] == col_ref[...], s, NEGATIVE)
    p = jnp.exp(s - jnp.max(s, axis=-1, keepdims=True))
    return p / jnp.sum(p, axis=-1, keepdims=True)

def forward_kernel(dh, joined_ref, cos_ref, sin_ref, gain_ref, row_ref, col_ref, *refs):
    o_ref = refs[-1]
    _, _, _, _, qr, kr, v = head_parts(joined_ref[...], cos_ref[...], sin_ref[...], gain_ref[0:1, :], gain_ref[1:2, :], dh)
    p = probabilities(qr, kr, row_ref, col_ref, dh)
    o_ref[...] = dot(p.astype(BF16), v).astype(BF16)

def backward_kernel(dh, joined_ref, do_ref, cos_ref, sin_ref, gain_ref, row_ref, col_ref, *refs):
    d_ref, pair_ref = refs[-2:]
    cos = cos_ref[...]; sin = sin_ref[...]
    gq = gain_ref[0:1, :]; gk = gain_ref[1:2, :]
    rq, uq, rk, uk, qr, kr, v = head_parts(joined_ref[...], cos, sin, gq, gk, dh)
    p = probabilities(qr, kr, row_ref, col_ref, dh)
    do = do_ref[...]
    dp = dot_t(do, v)
    ds = (p * (dp - jnp.sum(p * dp, axis=-1, keepdims=True))).astype(BF16)
    scale = dh ** (-0.5)
    dq = (dot(ds, kr) * scale).astype(BF16).astype(F32)
    dk = (dot_l(ds, qr) * scale).astype(BF16).astype(F32)
    dv = dot_l(p.astype(BF16), do).astype(BF16)
    def back(w):
        return w * cos - pltpu.roll(w, dh // 2, 1) * sin
    def norm_back(up, unit, scaling, gain):
        weighted = up * gain
        return scaling * (weighted - unit * jnp.mean(weighted * unit, axis=-1, keepdims=True))
    nq = back(dq); nk = back(dk)
    d_ref[:, :dh] = norm_back(nq, uq, rq, gq).astype(BF16)
    d_ref[:, dh:2 * dh] = norm_back(nk, uk, rk, gk).astype(BF16)
    d_ref[:, 2 * dh:] = dv
    part = jnp.concatenate([jnp.sum(nq * uq, axis=0, keepdims=True), jnp.sum(nk * uk, axis=0, keepdims=True)], axis=0)
    @pl.when(pl.program_id(0) == 0)
    def _():
        pair_ref[...] = part
    @pl.when(pl.program_id(0) > 0)
    def _():
        pair_ref[...] += part

def attention_specs(tokens, heads, dh, deps):
    fixed = lambda shape: pl.BlockSpec(shape, lambda h: (0, 0))
    return (pl.BlockSpec((tokens, 3 * dh), lambda h: (0, h)), pl.BlockSpec((tokens, dh), lambda h: (0, h)),
            [fixed((tokens, dh)), fixed((tokens, dh)), fixed((2, dh)), fixed((tokens, 1)), fixed((1, tokens))] + [pl.BlockSpec(memory_space=pl.ANY)] * len(deps))

def attention_forward_call(joined, cos, sin, gains, segment, deps, dh=128):
    tokens = joined.shape[0]; heads = joined.shape[1] // (3 * dh)
    three, one, rest = attention_specs(tokens, heads, dh, deps)
    return pl.pallas_call(
        functools.partial(forward_kernel, dh), grid=(heads,), in_specs=[three] + rest, out_specs=one,
        out_shape=jax.ShapeDtypeStruct((tokens, heads * dh), BF16),
        compiler_params=pltpu.CompilerParams(vmem_limit_bytes=40 * 2**20),
        cost_estimate=QUICK,
    )(joined, cos, sin, gains, segment[:, None], segment[None, :], *deps)

def attention_backward_call(joined, grad, cos, sin, gains, segment, deps, dh=128):
    tokens = joined.shape[0]; heads = joined.shape[1] // (3 * dh)
    three, one, rest = attention_specs(tokens, heads, dh, deps)
    return pl.pallas_call(
        functools.partial(backward_kernel, dh), grid=(heads,), in_specs=[three, one] + rest,
        out_specs=[three, pl.BlockSpec((2, dh), lambda h: (0, 0))],
        out_shape=[jax.ShapeDtypeStruct(joined.shape, BF16), jax.ShapeDtypeStruct((2, dh), F32)],
        compiler_params=pltpu.CompilerParams(vmem_limit_bytes=40 * 2**20),
        cost_estimate=QUICK,
    )(joined, grad, cos, sin, gains, segment[:, None], segment[None, :], *deps)


def swap(value, axis, bit):
    return lax.ppermute(value, axis, [(i, i ^ bit) for i in range(lax.axis_size(axis))])


MIDDLE = [(1, 2), (2, 1)]
OUTWARD = [(1, 0), (2, 3)]
INWARD = [(0, 1), (3, 2)]


def scatter_ctx_steps(terms, result):
    (beside,) = yield [swap(terms[2:], "ctx", 1)]
    far = (terms[1].astype(F32) + beside[1].astype(F32)).astype(BF16)
    (across,) = yield [swap(far, "ctx", 2)]
    result.append(terms[0].astype(F32) + beside[0].astype(F32) + across.astype(F32))
    yield from idle()


def gather_ctx_steps(own, blocks):
    across, beside = yield [swap(own, "ctx", 2), swap(own, "ctx", 1)]
    (corner,) = yield [swap(across, "ctx", 1)]
    blocks += [own, across, beside, corner]
    yield from idle()


def line_steps(own, slots, across_dp=None, pause=0):
    place = lax.axis_index("expert")
    middle = (place == 1) | (place == 2)

    def over(block):
        return [] if across_dp is None else [swap(block, "dp", 1)]

    pair, third_mid, *x0 = yield [
        swap(own, "expert", 1),
        lax.ppermute(own, "expert", MIDDLE),
    ] + over(own)
    for _ in range(pause):
        yield []
    second_mid, second_end, *x1 = yield [
        lax.ppermute(pair, "expert", MIDDLE),
        lax.ppermute(third_mid, "expert", OUTWARD),
    ] + over(pair)
    second = jnp.where(middle, second_mid, second_end)
    third_end, *x2 = yield [lax.ppermute(second_mid, "expert", OUTWARD)] + over(second)
    third = jnp.where(middle, third_mid, third_end)
    slots += [own, pair, second, third]
    if across_dp is not None:
        (x3,) = yield over(third)
        across_dp += [x0[0], x1[0], x2[0], x3]
    yield from idle()


def unline_steps(slots, result):
    (three,) = yield [lax.ppermute(slots[3], "expert", INWARD)]
    second = (slots[2].astype(F32) + three.astype(F32)).astype(BF16)
    over, inward = yield [
        lax.ppermute(second, "expert", MIDDLE),
        lax.ppermute(second, "expert", INWARD),
    ]
    first = (slots[1].astype(F32) + over.astype(F32)).astype(BF16)
    third = (slots[3].astype(F32) + inward.astype(F32)).astype(BF16)
    home, pair = yield [lax.ppermute(third, "expert", MIDDLE), swap(first, "expert", 1)]
    result.append(slots[0].astype(F32) + pair.astype(F32) + home.astype(F32))
    yield from idle()


def undp_steps(here, there, result):
    moving = [swap(piece, "dp", 1) for piece in there]
    (x3,) = yield [moving[3]]
    sum3 = here[3].astype(F32) + x3.astype(F32)
    x2, three = yield [moving[2], lax.ppermute(sum3.astype(BF16), "expert", INWARD)]
    second = (here[2].astype(F32) + x2.astype(F32) + three.astype(F32)).astype(BF16)
    x1, over, inward = yield [
        moving[1],
        lax.ppermute(second, "expert", MIDDLE),
        lax.ppermute(second, "expert", INWARD),
    ]
    first = (here[1].astype(F32) + x1.astype(F32) + over.astype(F32)).astype(BF16)
    third = (sum3 + inward.astype(F32)).astype(BF16)
    x0, home, pair = yield [
        moving[0],
        lax.ppermute(third, "expert", MIDDLE),
        swap(first, "expert", 1),
    ]
    result.append(
        here[0].astype(F32) + x0.astype(F32) + pair.astype(F32) + home.astype(F32)
    )
    yield from idle()


def gather_steps(own, groups, plan):
    place = lax.axis_index("expert")
    middle = (place == 1) | (place == 2)
    blocks = [own]
    crossed = [None] * 4

    def across(step):
        return {s: swap(blocks[s], "ctx", 2) for s in range(len(blocks)) if plan[s] == step}

    def note(moving, values):
        for s, value in zip(moving, values):
            crossed[s] = value

    moving = across(0)
    pair, third_mid, *rest = yield [
        swap(own, "expert", 1),
        lax.ppermute(own, "expert", MIDDLE),
    ] + list(moving.values())
    note(moving, rest)
    blocks.append(pair)
    moving = across(1)
    second_mid, second_end, *rest = yield [
        lax.ppermute(pair, "expert", MIDDLE),
        lax.ppermute(third_mid, "expert", OUTWARD),
    ] + list(moving.values())
    note(moving, rest)
    blocks.append(jnp.where(middle, second_mid, second_end))
    moving = across(2)
    third_end, *rest = yield [lax.ppermute(second_mid, "expert", OUTWARD)] + list(moving.values())
    note(moving, rest)
    blocks.append(jnp.where(middle, third_mid, third_end))
    groups[0] = jnp.stack(blocks)
    if plan == (3, 3, 3, 3):
        moving = swap(groups[0], "ctx", 2)
        (groups[1],) = yield [swap(groups[0], "ctx", 1)]
        (groups[2],) = yield [moving]
    else:
        moving = across(3)
        groups[1], *rest = yield [swap(groups[0], "ctx", 1)] + list(moving.values())
        note(moving, rest)
        groups[2] = jnp.stack(crossed)
    (groups[3],) = yield [swap(groups[2], "ctx", 1)]
    yield from idle()


def early_gather_steps(own, groups):
    place = lax.axis_index("expert")
    middle = (place == 1) | (place == 2)
    pair, third_mid = yield [swap(own, "expert", 1), lax.ppermute(own, "expert", MIDDLE)]
    (y0,) = yield [swap(own, "ctx", 2)]
    (y1,) = yield [swap(pair, "ctx", 2)]
    second_mid, second_end = yield [
        lax.ppermute(pair, "expert", MIDDLE),
        lax.ppermute(third_mid, "expert", OUTWARD),
    ]
    second = jnp.where(middle, second_mid, second_end)
    third_end, y2 = yield [lax.ppermute(second_mid, "expert", OUTWARD), swap(second, "ctx", 2)]
    third = jnp.where(middle, third_mid, third_end)
    groups[0] = jnp.stack([own, pair, second, third])
    y3, groups[1] = yield [swap(third, "ctx", 2), swap(groups[0], "ctx", 1)]
    groups[2] = jnp.stack([y0, y1, y2, y3])
    (groups[3],) = yield [swap(groups[2], "ctx", 1)]
    yield from idle()


def scatter_steps(groups, result, slow=False):
    def slot(values, s):
        return values[..., s, :, :]

    (far,) = yield [swap(groups[3], "ctx", 1)]
    over_y = (groups[2].astype(F32) + far.astype(F32)).astype(BF16)

    def across(*slots):
        return [swap(slot(over_y, s), "ctx", 2) for s in slots]

    def total(s, moved):
        return slot(groups[0], s).astype(F32) + slot(near, s).astype(F32) + moved.astype(F32)

    def inwards(sum3):
        return lax.ppermute(sum3.astype(BF16), "expert", INWARD)

    if slow:
        (y3,) = yield across(3)
        (y2,) = yield across(2)
        y1, near = yield across(1) + [swap(groups[1], "ctx", 1)]
        sum3 = total(3, y3)
        (three,) = yield [inwards(sum3)]
        moving = across(0)
    else:
        y3, y2 = yield across(3, 2)
        y1, y0, near = yield across(1, 0) + [swap(groups[1], "ctx", 1)]
        sum3 = total(3, y3)
        (three,) = yield [inwards(sum3)]
        moving = []
    second = (total(2, y2) + three.astype(F32)).astype(BF16)
    over, inward, *rest = yield [
        lax.ppermute(second, "expert", MIDDLE),
        lax.ppermute(second, "expert", INWARD),
    ] + moving
    y0 = rest[0] if rest else y0
    first = (total(1, y1) + over.astype(F32)).astype(BF16)
    third = (sum3 + inward.astype(F32)).astype(BF16)
    home, pair = yield [lax.ppermute(third, "expert", MIDDLE), swap(first, "expert", 1)]
    result.append(total(0, y0) + pair.astype(F32) + home.astype(F32))
    yield from idle()


def places(index, lengths, block_order):
    blocks = jnp.arange(block_order.shape[0], dtype=jnp.int32)
    holder = (index // BLOCK)[:, None] == blocks[None, :]
    logical = (
        jnp.sum(jnp.where(holder, block_order[None, :], 0), axis=1) * BLOCK + index % BLOCK
    )
    seq_ends = jnp.cumsum(lengths)
    segment = jnp.sum((logical[:, None] >= seq_ends[None, :]).astype(jnp.int32), axis=1)
    starts = seq_ends - lengths
    member = segment[:, None] == jnp.arange(lengths.shape[0], dtype=jnp.int32)[None, :]
    seq_first = jnp.sum(jnp.where(member, starts[None, :], 0), axis=1)
    return (segment, (logical - seq_first).astype(F32))


def rotary_tables(positions, half_size):
    frequency = THETA_BASE ** (-(jnp.arange(half_size, dtype=F32) / half_size))
    angles = positions[:, None] * frequency[None, :]
    cosine, sine = jnp.cos(angles), jnp.sin(angles)
    return jnp.concatenate([cosine, cosine], axis=1), jnp.concatenate([-sine, sine], axis=1)


def norm_back(upstream, unit_rows, scaling, gain_vector):
    weighted = upstream * gain_vector
    return scaling * (weighted - unit_rows * jnp.mean(weighted * unit_rows, axis=-1, keepdims=True))


def row_scale(rows):
    return lax.rsqrt(jnp.mean(rows * rows, axis=-1, keepdims=True) + EPSILON)


def whole_heads(rows, share):
    return lax.axis_size("dp") == HALVES and rows * lax.axis_size("expert") == share


def assemble(pieces, shape):
    d, z = lax.axis_index("dp"), lax.axis_index("expert")
    whole = jnp.zeros(shape, BF16)
    for dx, line in enumerate(pieces):
        for s, piece in enumerate(line):
            whole = lax.dynamic_update_slice(
                whole, piece[None, :, None], (d ^ dx if shape[0] > 1 else 0, 0, z ^ s) + (0,) * (len(shape) - 3)
            )
    return whole


def piece_of(whole, dx, s):
    first = lax.axis_index("dp") ^ dx if whole.shape[0] > 1 else 0
    start = (first, 0, lax.axis_index("expert") ^ s) + (0,) * (whole.ndim - 3)
    return lax.dynamic_slice(whole, start, (1, whole.shape[1], 1) + whole.shape[3:])[0, :, 0]


def sum_rows(whole):
    return lax.psum_scatter(whole, "dp", scatter_dimension=0, tiled=True)


def pack_weights(query_weight, key_weight, value_weight, attention_gain, mixture_gain, query_key_gain, router):
    rows, width = query_weight.shape
    ctx_size = lax.axis_size("ctx")
    share = width // (HALVES * ctx_size)
    stacked = jnp.stack([query_weight, key_weight, value_weight], axis=1)
    stacked = stacked.reshape(rows, 3, HALVES, ctx_size, share // DH, DH)
    stacked = stacked.transpose(3, 0, 2, 4, 1, 5).reshape(ctx_size, rows, 3 * HALVES * share)
    small = jnp.concatenate(
        [
            attention_gain[:, None],
            mixture_gain[:, None],
            jnp.pad(query_key_gain, (0, rows - query_key_gain.shape[0]))[:, None],
            router,
        ],
        axis=1,
    )
    small = jnp.pad(small, ((0, 0), (0, SMALL - small.shape[1])))
    return jnp.concatenate(
        [stacked, jnp.broadcast_to(small[None], (ctx_size, rows, SMALL))], axis=2
    )


def chosen_gates(normed, router, chosen):
    logits = jnp.where(chosen, dot(normed, router), NEGATIVE)
    powers = jnp.where(chosen, jnp.exp(logits - jnp.max(logits, axis=1, keepdims=True)), 0.0)
    return powers / jnp.sum(powers, axis=1, keepdims=True)


def with_gates(normed, gates):
    flat = gates.T.reshape(1, -1)
    high = flat.astype(BF16).astype(F32)
    low = (flat - high).astype(BF16).astype(F32)
    row = lax.broadcasted_iota(jnp.int32, (TAIL, flat.shape[1]), 0)
    tail = jnp.where(row == 0, high, jnp.where(row == 1, low, jnp.where(row == 2, flat - high - low, 0.0)))
    return jnp.concatenate([normed, tail.astype(BF16)])


def body(
    inputs,
    cotangent,
    lengths,
    block_order,
    routes,
    query_weight,
    key_weight,
    value_weight,
    output_weight,
    attention_gain,
    mixture_gain,
    query_key_gain,
    router,
    expert_gate,
    expert_up,
    expert_down,
):
    micro_count, _, tokens, width = inputs.shape
    top = routes.shape[3]
    expert_count = router.shape[1]
    most = tokens * top * 9 // (8 * expert_count) + 2
    capacity = -(-most // 16) * 16
    place = lax.axis_index("ctx")
    rows, few = query_weight.shape[0], query_key_gain.shape[0]
    micros = range(micro_count)

    line = lax.axis_index("expert")
    dp_size = lax.axis_size("dp")
    two = dp_size == 2
    share = width // (HALVES * 4)
    per_ctx = HALVES * share

    slots, slots_dp, blocks = [], [] if two else None, []
    heads_here = whole_heads(rows, share)
    upstream_groups = [None] * 4
    upstream_flow = Flow(early_gather_steps(cotangent[:, 0], upstream_groups))
    payload = pack_weights(
        query_weight, key_weight, value_weight, attention_gain, mixture_gain, query_key_gain, router
    )
    payload = lax.all_to_all(payload, "ctx", split_axis=0, concat_axis=0, tiled=True)
    if heads_here:
        chunks = output_weight.reshape(rows, 4, width // 4).transpose(1, 0, 2)
        payload = jnp.concatenate([payload, chunks], axis=2)
    spread = Flow(line_steps(payload, slots, slots_dp))
    stream_flow = Flow(
        gather_ctx_steps(copy_after(inputs.reshape(-1, width), payload).reshape(-1, tokens, width), blocks)
    )
    token = turn([spread, upstream_flow])
    token = turn([spread, stream_flow, upstream_flow])
    token = turn([spread, stream_flow, upstream_flow], token)
    copies = [copy_after(own[0], token) for own in (expert_gate, expert_up, expert_down)]
    token = turn([spread, upstream_flow], token, *copies)
    experts = [lax.all_gather(own, "dp", axis=0, tiled=True) for own in copies]
    shape = (dp_size, 4, 4) + payload.shape[1:]
    if two:
        packed = assemble([slots, slots_dp], shape)
    else:
        packed = lax.all_gather(
            assemble([slots], (1,) + shape[1:])[0], "dp", axis=0, tiled=False
        )
    if heads_here:
        out_rows = packed[..., 3 * per_ctx + SMALL :].transpose(0, 2, 3, 1, 4).reshape(per_ctx, width)
    packed = packed.reshape(width, -1)
    projections = packed[:, : 3 * per_ctx]
    small = packed[:, 3 * per_ctx : 3 * per_ctx + SMALL].astype(F32)
    gain_one, gain_two = small[:, 0], small[:, 1]
    gain_pair = small[:, 2].reshape(-1, rows)[:, :few].reshape(2, DH)
    router_all = packed[:, 3 * per_ctx + 3 : 3 * per_ctx + 3 + expert_count]

    index = jnp.concatenate(
        [(place ^ s) * tokens + jnp.arange(tokens, dtype=jnp.int32) for s in (0, 2, 1, 3)]
    )
    tables = []
    for m in micros:
        segment, position = places(index, lengths[m, 0], block_order[m, 0])
        tables.append(rotary_tables(position, DH // 2) + (gain_pair, segment))
    stream_all = jnp.concatenate(blocks, axis=1)

    normed_one, units, joined_list, attended_list = [], [], [], []

    def attention(m, token, flows):
        stream = stream_all[m].astype(F32)
        unit = stream * row_scale(stream)
        normed = (unit * gain_one).astype(BF16)
        joined = dot(normed, projections)
        if flows:
            token, (joined,) = turn(flows, token, values=[joined])
        attended = attention_forward_call(joined, *tables[m], [token])
        normed_one.append(normed)
        units.append(unit)
        joined_list.append(joined)
        attended_list.append(attended)
        return attended

    def out_terms_of(m):
        return dot(attended_list[m], out_rows).astype(BF16).reshape(4, tokens, width)

    done = attention(0, token, [])
    if not heads_here:
        out_rows = lax.all_gather(output_weight, ("dp", "ctx", "expert"), axis=0, tiled=True)
        out_rows = out_rows.reshape(HALVES, 4, share, -1)
        out_rows = lax.dynamic_index_in_dim(out_rows, place, 1, keepdims=False)
        out_rows = out_rows.reshape(per_ctx, -1)
    sum_a, sum_b = [], []
    flow_a = Flow(scatter_ctx_steps(out_terms_of(0), sum_a))
    token = turn([flow_a], experts[0])
    done = attention(1, token, [])
    token = turn([flow_a, upstream_flow], done)
    flow_b = Flow(scatter_ctx_steps(out_terms_of(1), sum_b))

    normed_two, unit_two, scale_two, gates_own, residuals = [], [], [], [], []

    def route(m, attention_sum):
        residual = inputs[m, 0].astype(F32) + attention_sum
        scale = row_scale(residual)
        unit = residual * scale
        normed = (unit * gain_two).astype(BF16)
        chosen = jnp.any(
            routes[m, 0][..., None] == jnp.arange(expert_count, dtype=jnp.int32), axis=1
        )
        gates = chosen_gates(normed, router_all, chosen)
        residuals.append(residual)
        normed_two.append(normed)
        unit_two.append(unit)
        scale_two.append(scale)
        gates_own.append(gates)
        return with_gates(normed, gates)

    groups = [[None] * 4 for _ in micros]
    gather_a = Flow(gather_steps(route(0, sum_a[0]), groups[0], (3, 3, 3, 3)))
    token = turn([flow_b, gather_a], experts[1])
    token = turn([gather_a, upstream_flow])
    token = turn([gather_a, upstream_flow, flow_b], experts[2])
    second_payload = route(1, sum_b[0])
    gather_b = Flow(gather_steps(second_payload, groups[1], (1, 1, 2, 3)))

    shared, kept, calls = [None] * 4, None, 0
    back = [[None] * 4 for _ in micros]
    expert_index = place * 4 + line
    order = jnp.stack([expert_index, expert_index * tokens // 512]).astype(jnp.int32)

    def expert(m, k, token, flows):
        nonlocal kept, calls
        shared[k], back[m][k], kept = expert_call(
            order, groups[m][k], upstream_groups[k], tokens, experts, kept, calls, 8, (m, shared[k]), capacity, [token]
        )
        calls += 1
        token, met = turn(flows, values=[shared[k], back[m][k], *kept])
        shared[k], back[m][k], kept = met[0], met[1], met[2:]
        return token

    token = expert(0, 0, token, [gather_a, gather_b])
    token = expert(0, 1, token, [gather_a, gather_b])
    token = expert(0, 2, token, [gather_a, gather_b])
    token = expert(0, 3, token, [gather_b])
    down_a, down_b, out_sum = [], [], []
    scatter_a = Flow(scatter_steps(back[0], down_a))
    token = expert(1, 2, token, [gather_b, scatter_a])
    token = expert(1, 3, token, [scatter_a])
    scatter_b = Flow(scatter_steps(back[1], down_b))
    token = expert(1, 1, token, [scatter_a, scatter_b])
    token = expert(1, 0, token, [scatter_a, scatter_b])
    rows_in, out_grad, hidden, gate_pre_grad, up_pre_grad = kept
    out_flow = Flow(scatter_steps(shared, out_sum, True))
    down_whole = product_call(hidden, out_grad, [token])
    token, (down_whole,) = turn([scatter_a, scatter_b, out_flow], values=[down_whole])
    down_sum = sum_rows(down_whole)
    gate_whole = product_call(rows_in, gate_pre_grad, [token])
    token, (gate_whole,) = turn([scatter_a, scatter_b, out_flow], values=[gate_whole])

    gate_sum = sum_rows(gate_whole)
    residual_grads, normed_grads, logit_grads = [], [], []

    def residual_back(m, summed):
        gates = gates_own[m]
        gate_value_grad = jnp.sum(summed[tokens:], axis=0).reshape(expert_count, tokens).T
        select_grad = gates * (
            gate_value_grad - jnp.sum(gates * gate_value_grad, axis=1, keepdims=True)
        )
        logit_grad = select_grad.astype(BF16)
        normed_grad = summed[:tokens] + dot_t(logit_grad, router_all)
        residual_grad = cotangent[m, 0].astype(F32) + norm_back(
            normed_grad, unit_two[m], scale_two[m], gain_two
        )
        residual_grads.append(residual_grad)
        normed_grads.append(normed_grad)
        logit_grads.append(logit_grad)
        return residual_grad.astype(BF16)

    branch = [[], []]
    branch_a = Flow(gather_ctx_steps(residual_back(0, down_a[0]), branch[0]))
    up_whole = product_call(rows_in, up_pre_grad, [token])
    token, (up_whole,) = turn([branch_a, scatter_b, out_flow], values=[up_whole])
    up_sum = sum_rows(up_whole)
    token = turn([branch_a])

    joined_grads, normed_one_grads, pair_grads, branch_list = [], [], [], []

    def attention_back(m, token):
        branch_grad = jnp.concatenate(branch[m])
        attended_grad = dot_t(branch_grad, out_rows).astype(BF16)
        joined_grad, pair_part = attention_backward_call(
            joined_list[m], attended_grad, *tables[m], [token]
        )
        branch_list.append(branch_grad)
        joined_grads.append(joined_grad)
        pair_grads.append(pair_part)
        return pair_part

    done = attention_back(0, token)
    token = turn([scatter_b, out_flow], done, down_sum)
    branch_b = Flow(gather_ctx_steps(residual_back(1, down_b[0]), branch[1]))
    normed_one_grads.append(dot_t(joined_grads[0], projections))
    token = turn([branch_b], normed_one_grads[0])
    token = turn([branch_b])
    done = attention_back(1, token)
    token = turn([out_flow], done, gate_sum)
    normed_one_grads.append(dot_t(joined_grads[1], projections))
    attention_gain_grad = sum(
        jnp.sum(grad * unit, axis=0) for grad, unit in zip(normed_one_grads, units)
    )
    mixture_gain_grad = sum(
        jnp.sum(grad * unit, axis=0) for grad, unit in zip(normed_grads, unit_two)
    )
    router_grad = sum(dot_l(left, right) for left, right in zip(normed_two, logit_grads))
    pair_grad = (pair_grads[0] + pair_grads[1]).reshape(-1, few)
    pair_column = jnp.pad(pair_grad, ((0, 0), (0, rows - few))).reshape(-1)
    small_columns = jnp.concatenate(
        [attention_gain_grad[:, None], mixture_gain_grad[:, None], pair_column[:, None], router_grad], axis=1
    )
    small_columns = jnp.pad(small_columns, ((0, 0), (0, SMALL - small_columns.shape[1])))
    terms = jnp.stack(
        [grad.astype(BF16).reshape(4, tokens, width) for grad in normed_one_grads], axis=1
    )

    others = [attended_list[0], branch_list[0], attended_list[1], branch_list[1]] if heads_here else []

    def gradient_rows(part, parts, token):
        product = pair_product_call(
            part, parts, normed_one, joined_grads, small_columns.astype(BF16), others, [token]
        )
        return product.reshape(dp_size // parts, 4, 4, rows, -1)

    packed_sum, back_sum = [], []
    if two:
        d = lax.axis_index("dp").astype(jnp.int32)
        there = gradient_rows(1 - d, 2, token)
        here = gradient_rows(d, 2, there)
        token, (here,) = turn([out_flow], values=[here])
        last = Flow(
            undp_steps(*[[piece_of(part, 0, s) for s in range(4)] for part in (here, there)], packed_sum)
        )
    else:
        whole = gradient_rows(jnp.zeros((), jnp.int32), 1, token)
        whole = lax.psum_scatter(whole, "dp", scatter_dimension=0, tiled=True)
        token = turn([out_flow])
        last = Flow(unline_steps([piece_of(whole, 0, s) for s in range(4)], packed_sum))
    back_flow = Flow(scatter_ctx_steps(terms, back_sum))
    token = turn([last, back_flow, out_flow])
    token = turn([last, back_flow], up_sum)
    token, (gate_sum, up_sum, down_sum) = turn(
        [last], token, values=[value.astype(F32) for value in (gate_sum, up_sum, down_sum)]
    )
    if two:
        token = turn([last])
    summed = packed_sum[0]
    columns = 3 * per_ctx + SMALL
    swapped = lax.all_to_all(
        summed[..., :columns].astype(BF16), "ctx", split_axis=0, concat_axis=0, tiled=True
    )
    if heads_here:
        out_rows_sum = summed[..., columns:]
    else:
        out_grad_rows = sum(
            dot_l(left, right) for left, right in zip(attended_list, branch_list)
        ).astype(BF16)
        spread_rows = jnp.zeros((HALVES, 4, share, width), BF16)
        spread_rows = lax.dynamic_update_slice_in_dim(
            spread_rows, out_grad_rows.reshape(HALVES, 1, share, width), place, 1
        )
        out_rows_sum = lax.psum_scatter(
            spread_rows.reshape(-1, width), ("dp", "ctx", "expert"), scatter_dimension=0, tiled=True
        ).astype(F32)
        out_rows_sum = out_rows_sum.reshape(rows, 4, width // 4).transpose(1, 0, 2)
    *gradients, small_sums = unpack_call(swapped, out_rows_sum)
    outputs = [(residuals[m] + out_sum[0][m]).astype(BF16) for m in micros]
    input_grads = []
    for m in micros:
        stream = inputs[m, 0].astype(F32)
        scale_one = row_scale(stream)
        input_grads.append(
            residual_grads[m] + norm_back(back_sum[0][m], stream * scale_one, scale_one, gain_one)
        )
    return (
        jnp.stack(outputs)[:, None],
        jnp.stack(input_grads)[:, None],
        gradients[0],
        gradients[1],
        gradients[2],
        gradients[3],
        small_sums[:, 0],
        small_sums[:, 1],
        small_sums[:few, 2],
        small_sums[:, 3 : 3 + expert_count],
        gate_sum[None],
        up_sum[None],
        down_sum[None],
    )


def solution(mesh):
    tokens_4 = P(None, ("dp", "expert"), "ctx", None)
    group = P(None, ("dp", "expert"), None)
    matrix = P(("dp", "ctx", "expert"), None)
    vector = P(("dp", "ctx", "expert"))
    experts = P(("ctx", "expert"), "dp", None)
    return jax.shard_map(
        body,
        mesh=mesh,
        in_specs=(tokens_4, tokens_4, group, group, tokens_4)
        + (matrix,) * 4
        + (vector,) * 3
        + (matrix,)
        + (experts,) * 3,
        out_specs=(tokens_4, tokens_4)
        + (matrix,) * 4
        + (vector,) * 3
        + (matrix,)
        + (experts,) * 3,
        check_vma=False,
    )
```

time: 1350 us -> 1040 us (0.77)
  Pallas kernels: 0 us -> 294 us
  waiting for transfers between devices: 559 us -> 293 us
  matrix products: 296 us -> 49.4 us
  blocking collectives: 90.8 us -> 0 us
  local copies, waits for them, and re-layouts: 126 us -> 88 us
  other arithmetic: 108 us -> 145 us
    pallas_call x0 -> x52, Pallas kernels: none -> 294 us  [the longest x8 173 us: expert_call(): pl.pallas_call(functools.partial(expert_kernel, capacity, tile_f, tile_d,...]
    dot_general x54 -> x14, matrix products: 286 us -> 49.4 us  [the longest x6 29.7 us: dot_t(): lax.dot_general(a, b, (((1,), (1,)), ((), ())), preferred_element_type=F32)]
    ppermute x129 -> x96, waiting for transfers between devices: 399 us -> 233 us  [the longest x64 207 us: swap(): lax.ppermute(value, axis, [(i, i ^ bit) for i in range(lax.axis_size(axis...]
    reduce_scatter x5 -> x3, waiting for transfers between devices: 156 us -> 0.04 us  [sum_rows(): return lax.psum_scatter(whole, 'dp', scatter_dimension=0, tiled=True)]
    all_gather x1 -> x0, blocking collectives: 74.2 us -> none  [body(): lax.all_gather(routes[:, 0], ('ctx', 'expert'), axis=0, tiled=False)]
    all_gather x5 -> x3, waiting for transfers between devices: 0.01 us -> 33.3 us  [body(): experts = [lax.all_gather(own, 'dp', axis=0, tiled=True) for own in copies]]
    all_to_all x3 -> x2, waiting for transfers between devices: 2.24 us -> 26.2 us  [the longest x1 20.9 us: body(): lax.all_to_all(payload, 'ctx', split_axis=0, concat_axis=0, tiled=True)]
    another operation x13 -> x17, other arithmetic: 5.01 us -> 24.1 us  [the longest x6 8.86 us: gather_steps(): groups[0] = jnp.stack(blocks)]
  transfers between devices with their start and end apart: 142 -> 104, of which waited for: 50 -> 28; matrix products, arithmetic and copies ran while one was open for 35% -> 21% of each run, Pallas kernels for 0% -> 28%
where the time goes in v1:
time: 1040 us; the launch traced here: 1030 us
  Pallas kernels  294 us (28%)
  waiting for transfers between devices  293 us (28%)
  other arithmetic  145 us (14%)
  starting transfers between devices  141 us (14%)
  local copies, waits for them, and re-layouts  88 us (8%)
  matrix products  49.4 us (5%)
  between operations  17.6 us (2%)
    ppermute x64, waiting for transfers between devices, swap(): lax.ppermute(value, axis, [(i, i ^ bit) for i in range(lax.axis_size(axis...  207 us
    pallas_call x8, Pallas kernels, expert_call(): pl.pallas_call(functools.partial(expert_kernel, capacity, tile_f, tile_d,...  173 us
    ppermute x64, starting transfers between devices, swap(): lax.ppermute(value, axis, [(i, i ^ bit) for i in range(lax.axis_size(axis...  64.2 us
    pallas_call x3, Pallas kernels, product_call(): pl.pallas_call(product_kernel, grid=(columns // wide, rows // tile), in_s...  49.1 us
    unnamed x415, local copies, waits for them, and re-layouts  44.4 us
    all_gather x3, waiting for transfers between devices, body(): experts = [lax.all_gather(own, 'dp', axis=0, tiled=True) for own in copies]  33.3 us
    dot_general x6, matrix products, dot_t(): lax.dot_general(a, b, (((1,), (1,)), ((), ())), preferred_element_type=F32)  29.7 us
    pallas_call x2, Pallas kernels, attention_backward_call(): pl.pallas_call(functools.partial(backward_kernel, dh), grid=(heads,), in_...  22.6 us
  transfers between devices with their start and end apart: 104, of which 28 were waited for; matrix products, arithmetic and copies ran while one was open for 21% of the time, Pallas kernels for 28%

profile of v1, /device:TPU:0, one launch (start us, length us, event | category | flops | bytes accessed | tf_op | source)
XLA Modules:
  0.0 1027.2 jit_solution(2333260569922290392)
XLA Ops:
  25.0 20.9 %all-to-all-done = bf16[4,64,1664]{2,1,0:T(8,128)(2,1)S(1)} async-done(((bf16[4,64,1664]{2,1,0:T(8,128)(2,1)}), bf16[4,64,1664]{2,1,0:T(8,128)(2,1)S(1)}, u32[]{:S(2)}, u32[]{:S(2)}) %all-to-all-start) | async-done | bytes 852000 | tf_op jit(solution)/shard_map/all_to_all | solution.py:751
  57.9 14.6 %collective-permute-done.refs_0_ = bf16[4,64,2176]{2,1,0:T(8,128)(2,1)} collective-permute-done((bf16[4,64,2176]{2,1,0:T(8,128)(2,1)S(1)}, bf16[4,64,2176]{2,1,0:T(8,128)(2,1)}, u32[]{:S(2)}, u32[]{:S(2)}) %collective-permute-start) | collective-permute-done | bytes 1114144 | tf_op jit(solution)/shard_map/ppermute | solution.py:424
  86.3 15.2 %collective-permute-done.7.refs_2_ = bf16[4,64,2176]{2,1,0:T(8,128)(2,1)} collective-permute-done((bf16[4,64,2176]{2,1,0:T(8,128)(2,1)}, bf16[4,64,2176]{2,1,0:T(8,128)(2,1)}, u32[]{:S(2)}, u32[]{:S(2)}) %collective-permute-start.7) | collective-permute-done | bytes 1114144 | tf_op jit(solution)/shard_map/ppermute | solution.py:424
  118.5 15.4 %collective-permute-done.14.refs_3_ = bf16[2,128,2048]{2,1,0:T(8,128)(2,1)S(1)} collective-permute-done((bf16[2,128,2048]{2,1,0:T(8,128)(2,1)}, bf16[2,128,2048]{2,1,0:T(8,128)(2,1)S(1)}, u32[]{:S(2)}, u32[]{:S(2)}) %collective-permute-start.14) | collective-permute-done | bytes 1048608 | tf_op jit(solution)/shard_map/ppermute | solution.py:424
  163.7 13.8 %collective-permute-done.15.refs_0_ = bf16[4,64,2176]{2,1,0:T(8,128)(2,1)S(1)} collective-permute-done((bf16[4,64,2176]{2,1,0:T(8,128)(2,1)}, bf16[4,64,2176]{2,1,0:T(8,128)(2,1)S(1)}, u32[]{:S(2)}, u32[]{:S(2)}) %collective-permute-start.15) | collective-permute-done | bytes 1114144 | tf_op jit(solution)/shard_map/ppermute | solution.py:424
  187.2 6.3 fusion.16.joined_ref
  193.6 8.5 shard_map.263.refs_0_
  218.0 6.3 fusion.14.joined_ref
  224.3 8.5 shard_map.265.refs_3_.refs_2_
  233.7 6.2 collective-permute-done.21.refs_2_
  240.4 10.3 %collective-permute-done.19.refs_0_ = bf16[128,2048]{1,0:T(8,128)(2,1)} collective-permute-done((bf16[128,2048]{1,0:T(8,128)(2,1)S(1)}, bf16[128,2048]{1,0:T(8,128)(2,1)}, u32[]{:S(2)}, u32[]{:S(2)}) %collective-permute-start.19) | collective-permute-done | bytes 524320 | tf_op jit(solution)/shard_map/ppermute | solution.py:424
  267.4 5.4 collective-permute-start.23
  275.8 11.2 %collective-permute-done.23.refs_1_ = bf16[144,2048]{1,0:T(8,128)(2,1)} collective-permute-done((bf16[144,2048]{1,0:T(8,128)(2,1)}, bf16[144,2048]{1,0:T(8,128)(2,1)}, u32[]{:S(2)}, u32[]{:S(2)}) %collective-permute-start.23) | collective-permute-done | bytes 589856 | tf_op jit(solution)/shard_map/ppermute | solution.py:424
  290.0 9.8 collective-permute-done.27.refs_2_
  299.8 9.7 collective-permute-done.26.refs_1_
  319.2 33.2 %all-gather.8.cloned.1.call-done.refs_3_.wd_row.wd_col = bf16[1024,2048]{1,0:T(8,128)(2,1)} async-done(((bf16[512,2048]{1,0:T(8,128)(2,1)}), bf16[1024,2048]{1,0:T(8,128)(2,1)}) %all-gather.8.cloned.1.call-update) | async-done | bytes 4194320 | tf_op jit(solution)/shard_map/all_gather | solution.py:764
  369.7 21.7 %shard_map.270 = (bf16[2,4,128,2048]{3,2,1,0:T(8,128)(2,1)}, bf16[4,144,2048]{2,1,0:T(8,128)(2,1)}, bf16[2560,2048]{1,0:T(8,128)(2,1)}, bf16[2560,2048]{1,0:T(8,...) custom-call(s32[2]{0:T(128)} %pad_add_fusion.1.order_ref, ...), custom_call_target="tpu_custom_call" | custom-call | flops 1000 | bytes 1000 | tf_op jit(solution)/shard_map/pallas_call | solution.py:152
  395.9 21.6 %shard_map.272 = (bf16[2,4,128,2048]{3,2,1,0:T(8,128)(2,1)}, bf16[4,144,2048]{2,1,0:T(8,128)(2,1)}, bf16[2560,2048]{1,0:T(8,128)(2,1)}, bf16[2560,2048]{1,0:T(8,...) custom-call(s32[2]{0:T(128)} %pad_add_fusion.1.order_ref, ...), custom_call_target="tpu_custom_call", output_to_operand_aliasing={{2}: (10, {}), {3}: (11, {}), {4}: (12, {}), {5}: (13, {}),... | custom-call | flops 1000 | bytes 1000 | tf_op jit(solution)/shard_map/pallas_call | solution.py:152
  417.5 6.9 collective-permute-done.38.refs_3_
  424.5 12.3 %collective-permute-done.39.refs_4_ = bf16[144,2048]{1,0:T(8,128)(2,1)} collective-permute-done((bf16[144,2048]{1,0:T(8,128)(2,1)}, bf16[144,2048]{1,0:T(8,128)(2,1)}, u32[]{:S(2)}, u32[]{:S(2)}) %collective-permute-start.39) | collective-permute-done | bytes 589856 | tf_op jit(solution)/shard_map/ppermute | solution.py:424
  441.2 21.6 %shard_map.274 = (bf16[2,4,128,2048]{3,2,1,0:T(8,128)(2,1)}, bf16[4,144,2048]{2,1,0:T(8,128)(2,1)}, bf16[2560,2048]{1,0:T(8,128)(2,1)}, bf16[2560,2048]{1,0:T(8,...) custom-call(s32[2]{0:T(128)} %pad_add_fusion.1.order_ref, ...), custom_call_target="tpu_custom_call", output_to_operand_aliasing={{2}: (10, {}), {3}: (11, {}), {4}: (12, {}), {5}: (13, {}),... | custom-call | flops 1000 | bytes 1000 | tf_op jit(solution)/shard_map/pallas_call | solution.py:152
  468.1 21.6 %shard_map.276 = (bf16[2,4,128,2048]{3,2,1,0:T(8,128)(2,1)}, bf16[4,144,2048]{2,1,0:T(8,128)(2,1)}, bf16[2560,2048]{1,0:T(8,128)(2,1)}, bf16[2560,2048]{1,0:T(8,...) custom-call(s32[2]{0:T(128)} %pad_add_fusion.1.order_ref, ...), custom_call_target="tpu_custom_call", output_to_operand_aliasing={{2}: (10, {}), {3}: (11, {}), {4}: (12, {}), {5}: (13, {}),... | custom-call | flops 1000 | bytes 1000 | tf_op jit(solution)/shard_map/pallas_call | solution.py:152
  495.7 21.8 %shard_map.278 = (bf16[2,4,128,2048]{3,2,1,0:T(8,128)(2,1)}, bf16[4,144,2048]{2,1,0:T(8,128)(2,1)}, bf16[2560,2048]{1,0:T(8,128)(2,1)}, bf16[2560,2048]{1,0:T(8,...) custom-call(s32[2]{0:T(128)} %pad_add_fusion.1.order_ref, ...), custom_call_target="tpu_custom_call", output_to_operand_aliasing={{0}: (10, {}), {2}: (11, {}), {3}: (12, {}), {4}: (13, {}),... | custom-call | flops 1000 | bytes 1000 | tf_op jit(solution)/shard_map/pallas_call | solution.py:152
  525.7 21.5 %shard_map.280 = (bf16[2,4,128,2048]{3,2,1,0:T(8,128)(2,1)}, bf16[4,144,2048]{2,1,0:T(8,128)(2,1)}, bf16[2560,2048]{1,0:T(8,128)(2,1)}, bf16[2560,2048]{1,0:T(8,...) custom-call(s32[2]{0:T(128)} %pad_add_fusion.1.order_ref, ...), custom_call_target="tpu_custom_call", output_to_operand_aliasing={{0}: (10, {}), {2}: (11, {}), {3}: (12, {}), {4}: (13, {}),... | custom-call | flops 1000 | bytes 1000 | tf_op jit(solution)/shard_map/pallas_call | solution.py:152
  554.9 21.7 %shard_map.282 = (bf16[2,4,128,2048]{3,2,1,0:T(8,128)(2,1)}, bf16[4,144,2048]{2,1,0:T(8,128)(2,1)}, bf16[2560,2048]{1,0:T(8,128)(2,1)}, bf16[2560,2048]{1,0:T(8,...) custom-call(s32[2]{0:T(128)} %pad_add_fusion.1.order_ref, ...), custom_call_target="tpu_custom_call", output_to_operand_aliasing={{0}: (10, {}), {2}: (11, {}), {3}: (12, {}), {4}: (13, {}),... | custom-call | flops 1000 | bytes 1000 | tf_op jit(solution)/shard_map/pallas_call | solution.py:152
  590.0 5.4 collective-permute-start.53
  595.4 7.3 collective-permute-done.54.refs_1_
  604.1 21.7 %shard_map.284 = (bf16[2,4,128,2048]{3,2,1,0:T(8,128)(2,1)}, bf16[4,144,2048]{2,1,0:T(8,128)(2,1)}, bf16[2560,2048]{1,0:T(8,128)(2,1)}, bf16[2560,2048]{1,0:T(8,...) custom-call(s32[2]{0:T(128)} %pad_add_fusion.1.order_ref, ...), custom_call_target="tpu_custom_call", output_to_operand_aliasing={{0}: (10, {}), {2}: (11, {}), {3}: (12, {}), {4}: (13, {}),... | custom-call | flops 1000 | bytes 1000 | tf_op jit(solution)/shard_map/pallas_call | solution.py:152
  630.6 9.1 collective-permute-start.57
  639.7 17.0 %shard_map.286.refs_6_ = bf16[1024,2048]{1,0:T(8,128)(2,1)} custom-call(bf16[2560,1024]{1,0:T(8,128)(2,1)} %get-tuple-element.390.left_ref, bf16[2560,2048]{1,0:T(8,128)(2,1)} %get-tuple-element.391.right_ref, bf16[144,2048]{1,0:T(8,128)(2,1)} %get-tuple-element.387.refs_0_), custom_call_target="tpu_custom_call" | custom-call | flops 1000 | bytes 1000 | tf_op jit(solution)/shard_map/pallas_call | solution.py:198
  671.0 15.9 %shard_map.288.refs_4_ = bf16[2048,1024]{1,0:T(8,128)(2,1)} custom-call(bf16[2560,2048]{1,0:T(8,128)(2,1)} %get-tuple-element.399.left_ref, bf16[2560,1024]{1,0:T(8,128)(2,1)} %get-tuple-element.400.right_ref, bf16[144,2048]{1,0:T(8,128)(2,1)} %get-tuple-element.396.refs_0_), custom_call_target="tpu_custom_call" | custom-call | flops 1000 | bytes 1000 | tf_op jit(solution)/shard_map/pallas_call | solution.py:198
  698.3 5.9 collective-permute-start.69
  710.1 9.0 collective-permute-done.70.refs_4_
  719.2 16.1 %shard_map.290.refs_5_ = bf16[2048,1024]{1,0:T(8,128)(2,1)} custom-call(bf16[2560,2048]{1,0:T(8,128)(2,1)} %get-tuple-element.399.left_ref, bf16[2560,1024]{1,0:T(8,128)(2,1)} %get-tuple-element.405.right_ref, bf16[144,2048]{1,0:T(8,128)(2,1)} %get-tuple-element.402.refs_0_), custom_call_target="tpu_custom_call" | custom-call | flops 1000 | bytes 1000 | tf_op jit(solution)/shard_map/pallas_call | solution.py:198
  758.7 11.2 %shard_map.293 = (bf16[512,1536]{1,0:T(8,128)(2,1)S(1)}, f32[2,128]{1,0:T(2,128)S(1)}) custom-call(f32[512,1536]{1,0:T(8,128)S(1)} %copy-done.3, bf16[512,512]{1,0:T(8,128)(2,1)S(1)} %copy-done.34, f32[512,128]{1,0:T(8,128)S(1)} %copy-done.31, f32[512,128]{1,0:T(8,128)S(1)} %copy-done.23, f32[2,128]{1,0:T(2,128)S(1)} %copy-done.40, s32[512,1]{1,0:T(8,128)S(1)} %copy-done.29, ...), custom_call_target="tpu_custom_call" | custom-call | flops 1000 | bytes 1000 | tf_op jit(solution)/shard_map/pallas_call | solution.py:414
  770.0 8.4 fusion.12.refs_2_
  791.0 5.9 collective-permute-done.77.refs_0_
  806.1 11.4 %shard_map.297 = (bf16[512,1536]{1,0:T(8,128)(2,1)S(1)}, f32[2,128]{1,0:T(2,128)S(1)}) custom-call(f32[512,1536]{1,0:T(8,128)S(1)} %copy-done.1, bf16[512,512]{1,0:T(8,128)(2,1)S(1)} %convolution_convert_fusion.2.do_ref, f32[512,128]{1,0:T(8,128)S(1)} %copy-done.33, f32[512,128]{1,0:T(8,128)S(1)} %copy-done.25, f32[2,128]{1,0:T(2,128)S(1)} %copy-done.40, ...), custom_call_target="tpu_custom_call" | custom-call | flops 1000 | bytes 1000 | tf_op jit(solution)/shard_map/pallas_call | solution.py:414
  823.3 6.5 collective-permute-start.81
  829.8 9.8 fusion.5
  848.0 8.2 shard_map.299
  856.2 8.3 shard_map.300
  876.9 17.5 %collective-permute-done.83.refs_0_ = bf16[4,64,2176]{2,1,0:T(8,128)(2,1)S(1)} collective-permute-done((bf16[4,64,2176]{2,1,0:T(8,128)(2,1)}, bf16[4,64,2176]{2,1,0:T(8,128)(2,1)S(1)}, u32[]{:S(2)}, u32[]{:S(2)}) %collective-permute-start.83) | collective-permute-done | bytes 1114144 | tf_op jit(solution)/shard_map/ppermute | solution.py:424
  894.5 5.8 collective-permute-done.86.refs_3_
  921.4 11.8 %collective-permute-done.89.refs_2_ = bf16[2,128,2048]{2,1,0:T(8,128)(2,1)} collective-permute-done((bf16[2,128,2048]{2,1,0:T(8,128)(2,1)}, bf16[2,128,2048]{2,1,0:T(8,128)(2,1)}, u32[]{:S(2)}, u32[]{:S(2)}) %collective-permute-start.89) | collective-permute-done | bytes 1048608 | tf_op jit(solution)/shard_map/ppermute | solution.py:424
  948.2 12.2 %collective-permute-done.93.refs_2_ = bf16[4,64,2176]{2,1,0:T(8,128)(2,1)} collective-permute-done((bf16[4,64,2176]{2,1,0:T(8,128)(2,1)S(1)}, bf16[4,64,2176]{2,1,0:T(8,128)(2,1)}, u32[]{:S(2)}, u32[]{:S(2)}) %collective-permute-start.93) | collective-permute-done | bytes 1114144 | tf_op jit(solution)/shard_map/ppermute | solution.py:497
  972.4 18.5 %collective-permute-done.95.refs_2_ = bf16[4,64,2176]{2,1,0:T(8,128)(2,1)} collective-permute-done((bf16[4,64,2176]{2,1,0:T(8,128)(2,1)S(1)}, bf16[4,64,2176]{2,1,0:T(8,128)(2,1)}, u32[]{:S(2)}, u32[]{:S(2)}) %collective-permute-start.95) | collective-permute-done | bytes 1114144 | tf_op jit(solution)/shard_map/ppermute | solution.py:424
  1007.5 5.3 all-to-all-done.1.payload_ref
  (810 shorter events, 395.1 us)
Async XLA Ops:
  7.2 42.8 %collective-permute-start.3 = (bf16[2,128,2048]{2,1,0:T(8,128)(2,1)}, bf16[2,128,2048]{2,1,0:T(8,128)(2,1)}, u32[]{:S(2)}, u32[]{:S(2)}) collective-permute-start(bf16[2,128,2048]{2,1,0:T(8,128)(2,1)} %bitcast.489), channel_id=1, source_target_pairs={{0,1},{1,0},{2,3},{3,2},{4,5},{5,4},{6,7},{7,6},{8,9},{9,8},{10,11... | collective-permute-start | bytes 3145736 | tf_op jit(solution)/shard_map/ppermute | solution.py:424
  10.3 46.1 %collective-permute-start.4 = (bf16[2,128,2048]{2,1,0:T(8,128)(2,1)}, bf16[2,128,2048]{2,1,0:T(8,128)(2,1)}, u32[]{:S(2)}, u32[]{:S(2)}) collective-permute-start(bf16[2,128,2048]{2,1,0:T(8,128)(2,1)} %bitcast.490), channel_id=1, source_target_pairs={{1,2},{2,1},{5,6},{6,5},{9,10},{10,9},{13,14},{14,13},{17,18},{18,... | collective-permute-start | bytes 3145736 | tf_op jit(solution)/shard_map/ppermute | solution.py:560
  11.9 65.1 %collective-permute-start.10 = (bf16[2,128,2048]{2,1,0:T(8,128)(2,1)}, bf16[2,128,2048]{2,1,0:T(8,128)(2,1)}, u32[]{:S(2)}, u32[]{:S(2)}) collective-permute-start(bf16[2,128,2048]{2,1,0:T(8,128)(2,1)} %bitcast.491), channel_id=1, source_target_pairs={{0,8},{4,12},{8,0},{12,4},{1,9},{5,13},{9,1},{13,5},{2,10},{6,14},... | collective-permute-start | bytes 3145736 | tf_op jit(solution)/shard_map/ppermute | solution.py:424
  24.8 190.1 %all-gather.4.cloned.1.call-start = ((), (), s32[]{:S(2)}) async-start(), calls=%async_computation.5 | async-start | bytes 6291456 | tf_op jit(solution)/shard_map/all_gather | solution.py:764
  56.3 30.0 %collective-permute-start.8 = (bf16[2,128,2048]{2,1,0:T(8,128)(2,1)}, bf16[2,128,2048]{2,1,0:T(8,128)(2,1)}, u32[]{:S(2)}, u32[]{:S(2)}) collective-permute-start(bf16[2,128,2048]{2,1,0:T(8,128)(2,1)} %bitcast.494), channel_id=1, source_target_pairs={{0,8},{4,12},{8,0},{12,4},{1,9},{5,13},{9,1},{13,5},{2,10},{6,14},... | collective-permute-start | bytes 3145736 | tf_op jit(solution)/shard_map/ppermute | solution.py:424
  106.4 29.8 %collective-permute-start.11 = (bf16[4,64,2176]{2,1,0:T(8,128)(2,1)}, bf16[4,64,2176]{2,1,0:T(8,128)(2,1)S(1)}, u32[]{:S(2)}, u32[]{:S(2)}) collective-permute-start(bf16[4,64,2176]{2,1,0:T(8,128)(2,1)} %get-tuple-element.237.refs_4_), channel_id=1, source_target_pairs={{1,0},{2,3},{5,4},{6,7},{9,8},{10,11},{13,12},{14,15},{17,16},{18,... | collective-permute-start | bytes 3342344 | tf_op jit(solution)/shard_map/ppermute | solution.py:465
  116.8 46.8 %collective-permute-start.16 = (bf16[2,128,2048]{2,1,0:T(8,128)(2,1)}, bf16[2,128,2048]{2,1,0:T(8,128)(2,1)}, u32[]{:S(2)}, u32[]{:S(2)}) collective-permute-start(bf16[2,128,2048]{2,1,0:T(8,128)(2,1)} %get-tuple-element.239), channel_id=1, source_target_pairs={{1,2},{2,1},{5,6},{6,5},{9,10},{10,9},{13,14},{14,13},{17,18},{18,... | collective-permute-start | bytes 3145736 | tf_op jit(solution)/shard_map/ppermute | solution.py:564
  133.9 29.8 %collective-permute-start.17 = (bf16[2,128,2048]{2,1,0:T(8,128)(2,1)}, bf16[2,128,2048]{2,1,0:T(8,128)(2,1)}, u32[]{:S(2)}, u32[]{:S(2)}) collective-permute-start(bf16[2,128,2048]{2,1,0:T(8,128)(2,1)} %get-tuple-element.245), channel_id=1, source_target_pairs={{1,0},{2,3},{5,4},{6,7},{9,8},{10,11},{13,12},{14,15},{17,16},{18,... | collective-permute-start | bytes 3145736 | tf_op jit(solution)/shard_map/ppermute | solution.py:565
  145.5 32.0 %collective-permute-start.15 = (bf16[4,64,2176]{2,1,0:T(8,128)(2,1)}, bf16[4,64,2176]{2,1,0:T(8,128)(2,1)S(1)}, u32[]{:S(2)}, u32[]{:S(2)}) collective-permute-start(bf16[4,64,2176]{2,1,0:T(8,128)(2,1)} %get-tuple-element.542), channel_id=1, source_target_pairs={{0,16},{16,0},{1,17},{17,1},{2,18},{18,2},{3,19},{19,3},{4,20},{20... | collective-permute-start | bytes 3342344 | tf_op jit(solution)/shard_map/ppermute | solution.py:424
  150.8 125.0 %all-gather.6.cloned.1.call-start = ((), (), s32[]{:S(2)}) async-start(), calls=%async_computation.6 | async-start | bytes 6291456 | tf_op jit(solution)/shard_map/all_gather | solution.py:764
  209.7 142.7 %all-gather.8.cloned.1.call-start = ((), (), s32[]{:S(2)}) async-start(), calls=%async_computation.7 | async-start | bytes 6291456 | tf_op jit(solution)/shard_map/all_gather | solution.py:764
  209.8 30.6 %collective-permute-start.20 = (bf16[2,128,2048]{2,1,0:T(8,128)(2,1)}, bf16[2,128,2048]{2,1,0:T(8,128)(2,1)S(1)}, u32[]{:S(2)}, u32[]{:S(2)}) collective-permute-start(bf16[2,128,2048]{2,1,0:T(8,128)(2,1)} %get-tuple-element.247), channel_id=1, source_target_pairs={{1,0},{2,3},{5,4},{6,7},{9,8},{10,11},{13,12},{14,15},{17,16},{18,... | collective-permute-start | bytes 3145736 | tf_op jit(solution)/shard_map/ppermute | solution.py:568
  217.2 33.5 %collective-permute-start.19 = (bf16[128,2048]{1,0:T(8,128)(2,1)S(1)}, bf16[128,2048]{1,0:T(8,128)(2,1)}, u32[]{:S(2)}, u32[]{:S(2)}) collective-permute-start(bf16[128,2048]{1,0:T(8,128)(2,1)S(1)} %fusion.72), channel_id=1, source_target_pairs={{0,8},{4,12},{8,0},{12,4},{1,9},{5,13},{9,1},{13,5},{2,10},{6,14},... | collective-permute-start | bytes 1572872 | tf_op jit(solution)/shard_map/ppermute | solution.py:424
  256.9 52.5 %collective-permute-start.28 = (bf16[4,2,128,2048]{3,2,1,0:T(8,128)(2,1)}, bf16[4,2,128,2048]{3,2,1,0:T(8,128)(2,1)}, u32[]{:S(2)}, u32[]{:S(2)}) collective-permute-start(bf16[4,2,128,2048]{3,2,1,0:T(8,128)(2,1)} %pad_maximum_fusion.1.up_ref), channel_id=1, source_target_pairs={{0,4},{4,0},{8,12},{12,8},{1,5},{5,1},{9,13},{13,9},{2,6},{6,2},{1... | collective-permute-start | bytes 12582920 | tf_op jit(solution)/shard_map/ppermute | solution.py:424
  289.9 488.4 %reduce-scatter.4.cloned.1.call-start = ((), (), s32[]{:S(2)}) async-start(), calls=%async_computation.8 | async-start | bytes 6291456 | tf_op jit(solution)/shard_map/reduce_scatter | solution.py:671
  313.2 39.3 %collective-permute-start.30 = (bf16[4,2,128,2048]{3,2,1,0:T(8,128)(2,1)}, bf16[4,2,128,2048]{3,2,1,0:T(8,128)(2,1)}, u32[]{:S(2)}, u32[]{:S(2)}) collective-permute-start(bf16[4,2,128,2048]{3,2,1,0:T(8,128)(2,1)} %pad_maximum_fusion.2.up_ref), channel_id=1, source_target_pairs={{0,4},{4,0},{8,12},{12,8},{1,5},{5,1},{9,13},{13,9},{2,6},{6,2},{1... | collective-permute-start | bytes 12582920 | tf_op jit(solution)/shard_map/ppermute | solution.py:424
  315.2 37.3 %collective-permute-start.31 = (bf16[128,2048]{1,0:T(8,128)(2,1)}, bf16[128,2048]{1,0:T(8,128)(2,1)S(1)}, u32[]{:S(2)}, u32[]{:S(2)}) collective-permute-start(bf16[128,2048]{1,0:T(8,128)(2,1)} %fusion.71), channel_id=1, source_target_pairs={{0,8},{4,12},{8,0},{12,4},{1,9},{5,13},{9,1},{13,5},{2,10},{6,14},... | collective-permute-start | bytes 1572872 | tf_op jit(solution)/shard_map/ppermute | solution.py:424
  316.7 35.7 %collective-permute-start.29 = (bf16[144,2048]{1,0:T(8,128)(2,1)}, bf16[144,2048]{1,0:T(8,128)(2,1)S(1)}, u32[]{:S(2)}, u32[]{:S(2)}) collective-permute-start(bf16[144,2048]{1,0:T(8,128)(2,1)} %get-tuple-element.253), channel_id=1, source_target_pairs={{1,0},{2,3},{5,4},{6,7},{9,8},{10,11},{13,12},{14,15},{17,16},{18,... | collective-permute-start | bytes 1769480 | tf_op jit(solution)/shard_map/ppermute | solution.py:540
  357.5 33.9 %collective-permute-start.32 = (bf16[4,144,2048]{2,1,0:T(8,128)(2,1)}, bf16[4,144,2048]{2,1,0:T(8,128)(2,1)}, u32[]{:S(2)}, u32[]{:S(2)}) collective-permute-start(bf16[4,144,2048]{2,1,0:T(8,128)(2,1)} %pad_maximum_fusion.3.norm_ref), channel_id=1, source_target_pairs={{0,4},{4,0},{8,12},{12,8},{1,5},{5,1},{9,13},{13,9},{2,6},{6,2},{1... | collective-permute-start | bytes 7077896 | tf_op jit(solution)/shard_map/ppermute | solution.py:424
  357.5 66.9 %collective-permute-start.35 = (bf16[4,144,2048]{2,1,0:T(8,128)(2,1)}, bf16[4,144,2048]{2,1,0:T(8,128)(2,1)S(1)}, u32[]{:S(2)}, u32[]{:S(2)}) collective-permute-start(bf16[4,144,2048]{2,1,0:T(8,128)(2,1)} %pad_maximum_fusion.3.norm_ref), channel_id=1, source_target_pairs={{0,8},{4,12},{8,0},{12,4},{1,9},{5,13},{9,1},{13,5},{2,10},{6,14},... | collective-permute-start | bytes 7077896 | tf_op jit(solution)/shard_map/ppermute | solution.py:424
  369.2 55.2 %collective-permute-start.38 = (bf16[144,2048]{1,0:T(8,128)(2,1)}, bf16[144,2048]{1,0:T(8,128)(2,1)S(1)}, u32[]{:S(2)}, u32[]{:S(2)}) collective-permute-start(bf16[144,2048]{1,0:T(8,128)(2,1)} %get-tuple-element.579), channel_id=1, source_target_pairs={{0,8},{4,12},{8,0},{12,4},{1,9},{5,13},{9,1},{13,5},{2,10},{6,14},... | collective-permute-start | bytes 1769480 | tf_op jit(solution)/shard_map/ppermute | solution.py:424
  391.5 33.0 %collective-permute-start.36 = (bf16[144,2048]{1,0:T(8,128)(2,1)}, bf16[144,2048]{1,0:T(8,128)(2,1)}, u32[]{:S(2)}, u32[]{:S(2)}) collective-permute-start(bf16[144,2048]{1,0:T(8,128)(2,1)} %get-tuple-element.270), channel_id=1, source_target_pairs={{1,2},{2,1},{5,6},{6,5},{9,10},{10,9},{13,14},{14,13},{17,18},{18,... | collective-permute-start | bytes 1769480 | tf_op jit(solution)/shard_map/ppermute | solution.py:534
  393.0 31.5 %collective-permute-start.37 = (bf16[144,2048]{1,0:T(8,128)(2,1)}, bf16[144,2048]{1,0:T(8,128)(2,1)}, u32[]{:S(2)}, u32[]{:S(2)}) collective-permute-start(bf16[144,2048]{1,0:T(8,128)(2,1)} %get-tuple-element.271), channel_id=1, source_target_pairs={{1,0},{2,3},{5,4},{6,7},{9,8},{10,11},{13,12},{14,15},{17,16},{18,... | collective-permute-start | bytes 1769480 | tf_op jit(solution)/shard_map/ppermute | solution.py:535
  394.3 42.5 %collective-permute-start.39 = (bf16[144,2048]{1,0:T(8,128)(2,1)}, bf16[144,2048]{1,0:T(8,128)(2,1)}, u32[]{:S(2)}, u32[]{:S(2)}) collective-permute-start(bf16[144,2048]{1,0:T(8,128)(2,1)} %get-tuple-element.270), channel_id=1, source_target_pairs={{0,8},{4,12},{8,0},{12,4},{1,9},{5,13},{9,1},{13,5},{2,10},{6,14},... | collective-permute-start | bytes 1769480 | tf_op jit(solution)/shard_map/ppermute | solution.py:424
  525.7 50.9 %collective-permute-start.49 = (bf16[4,144,2048]{2,1,0:T(8,128)(2,1)}, bf16[4,144,2048]{2,1,0:T(8,128)(2,1)S(1)}, u32[]{:S(2)}, u32[]{:S(2)}) collective-permute-start(bf16[4,144,2048]{2,1,0:T(8,128)(2,1)} %get-tuple-element.337), channel_id=1, source_target_pairs={{0,4},{4,0},{8,12},{12,8},{1,5},{5,1},{9,13},{13,9},{2,6},{6,2},{1... | collective-permute-start | bytes 7077896 | tf_op jit(solution)/shard_map/ppermute | solution.py:424
  552.4 104.4 %collective-permute-start.61 = (bf16[2,4,128,2048]{3,2,1,0:T(8,128)(2,1)}, bf16[2,4,128,2048]{3,2,1,0:T(8,128)(2,1)}, u32[]{:S(2)}, u32[]{:S(2)}) collective-permute-start(bf16[2,4,128,2048]{3,2,1,0:T(8,128)(2,1)} %get-tuple-element.389), channel_id=1, source_target_pairs={{0,4},{4,0},{8,12},{12,8},{1,5},{5,1},{9,13},{13,9},{2,6},{6,2},{1... | collective-permute-start | bytes 12582920 | tf_op jit(solution)/shard_map/ppermute | solution.py:424
  581.8 74.9 %collective-permute-start.60 = (bf16[4,144,2048]{2,1,0:T(8,128)(2,1)}, bf16[4,144,2048]{2,1,0:T(8,128)(2,1)}, u32[]{:S(2)}, u32[]{:S(2)}) collective-permute-start(bf16[4,144,2048]{2,1,0:T(8,128)(2,1)} %get-tuple-element.388), channel_id=1, source_target_pairs={{0,4},{4,0},{8,12},{12,8},{1,5},{5,1},{9,13},{13,9},{2,6},{6,2},{1... | collective-permute-start | bytes 7077896 | tf_op jit(solution)/shard_map/ppermute | solution.py:424
  588.0 37.8 %collective-permute-start.55 = (bf16[144,2048]{1,0:T(8,128)(2,1)S(1)}, bf16[144,2048]{1,0:T(8,128)(2,1)S(1)}, u32[]{:S(2)}, u32[]{:S(2)}) collective-permute-start(bf16[144,2048]{1,0:T(8,128)(2,1)S(1)} %get-tuple-element.567), channel_id=1, source_target_pairs={{0,8},{4,12},{8,0},{12,4},{1,9},{5,13},{9,1},{13,5},{2,10},{6,14},... | collective-permute-start | bytes 1769480 | tf_op jit(solution)/shard_map/ppermute | solution.py:424
  590.0 37.3 %collective-permute-start.53 = (bf16[144,2048]{1,0:T(8,128)(2,1)S(1)}, bf16[144,2048]{1,0:T(8,128)(2,1)}, u32[]{:S(2)}, u32[]{:S(2)}) collective-permute-start(bf16[144,2048]{1,0:T(8,128)(2,1)S(1)} %fusion.74), channel_id=1, source_target_pairs={{0,1},{3,2},{4,5},{7,6},{8,9},{11,10},{12,13},{15,14},{16,17},{19,... | collective-permute-start | bytes 1769480 | tf_op jit(solution)/shard_map/ppermute | solution.py:591
  626.6 30.2 %collective-permute-start.59 = (bf16[144,2048]{1,0:T(8,128)(2,1)}, bf16[144,2048]{1,0:T(8,128)(2,1)}, u32[]{:S(2)}, u32[]{:S(2)}) collective-permute-start(bf16[144,2048]{1,0:T(8,128)(2,1)} %get-tuple-element.565), channel_id=1, source_target_pairs={{0,8},{4,12},{8,0},{12,4},{1,9},{5,13},{9,1},{13,5},{2,10},{6,14},... | collective-permute-start | bytes 1769480 | tf_op jit(solution)/shard_map/ppermute | solution.py:424
  657.6 159.9 %reduce-scatter.6.cloned.1.call-start = ((), (), s32[]{:S(2)}) async-start(), calls=%async_computation.9 | async-start | bytes 6291456 | tf_op jit(solution)/shard_map/reduce_scatter | solution.py:671
  663.9 28.7 %collective-permute-start.65 = (bf16[2,128,2048]{2,1,0:T(8,128)(2,1)S(1)}, bf16[2,128,2048]{2,1,0:T(8,128)(2,1)}, u32[]{:S(2)}, u32[]{:S(2)}) collective-permute-start(bf16[2,128,2048]{2,1,0:T(8,128)(2,1)S(1)} %get-tuple-element.562), channel_id=1, source_target_pairs={{0,8},{4,12},{8,0},{12,4},{1,9},{5,13},{9,1},{13,5},{2,10},{6,14},... | collective-permute-start | bytes 3145736 | tf_op jit(solution)/shard_map/ppermute | solution.py:424
  692.7 224.6 %reduce-scatter.8.cloned.1.call-start = ((), (), s32[]{:S(2)}) async-start(), calls=%async_computation.10 | async-start | bytes 6291456 | tf_op jit(solution)/shard_map/reduce_scatter | solution.py:671
  692.7 85.6 %collective-permute-start.74 = (bf16[2,4,128,2048]{3,2,1,0:T(8,128)(2,1)}, bf16[2,4,128,2048]{3,2,1,0:T(8,128)(2,1)}, u32[]{:S(2)}, u32[]{:S(2)}) collective-permute-start(bf16[2,4,128,2048]{3,2,1,0:T(8,128)(2,1)} %get-tuple-element.409), channel_id=1, source_target_pairs={{0,4},{4,0},{8,12},{12,8},{1,5},{5,1},{9,13},{13,9},{2,6},{6,2},{1... | collective-permute-start | bytes 12582920 | tf_op jit(solution)/shard_map/ppermute | solution.py:424
  696.6 42.3 %collective-permute-start.68 = (bf16[144,2048]{1,0:T(8,128)(2,1)}, bf16[144,2048]{1,0:T(8,128)(2,1)}, u32[]{:S(2)}, u32[]{:S(2)}) collective-permute-start(bf16[144,2048]{1,0:T(8,128)(2,1)} %fusion.43), channel_id=1, source_target_pairs={{1,2},{2,1},{5,6},{6,5},{9,10},{10,9},{13,14},{14,13},{17,18},{18,... | collective-permute-start | bytes 1769480 | tf_op jit(solution)/shard_map/ppermute | solution.py:608
  698.3 40.7 %collective-permute-start.69 = (bf16[144,2048]{1,0:T(8,128)(2,1)}, bf16[144,2048]{1,0:T(8,128)(2,1)}, u32[]{:S(2)}, u32[]{:S(2)}) collective-permute-start(bf16[144,2048]{1,0:T(8,128)(2,1)} %fusion.43), channel_id=1, source_target_pairs={{0,1},{3,2},{4,5},{7,6},{8,9},{11,10},{12,13},{15,14},{16,17},{19,... | collective-permute-start | bytes 1769480 | tf_op jit(solution)/shard_map/ppermute | solution.py:609
  736.1 42.2 %collective-permute-start.73 = (bf16[2,128,2048]{2,1,0:T(8,128)(2,1)}, bf16[2,128,2048]{2,1,0:T(8,128)(2,1)}, u32[]{:S(2)}, u32[]{:S(2)}) collective-permute-start(bf16[2,128,2048]{2,1,0:T(8,128)(2,1)} %get-tuple-element.560), channel_id=1, source_target_pairs={{0,8},{4,12},{8,0},{12,4},{1,9},{5,13},{9,1},{13,5},{2,10},{6,14},... | collective-permute-start | bytes 3145736 | tf_op jit(solution)/shard_map/ppermute | solution.py:424
  738.1 129.6 %collective-permute-start.82 = (bf16[2,128,2048]{2,1,0:T(8,128)(2,1)}, bf16[2,128,2048]{2,1,0:T(8,128)(2,1)}, u32[]{:S(2)}, u32[]{:S(2)}) collective-permute-start(bf16[2,128,2048]{2,1,0:T(8,128)(2,1)} %get-tuple-element.559), channel_id=1, source_target_pairs={{0,8},{4,12},{8,0},{12,4},{1,9},{5,13},{9,1},{13,5},{2,10},{6,14},... | collective-permute-start | bytes 3145736 | tf_op jit(solution)/shard_map/ppermute | solution.py:424
  743.5 34.8 %collective-permute-start.71 = (bf16[144,2048]{1,0:T(8,128)(2,1)}, bf16[144,2048]{1,0:T(8,128)(2,1)}, u32[]{:S(2)}, u32[]{:S(2)}) collective-permute-start(bf16[144,2048]{1,0:T(8,128)(2,1)} %get-tuple-element.548), channel_id=1, source_target_pairs={{1,2},{2,1},{5,6},{6,5},{9,10},{10,9},{13,14},{14,13},{17,18},{18,... | collective-permute-start | bytes 1769480 | tf_op jit(solution)/shard_map/ppermute | solution.py:614
  745.0 33.3 %collective-permute-start.72 = (bf16[144,2048]{1,0:T(8,128)(2,1)}, bf16[144,2048]{1,0:T(8,128)(2,1)}, u32[]{:S(2)}, u32[]{:S(2)}) collective-permute-start(bf16[144,2048]{1,0:T(8,128)(2,1)} %get-tuple-element.547), channel_id=1, source_target_pairs={{0,1},{1,0},{2,3},{3,2},{4,5},{5,4},{6,7},{7,6},{8,9},{9,8},{10,11... | collective-permute-start | bytes 1769480 | tf_op jit(solution)/shard_map/ppermute | solution.py:424
  788.1 29.4 %collective-permute-start.76 = (bf16[2,128,2048]{2,1,0:T(8,128)(2,1)}, bf16[2,128,2048]{2,1,0:T(8,128)(2,1)S(1)}, u32[]{:S(2)}, u32[]{:S(2)}) collective-permute-start(bf16[2,128,2048]{2,1,0:T(8,128)(2,1)} %fusion.33), channel_id=1, source_target_pairs={{0,1},{3,2},{4,5},{7,6},{8,9},{11,10},{12,13},{15,14},{16,17},{19,... | collective-permute-start | bytes 3145736 | tf_op jit(solution)/shard_map/ppermute | solution.py:591
  822.6 45.1 %collective-permute-start.80 = (bf16[2,128,2048]{2,1,0:T(8,128)(2,1)}, bf16[2,128,2048]{2,1,0:T(8,128)(2,1)S(1)}, u32[]{:S(2)}, u32[]{:S(2)}) collective-permute-start(bf16[2,128,2048]{2,1,0:T(8,128)(2,1)} %fusion.29), channel_id=1, source_target_pairs={{1,2},{2,1},{5,6},{6,5},{9,10},{10,9},{13,14},{14,13},{17,18},{18,... | collective-permute-start | bytes 3145736 | tf_op jit(solution)/shard_map/ppermute | solution.py:608
  823.3 44.4 %collective-permute-start.81 = (bf16[2,128,2048]{2,1,0:T(8,128)(2,1)}, bf16[2,128,2048]{2,1,0:T(8,128)(2,1)}, u32[]{:S(2)}, u32[]{:S(2)}) collective-permute-start(bf16[2,128,2048]{2,1,0:T(8,128)(2,1)} %fusion.29), channel_id=1, source_target_pairs={{0,1},{3,2},{4,5},{7,6},{8,9},{11,10},{12,13},{15,14},{16,17},{19,... | collective-permute-start | bytes 3145736 | tf_op jit(solution)/shard_map/ppermute | solution.py:609
  845.3 55.0 %collective-permute-start.84 = (bf16[2,2,128,2048]{3,2,1,0:T(8,128)(2,1)}, bf16[2,2,128,2048]{3,2,1,0:T(8,128)(2,1)}, u32[]{:S(2)}, u32[]{:S(2)}) collective-permute-start(bf16[2,2,128,2048]{3,2,1,0:T(8,128)(2,1)} %fusion.25), channel_id=1, source_target_pairs={{0,4},{4,0},{8,12},{12,8},{1,5},{5,1},{9,13},{13,9},{2,6},{6,2},{1... | collective-permute-start | bytes 6291464 | tf_op jit(solution)/shard_map/ppermute | solution.py:424
  875.9 45.5 %collective-permute-start.87 = (bf16[4,64,2176]{2,1,0:T(8,128)(2,1)}, bf16[4,64,2176]{2,1,0:T(8,128)(2,1)S(1)}, u32[]{:S(2)}, u32[]{:S(2)}) collective-permute-start(bf16[4,64,2176]{2,1,0:T(8,128)(2,1)} %get-tuple-element.555), channel_id=1, source_target_pairs={{0,16},{16,0},{1,17},{17,1},{2,18},{18,2},{3,19},{19,3},{4,20},{20... | collective-permute-start | bytes 3342344 | tf_op jit(solution)/shard_map/ppermute | solution.py:424
  903.4 29.8 %collective-permute-start.88 = (bf16[4,64,2176]{2,1,0:T(8,128)(2,1)}, bf16[4,64,2176]{2,1,0:T(8,128)(2,1)}, u32[]{:S(2)}, u32[]{:S(2)}) collective-permute-start(bf16[4,64,2176]{2,1,0:T(8,128)(2,1)} %fusion.32), channel_id=1, source_target_pairs={{0,1},{3,2},{4,5},{7,6},{8,9},{11,10},{12,13},{15,14},{16,17},{19,... | collective-permute-start | bytes 3342344 | tf_op jit(solution)/shard_map/ppermute | solution.py:492
  912.8 35.5 %collective-permute-start.91 = (bf16[4,64,2176]{2,1,0:T(8,128)(2,1)}, bf16[4,64,2176]{2,1,0:T(8,128)(2,1)}, u32[]{:S(2)}, u32[]{:S(2)}) collective-permute-start(bf16[4,64,2176]{2,1,0:T(8,128)(2,1)} %get-tuple-element.553), channel_id=1, source_target_pairs={{0,16},{16,0},{1,17},{17,1},{2,18},{18,2},{3,19},{19,3},{4,20},{20... | collective-permute-start | bytes 3342344 | tf_op jit(solution)/shard_map/ppermute | solution.py:424
  914.2 58.2 %collective-permute-start.90 = (bf16[4,64,2176]{2,1,0:T(8,128)(2,1)}, bf16[4,64,2176]{2,1,0:T(8,128)(2,1)}, u32[]{:S(2)}, u32[]{:S(2)}) collective-permute-start(bf16[4,64,2176]{2,1,0:T(8,128)(2,1)} %get-tuple-element.554), channel_id=1, source_target_pairs={{0,16},{16,0},{1,17},{17,1},{2,18},{18,2},{3,19},{19,3},{4,20},{20... | collective-permute-start | bytes 3342344 | tf_op jit(solution)/shard_map/ppermute | solution.py:424
  (262 other events, 3252.8 us)
Sparse Core Ops, SparseCore 0:
  150.9 62.4 all-gather.3
  215.5 59.1 all-gather.5
  290.1 62.3 all-gather.7
  657.7 51.7 reduce-scatter.3
  712.4 54.3 reduce-scatter.5
  768.9 54.2 reduce-scatter.7

commit v2 on v1

--- a/solution.py
+++ b/solution.py
@@ -31,10 +31,10 @@
 
 def expert_kernel(
     capacity, tile_f, tile_d, tokens, extra, order_ref, norm_ref, up_ref,
-    wg_col, wu_col, wd_row, wd_col, wg_row, wu_row, *refs
+    wg_hbm, wu_hbm, wd_hbm, *refs
 ):
     shared_ref, back_ref, rows_ref, dy_ref, h_ref, dhg_ref, dhu_ref = refs[extra : extra + 7]
-    ru_ref, gate_rows_ref, sums_ref, slot_ref = refs[extra + 7 :]
+    ru_ref, gate_rows_ref, sums_ref, slot_ref, wg_ref, wu_ref, wd_ref, arrived = refs[extra + 7 :]
     group, width = norm_ref.shape[0], norm_ref.shape[2]
     first_steps = h_ref.shape[1] // tile_f
     tiles = width // tile_d
@@ -42,12 +42,23 @@
     expert = order_ref[0]
     tail = pl.ds(tokens, TAIL)
 
+    def copies(j):
+        at = pl.ds(j * tile_f, tile_f)
+        return [
+            pltpu.make_async_copy(wg_hbm.at[:, at], wg_ref.at[:, at], arrived.at[j, 0]),
+            pltpu.make_async_copy(wu_hbm.at[:, at], wu_ref.at[:, at], arrived.at[j, 1]),
+            pltpu.make_async_copy(wd_hbm.at[at, :], wd_ref.at[at, :], arrived.at[j, 2]),
+        ]
+
     def chosen(b):
         slots = lax.broadcasted_iota(jnp.int32, (capacity, tokens), 0).astype(F32)
         return slots == slot_ref[b : b + 1, :]
 
     @pl.when(step == 0)
     def _():
+        for j in range(first_steps):
+            for copy in copies(j):
+                copy.start()
         lanes = pl.ds(pl.multiple_of(expert * tokens, tokens), tokens)
         gates = jnp.concatenate(
             [
@@ -77,12 +88,18 @@
             gate_rows_ref[at, :] = gate_rows
         sums_ref[...] = jnp.zeros_like(sums_ref)
 
+    for j in range(first_steps):
+        @pl.when(step == j)
+        def _():
+            for copy in copies(j):
+                copy.wait()
+
     @pl.when(step < first_steps)
     def _():
         at = pl.ds(pl.multiple_of(step * tile_f, tile_f), tile_f)
-        hg = dot(rows_ref[...], wg_col[...])
-        hu = dot(rows_ref[...], wu_col[...])
-        dh = dot_t(dy_ref[...], wd_row[...])
+        hg = dot(rows_ref[...], wg_ref[:, at])
+        hu = dot(rows_ref[...], wu_ref[:, at])
+        dh = dot_t(dy_ref[...], wd_ref[at, :])
         sig = jax.nn.sigmoid(hg)
         act = hg * sig
         h_ref[:, at] = (act * hu).astype(BF16)
@@ -93,10 +110,10 @@
     def _():
         tile = (step - first_steps + order_ref[1] + 1) % tiles
         at = pl.ds(pl.multiple_of(tile * tile_d, tile_d), tile_d)
-        y = dot(h_ref[...], wd_col[...]).astype(BF16).astype(F32)
+        y = dot(h_ref[...], wd_ref[:, at]).astype(BF16).astype(F32)
         sums_ref[...] += jnp.sum(y * ru_ref[:, at].astype(F32), axis=1, keepdims=True)
         gy = (gate_rows_ref[...] * y).astype(BF16)
-        dx = (dot_t(dhg_ref[...], wg_row[...]) + dot_t(dhu_ref[...], wu_row[...])).astype(BF16)
+        dx = (dot_t(dhg_ref[...], wg_ref[at, :]) + dot_t(dhu_ref[...], wu_ref[at, :])).astype(BF16)
         for b in range(group):
             hot = jnp.where(chosen(b), 1.0, 0.0).astype(BF16)
             lo = b * capacity
@@ -128,9 +145,6 @@
     tiles = width // tile_d
     anywhere = pl.BlockSpec(memory_space=pl.ANY)
 
-    def early(i, o):
-        return jnp.minimum(i, first_steps - 1)
-
     def late(i, o):
         return (jnp.maximum(i - first_steps, 0) + o[1] + 1) % tiles
 
@@ -139,9 +153,6 @@
 
     def column(shape, place):
         return pl.BlockSpec(shape, lambda i, o: (0,) * (len(shape) - 1) + (place(i, o),))
-
-    def row(shape, place):
-        return pl.BlockSpec(shape, lambda i, o: (place(i, o), 0))
 
     micro, shared_in = shared
     shared_in = [] if shared_in is None else [shared_in]
@@ -157,12 +168,9 @@
             in_specs=[
                 fixed(norm.shape),
                 pl.BlockSpec((group, 1, tokens, width), lambda i, o: (0, micro, 0, 0)),
-                column((width, tile_f), early),
-                column((width, tile_f), early),
-                row((tile_f, width), early),
-                column((hidden, tile_d), late),
-                row((tile_d, hidden), late),
-                row((tile_d, hidden), late),
+                anywhere,
+                anywhere,
+                anywhere,
             ]
             + [anywhere] * extra,
             out_specs=[
@@ -175,15 +183,19 @@
                 pltpu.VMEM((rows, 1), F32),
                 pltpu.VMEM((rows, 1), F32),
                 pltpu.VMEM((group, tokens), F32),
+                pltpu.VMEM(wg.shape, BF16),
+                pltpu.VMEM(wu.shape, BF16),
+                pltpu.VMEM(wd.shape, BF16),
+                pltpu.SemaphoreType.DMA((first_steps, 3)),
             ],
         ),
         out_shape=[struct((2, group, tokens, width), BF16), struct((group, tokens + TAIL, width), BF16)]
         + [struct((parts * rows, size), BF16) for size in sizes],
-        input_output_aliases={9 + len(deps) + i: i for i in range(len(shared_in))}
-        | {9 + len(deps) + len(shared_in) + i: 2 + i for i in range(len(kept_in))},
-        compiler_params=pltpu.CompilerParams(vmem_limit_bytes=56 * 2**20),
+        input_output_aliases={6 + len(deps) + i: i for i in range(len(shared_in))}
+        | {6 + len(deps) + len(shared_in) + i: 2 + i for i in range(len(kept_in))},
+        compiler_params=pltpu.CompilerParams(vmem_limit_bytes=58 * 2**20),
         cost_estimate=QUICK,
-    )(order, norm, up, wg, wu, wd, wd, wg, wu, *deps, *shared_in, *kept_in)
+    )(order, norm, up, wg, wu, wd, *deps, *shared_in, *kept_in)
     return results[0], results[1], results[2:]
 
 
@@ -260,7 +272,7 @@
     )(part.reshape(1), lefts[0], rights[0], lefts[1], rights[1], small, *others, *deps)
 
 
-def unpack_kernel(payload_ref, out_rows_ref, query_ref, key_ref, value_ref, output_ref, small_ref):
+def unpack_kernel(payload_ref, query_ref, key_ref, value_ref, small_ref):
     ctx_size, _, columns = payload_ref.shape
     heads = (columns - SMALL) // (3 * DH)
     half = heads // HALVES
@@ -270,21 +282,19 @@
             for t, ref in enumerate((query_ref, key_ref, value_ref)):
                 at = (3 * head + t) * DH
                 ref[:, to * DH : (to + 1) * DH] = payload_ref[c, :, at : at + DH].astype(F32)
-        wide = out_rows_ref.shape[2]
-        output_ref[:, c * wide : (c + 1) * wide] = out_rows_ref[c]
     small_ref[...] = sum(
         payload_ref[c, :, columns - SMALL :].astype(F32) for c in range(ctx_size)
     )
 
 
-def unpack_call(payload, out_rows):
-    rows = payload.shape[1]
-    width = out_rows.shape[0] * out_rows.shape[2]
+def unpack_call(payload):
+    ctx_size, rows, columns = payload.shape
+    width = ctx_size * (columns - SMALL) // 3
     struct = jax.ShapeDtypeStruct
     return pl.pallas_call(
         unpack_kernel,
-        out_shape=[struct((rows, width), F32)] * 4 + [struct((rows, SMALL), F32)],
-    )(payload, out_rows)
+        out_shape=[struct((rows, width), F32)] * 3 + [struct((rows, SMALL), F32)],
+    )(payload)
 
 
 def nothing_kernel(*refs):
@@ -338,6 +348,7 @@
         in_specs=[block] + [pl.BlockSpec(memory_space=pl.ANY)] * len(deps),
         out_specs=block,
         out_shape=jax.ShapeDtypeStruct(value.shape, value.dtype),
+        compiler_params=pltpu.CompilerParams(vmem_limit_bytes=16 * 2**20),
         cost_estimate=QUICK,
     )(value, *deps)
 
@@ -486,11 +497,13 @@
 
 
 def undp_steps(here, there, result):
-    moving = [swap(piece, "dp", 1) for piece in there]
+    moving = {s: swap(there[s], "dp", 1) for s in (3, 2)}
     (x3,) = yield [moving[3]]
     sum3 = here[3].astype(F32) + x3.astype(F32)
+    moving[1] = swap(there[1], "dp", 1)
     x2, three = yield [moving[2], lax.ppermute(sum3.astype(BF16), "expert", INWARD)]
     second = (here[2].astype(F32) + x2.astype(F32) + three.astype(F32)).astype(BF16)
+    moving[0] = swap(there[0], "dp", 1)
     x1, over, inward = yield [
         moving[1],
         lax.ppermute(second, "expert", MIDDLE),
@@ -557,7 +570,11 @@
 def early_gather_steps(own, groups):
     place = lax.axis_index("expert")
     middle = (place == 1) | (place == 2)
-    pair, third_mid = yield [swap(own, "expert", 1), lax.ppermute(own, "expert", MIDDLE)]
+    pair, third_mid, own = yield [
+        swap(own, "expert", 1),
+        lax.ppermute(own, "expert", MIDDLE),
+        own,
+    ]
     (y0,) = yield [swap(own, "ctx", 2)]
     (y1,) = yield [swap(pair, "ctx", 2)]
     second_mid, second_end = yield [
@@ -581,8 +598,8 @@
     (far,) = yield [swap(groups[3], "ctx", 1)]
     over_y = (groups[2].astype(F32) + far.astype(F32)).astype(BF16)
 
-    def across(*slots):
-        return [swap(slot(over_y, s), "ctx", 2) for s in slots]
+    def across(s, count=1):
+        return [swap(over_y[..., s : s + count, :, :], "ctx", 2)]
 
     def total(s, moved):
         return slot(groups[0], s).astype(F32) + slot(near, s).astype(F32) + moved.astype(F32)
@@ -591,15 +608,18 @@
         return lax.ppermute(sum3.astype(BF16), "expert", INWARD)
 
     if slow:
-        (y3,) = yield across(3)
-        (y2,) = yield across(2)
-        y1, near = yield across(1) + [swap(groups[1], "ctx", 1)]
+        y3, near = yield across(3) + [swap(groups[1], "ctx", 1)]
+        y3 = slot(y3, 0)
         sum3 = total(3, y3)
-        (three,) = yield [inwards(sum3)]
+        y2, three = yield across(2) + [inwards(sum3)]
+        y2 = slot(y2, 0)
+        (y1,) = yield across(1)
+        y1 = slot(y1, 0)
         moving = across(0)
     else:
-        y3, y2 = yield across(3, 2)
-        y1, y0, near = yield across(1, 0) + [swap(groups[1], "ctx", 1)]
+        (far_pair,) = yield across(2, 2)
+        near_pair, near = yield across(0, 2) + [swap(groups[1], "ctx", 1)]
+        y3, y2, y1, y0 = slot(far_pair, 1), slot(far_pair, 0), slot(near_pair, 1), slot(near_pair, 0)
         sum3 = total(3, y3)
         (three,) = yield [inwards(sum3)]
         moving = []
@@ -608,7 +628,7 @@
         lax.ppermute(second, "expert", MIDDLE),
         lax.ppermute(second, "expert", INWARD),
     ] + moving
-    y0 = rest[0] if rest else y0
+    y0 = slot(rest[0], 0) if rest else y0
     first = (total(1, y1) + over.astype(F32)).astype(BF16)
     third = (sum3 + inward.astype(F32)).astype(BF16)
     home, pair = yield [lax.ppermute(third, "expert", MIDDLE), swap(first, "expert", 1)]
@@ -665,6 +685,11 @@
     first = lax.axis_index("dp") ^ dx if whole.shape[0] > 1 else 0
     start = (first, 0, lax.axis_index("expert") ^ s) + (0,) * (whole.ndim - 3)
     return lax.dynamic_slice(whole, start, (1, whole.shape[1], 1) + whole.shape[3:])[0, :, 0]
+
+
+def join_rows(own, moved):
+    first = lax.axis_index("dp") == 0
+    return jnp.concatenate([jnp.where(first, own, moved), jnp.where(first, moved, own)])
 
 
 def sum_rows(whole):
@@ -744,7 +769,9 @@
     slots, slots_dp, blocks = [], [] if two else None, []
     heads_here = whole_heads(rows, share)
     upstream_groups = [None] * 4
-    upstream_flow = Flow(early_gather_steps(cotangent[:, 0], upstream_groups))
+    upstream_flow = Flow(early_gather_steps(
+            copy_after(cotangent.reshape(-1, width)).reshape(-1, tokens, width), upstream_groups
+        ))
     payload = pack_weights(
         query_weight, key_weight, value_weight, attention_gain, mixture_gain, query_key_gain, router
     )
@@ -761,7 +788,10 @@
     token = turn([spread, stream_flow, upstream_flow], token)
     copies = [copy_after(own[0], token) for own in (expert_gate, expert_up, expert_down)]
     token = turn([spread, upstream_flow], token, *copies)
-    experts = [lax.all_gather(own, "dp", axis=0, tiled=True) for own in copies]
+    up_moved = [swap(copies[1], "dp", 1)] if two else []
+    experts = [
+        lax.all_gather(own, "dp", axis=0, tiled=True) for own in copies[: 1 if two else 3]
+    ]
     shape = (dp_size, 4, 4) + payload.shape[1:]
     if two:
         packed = assemble([slots, slots_dp], shape)
@@ -816,7 +846,7 @@
     flow_a = Flow(scatter_ctx_steps(out_terms_of(0), sum_a))
     token = turn([flow_a], experts[0])
     done = attention(1, token, [])
-    token = turn([flow_a, upstream_flow], done)
+    token = turn([flow_a], done)
     flow_b = Flow(scatter_ctx_steps(out_terms_of(1), sum_b))
 
     normed_two, unit_two, scale_two, gates_own, residuals = [], [], [], [], []
@@ -839,9 +869,14 @@
 
     groups = [[None] * 4 for _ in micros]
     gather_a = Flow(gather_steps(route(0, sum_a[0]), groups[0], (3, 3, 3, 3)))
-    token = turn([flow_b, gather_a], experts[1])
-    token = turn([gather_a, upstream_flow])
-    token = turn([gather_a, upstream_flow, flow_b], experts[2])
+    token, up_moved = turn([flow_b, gather_a, upstream_flow], values=up_moved + [token])
+    if two:
+        last_moved = [swap(meet([copies[2]], token)[0], "dp", 1)]
+        experts.append(join_rows(expert_up[0], up_moved[0]))
+    token = turn([gather_a])
+    token = turn([gather_a, upstream_flow, flow_b], experts[0], experts[1])
+    if two:
+        experts.append(join_rows(expert_down[0], last_moved[0]))
     second_payload = route(1, sum_b[0])
     gather_b = Flow(gather_steps(second_payload, groups[1], (1, 1, 2, 3)))
 
@@ -860,7 +895,7 @@
         shared[k], back[m][k], kept = met[0], met[1], met[2:]
         return token
 
-    token = expert(0, 0, token, [gather_a, gather_b])
+    token = expert(0, 0, token, [gather_a, upstream_flow, gather_b])
     token = expert(0, 1, token, [gather_a, gather_b])
     token = expert(0, 2, token, [gather_a, gather_b])
     token = expert(0, 3, token, [gather_b])
@@ -924,8 +959,19 @@
     normed_one_grads.append(dot_t(joined_grads[0], projections))
     token = turn([branch_b], normed_one_grads[0])
     token = turn([branch_b])
+    out_last_sum = []
+    out_last = Flow(idle())
     done = attention_back(1, token)
-    token = turn([out_flow], done, gate_sum)
+    if heads_here:
+        split = sum(dot_l(left, right) for left, right in zip(attended_list, branch_list))
+        split = split.astype(BF16).reshape(2, 1, 4, rows, width)
+        out_last = Flow(
+            unline_steps(
+                [jnp.concatenate([piece_of(split, dx, s) for dx in range(2)]) for s in range(4)],
+                out_last_sum,
+            )
+        )
+    token = turn([out_flow, out_last], done, gate_sum)
     normed_one_grads.append(dot_t(joined_grads[1], projections))
     attention_gain_grad = sum(
         jnp.sum(grad * unit, axis=0) for grad, unit in zip(normed_one_grads, units)
@@ -944,43 +990,49 @@
         [grad.astype(BF16).reshape(4, tokens, width) for grad in normed_one_grads], axis=1
     )
 
-    others = [attended_list[0], branch_list[0], attended_list[1], branch_list[1]] if heads_here else []
-
-    def gradient_rows(part, parts, token):
+    def gradient_rows(part, parts, deps):
         product = pair_product_call(
-            part, parts, normed_one, joined_grads, small_columns.astype(BF16), others, [token]
+            part, parts, normed_one, joined_grads, small_columns.astype(BF16), [], deps
         )
         return product.reshape(dp_size // parts, 4, 4, rows, -1)
 
     packed_sum, back_sum = [], []
     if two:
         d = lax.axis_index("dp").astype(jnp.int32)
-        there = gradient_rows(1 - d, 2, token)
+        there = gradient_rows(1 - d, 2, [token])
+        there = [piece_of(there, 0, s) for s in range(4)]
         here = gradient_rows(d, 2, there)
-        token, (here,) = turn([out_flow], values=[here])
+        token, (here,) = turn([out_flow, out_last], values=[here])
         last = Flow(
-            undp_steps(*[[piece_of(part, 0, s) for s in range(4)] for part in (here, there)], packed_sum)
+            undp_steps([piece_of(here, 0, s) for s in range(4)], there, packed_sum)
         )
     else:
-        whole = gradient_rows(jnp.zeros((), jnp.int32), 1, token)
+        whole = gradient_rows(jnp.zeros((), jnp.int32), 1, [token])
         whole = lax.psum_scatter(whole, "dp", scatter_dimension=0, tiled=True)
-        token = turn([out_flow])
+        token = turn([out_flow, out_last])
         last = Flow(unline_steps([piece_of(whole, 0, s) for s in range(4)], packed_sum))
+    token = turn([last, out_last])
     back_flow = Flow(scatter_ctx_steps(terms, back_sum))
-    token = turn([last, back_flow, out_flow])
-    token = turn([last, back_flow], up_sum)
+    token = turn([last, back_flow, out_last], up_sum)
+    if heads_here:
+        own_sum, other_sum = out_last_sum[0]
+        out_moved = [swap(other_sum.astype(BF16), "dp", 1)]
+    else:
+        out_moved = []
     token, (gate_sum, up_sum, down_sum) = turn(
-        [last], token, values=[value.astype(F32) for value in (gate_sum, up_sum, down_sum)]
+        [last, back_flow], token, values=[value.astype(F32) for value in (gate_sum, up_sum, down_sum)]
     )
     if two:
-        token = turn([last])
+        token, out_moved = turn([last, back_flow], values=out_moved + [token])
+    else:
+        token = turn([back_flow], token)
     summed = packed_sum[0]
     columns = 3 * per_ctx + SMALL
     swapped = lax.all_to_all(
         summed[..., :columns].astype(BF16), "ctx", split_axis=0, concat_axis=0, tiled=True
     )
     if heads_here:
-        out_rows_sum = summed[..., columns:]
+        out_rows_sum = own_sum + out_moved[0].astype(F32)
     else:
         out_grad_rows = sum(
             dot_l(left, right) for left, right in zip(attended_list, branch_list)
@@ -992,8 +1044,7 @@
         out_rows_sum = lax.psum_scatter(
             spread_rows.reshape(-1, width), ("dp", "ctx", "expert"), scatter_dimension=0, tiled=True
         ).astype(F32)
-        out_rows_sum = out_rows_sum.reshape(rows, 4, width // 4).transpose(1, 0, 2)
-    *gradients, small_sums = unpack_call(swapped, out_rows_sum)
+    *gradients, small_sums = unpack_call(swapped)
     outputs = [(residuals[m] + out_sum[0][m]).astype(BF16) for m in micros]
     input_grads = []
     for m in micros:
@@ -1008,7 +1059,7 @@
         gradients[0],
         gradients[1],
         gradients[2],
-        gradients[3],
+        out_rows_sum,
         small_sums[:, 0],
         small_sums[:, 1],
         small_sums[:few, 2],

time: 1040 us -> 994 us (0.956)
  waiting for transfers between devices: 293 us -> 216 us
  starting transfers between devices: 141 us -> 172 us
  Pallas kernels: 294 us -> 267 us
  other arithmetic: 145 us -> 159 us
  local copies, waits for them, and re-layouts: 88 us -> 100 us
    ppermute x64, waiting for transfers between devices: 207 us -> 155 us  [swap(): lax.ppermute(value, axis, [(i, i ^ bit) for i in range(lax.axis_size(axis...]
    all_gather x3 -> x1, waiting for transfers between devices: 33.3 us -> 0.01 us  [body(): lax.all_gather(own, 'dp', axis=0, tiled=True)]
    ppermute x0 -> x4, waiting for transfers between devices: none -> 16.3 us  [the longest x1 9.22 us: unline_steps(): three, = (yield [lax.ppermute(slots[3], 'expert', INWARD)])]
    pallas_call x8, Pallas kernels: 173 us -> 159 us  [expert_call(): pl.pallas_call(functools.partial(expert_kernel, capacity, tile_f, tile_d,...]
    unnamed x415 -> x451, local copies, waits for them, and re-layouts: 44.4 us -> 56.4 us
    ppermute x64, starting transfers between devices: 64.2 us -> 75.4 us  [swap(): lax.ppermute(value, axis, [(i, i ^ bit) for i in range(lax.axis_size(axis...]
  transfers between devices with their start and end apart: 104 -> 106, of which waited for: 28 -> 27; matrix products, arithmetic and copies ran while one was open for 21% -> 24% of each run, Pallas kernels for 28% -> 27%
where the time goes in v2:
time: 994 us; the launch traced here: 983 us
  Pallas kernels  267 us (27%)
  waiting for transfers between devices  216 us (22%)
  starting transfers between devices  172 us (17%)
  other arithmetic  159 us (16%)
  local copies, waits for them, and re-layouts  100 us (10%)
  matrix products  51.7 us (5%)
  between operations  17.4 us (2%)
    pallas_call x8, Pallas kernels, expert_call(): pl.pallas_call(functools.partial(expert_kernel, capacity, tile_f, tile_d,...  159 us
    ppermute x64, waiting for transfers between devices, swap(): lax.ppermute(value, axis, [(i, i ^ bit) for i in range(lax.axis_size(axis...  155 us
    ppermute x64, starting transfers between devices, swap(): lax.ppermute(value, axis, [(i, i ^ bit) for i in range(lax.axis_size(axis...  75.4 us
    unnamed x451, local copies, waits for them, and re-layouts  56.4 us
    pallas_call x3, Pallas kernels, product_call(): pl.pallas_call(product_kernel, grid=(columns // wide, rows // tile), in_s...  49.3 us
    dot_general x6, matrix products, dot_t(): lax.dot_general(a, b, (((1,), (1,)), ((), ())), preferred_element_type=F32)  28.1 us
    ppermute x3, starting transfers between devices, scatter_steps(): lax.ppermute(second, 'expert', INWARD)  25 us
    pallas_call x2, Pallas kernels, attention_backward_call(): pl.pallas_call(functools.partial(backward_kernel, dh), grid=(heads,), in_...  22.5 us
  transfers between devices with their start and end apart: 106, of which 27 were waited for; matrix products, arithmetic and copies ran while one was open for 24% of the time, Pallas kernels for 27%

profile of v2, /device:TPU:0, one launch (start us, length us, event | category | flops | bytes accessed | tf_op | source)
XLA Modules:
  0.0 983.1 jit_solution(6116856396685446611)
XLA Ops:
  24.5 11.6 %all-to-all-done = bf16[4,64,1664]{2,1,0:T(8,128)(2,1)S(1)} async-done(((bf16[4,64,1664]{2,1,0:T(8,128)(2,1)}), bf16[4,64,1664]{2,1,0:T(8,128)(2,1)S(1)}, u32[]{:S(2)}, u32[]{:S(2)}) %all-to-all-start) | async-done | bytes 852000 | tf_op jit(solution)/shard_map/all_to_all | solution.py:778
  47.7 18.7 %collective-permute-done.refs_0_ = bf16[4,64,2176]{2,1,0:T(8,128)(2,1)} collective-permute-done((bf16[4,64,2176]{2,1,0:T(8,128)(2,1)S(1)}, bf16[4,64,2176]{2,1,0:T(8,128)(2,1)}, u32[]{:S(2)}, u32[]{:S(2)}) %collective-permute-start) | collective-permute-done | bytes 1114144 | tf_op jit(solution)/shard_map/ppermute | solution.py:435
  81.8 14.9 %collective-permute-done.10.refs_5_ = bf16[2,128,2048]{2,1,0:T(8,128)(2,1)S(1)} collective-permute-done((bf16[2,128,2048]{2,1,0:T(8,128)(2,1)}, bf16[2,128,2048]{2,1,0:T(8,128)(2,1)S(1)}, u32[]{:S(2)}, u32[]{:S(2)}) %collective-permute-start.10) | collective-permute-done | bytes 1048608 | tf_op jit(solution)/shard_map/ppermute | solution.py:435
  114.2 14.9 %collective-permute-done.14.refs_3_ = bf16[2,128,2048]{2,1,0:T(8,128)(2,1)S(1)} collective-permute-done((bf16[2,128,2048]{2,1,0:T(8,128)(2,1)}, bf16[2,128,2048]{2,1,0:T(8,128)(2,1)S(1)}, u32[]{:S(2)}, u32[]{:S(2)}) %collective-permute-start.14) | collective-permute-done | bytes 1048608 | tf_op jit(solution)/shard_map/ppermute | solution.py:435
  155.4 16.3 %collective-permute-done.15.refs_0_ = bf16[4,64,2176]{2,1,0:T(8,128)(2,1)S(1)} collective-permute-done((bf16[4,64,2176]{2,1,0:T(8,128)(2,1)}, bf16[4,64,2176]{2,1,0:T(8,128)(2,1)S(1)}, u32[]{:S(2)}, u32[]{:S(2)}) %collective-permute-start.15) | collective-permute-done | bytes 1114144 | tf_op jit(solution)/shard_map/ppermute | solution.py:435
  181.5 6.3 fusion.16.joined_ref
  187.9 8.5 shard_map.264
  214.3 6.3 fusion.14.joined_ref
  220.6 8.5 shard_map.266.refs_1_
  232.2 13.5 %collective-permute-done.19.refs_0_ = bf16[128,2048]{1,0:T(8,128)(2,1)S(1)} collective-permute-done((bf16[128,2048]{1,0:T(8,128)(2,1)S(1)}, bf16[128,2048]{1,0:T(8,128)(2,1)S(1)}, u32[]{:S(2)}, u32[]{:S(2)}) %collective-permute-start.19) | collective-permute-done | bytes 524320 | tf_op jit(solution)/shard_map/ppermute | solution.py:435
  253.5 7.4 collective-permute-start.21
  262.4 10.5 %collective-permute-done.21.refs_1_ = bf16[144,2048]{1,0:T(8,128)(2,1)} collective-permute-done((bf16[144,2048]{1,0:T(8,128)(2,1)S(1)}, bf16[144,2048]{1,0:T(8,128)(2,1)}, u32[]{:S(2)}, u32[]{:S(2)}) %collective-permute-start.21) | collective-permute-done | bytes 589856 | tf_op jit(solution)/shard_map/ppermute | solution.py:435
  291.0 9.1 collective-permute-done.27.refs_1_
  307.2 13.8 %collective-permute-done.31.refs_3_ = bf16[128,2048]{1,0:T(8,128)(2,1)} collective-permute-done((bf16[128,2048]{1,0:T(8,128)(2,1)}, bf16[128,2048]{1,0:T(8,128)(2,1)}, u32[]{:S(2)}, u32[]{:S(2)}) %collective-permute-start.31) | collective-permute-done | bytes 524320 | tf_op jit(solution)/shard_map/ppermute | solution.py:435
  336.5 5.9 collective-permute-start.34
  348.1 19.9 %shard_map.272 = (bf16[2,4,128,2048]{3,2,1,0:T(8,128)(2,1)}, bf16[4,144,2048]{2,1,0:T(8,128)(2,1)}, bf16[2560,2048]{1,0:T(8,128)(2,1)}, bf16[2560,2048]{1,0:T(8,...) custom-call(s32[2]{0:T(128)} %pad_add_fusion.1.order_ref, ...), custom_call_target="tpu_custom_call" | custom-call | flops 1000 | bytes 1000 | tf_op jit(solution)/shard_map/pallas_call | solution.py:163
  373.0 19.8 %shard_map.274 = (bf16[2,4,128,2048]{3,2,1,0:T(8,128)(2,1)}, bf16[4,144,2048]{2,1,0:T(8,128)(2,1)}, bf16[2560,2048]{1,0:T(8,128)(2,1)}, bf16[2560,2048]{1,0:T(8,...) custom-call(s32[2]{0:T(128)} %pad_add_fusion.1.order_ref, ...), custom_call_target="tpu_custom_call", output_to_operand_aliasing={{2}: (7, {}), {3}: (8, {}), {4}: (9, {}), {5}: (10, {}), {6... | custom-call | flops 1000 | bytes 1000 | tf_op jit(solution)/shard_map/pallas_call | solution.py:163
  395.8 11.7 %collective-permute-done.41.refs_4_ = bf16[144,2048]{1,0:T(8,128)(2,1)S(1)} collective-permute-done((bf16[144,2048]{1,0:T(8,128)(2,1)}, bf16[144,2048]{1,0:T(8,128)(2,1)S(1)}, u32[]{:S(2)}, u32[]{:S(2)}) %collective-permute-start.41) | collective-permute-done | bytes 589856 | tf_op jit(solution)/shard_map/ppermute | solution.py:435
  412.5 19.9 %shard_map.276 = (bf16[2,4,128,2048]{3,2,1,0:T(8,128)(2,1)}, bf16[4,144,2048]{2,1,0:T(8,128)(2,1)}, bf16[2560,2048]{1,0:T(8,128)(2,1)}, bf16[2560,2048]{1,0:T(8,...) custom-call(s32[2]{0:T(128)} %pad_add_fusion.1.order_ref, ...), custom_call_target="tpu_custom_call", output_to_operand_aliasing={{2}: (7, {}), {3}: (8, {}), {4}: (9, {}), {5}: (10, {}), {6... | custom-call | flops 1000 | bytes 1000 | tf_op jit(solution)/shard_map/pallas_call | solution.py:163
  439.4 20.0 %shard_map.278 = (bf16[2,4,128,2048]{3,2,1,0:T(8,128)(2,1)}, bf16[4,144,2048]{2,1,0:T(8,128)(2,1)}, bf16[2560,2048]{1,0:T(8,128)(2,1)}, bf16[2560,2048]{1,0:T(8,...) custom-call(s32[2]{0:T(128)} %pad_add_fusion.1.order_ref, ...), custom_call_target="tpu_custom_call", output_to_operand_aliasing={{2}: (7, {}), {3}: (8, {}), {4}: (9, {}), {5}: (10, {}), {6... | custom-call | flops 1000 | bytes 1000 | tf_op jit(solution)/shard_map/pallas_call | solution.py:163
  465.3 20.0 %shard_map.280 = (bf16[2,4,128,2048]{3,2,1,0:T(8,128)(2,1)}, bf16[4,144,2048]{2,1,0:T(8,128)(2,1)}, bf16[2560,2048]{1,0:T(8,128)(2,1)}, bf16[2560,2048]{1,0:T(8,...) custom-call(s32[2]{0:T(128)} %pad_add_fusion.1.order_ref, ...), custom_call_target="tpu_custom_call", output_to_operand_aliasing={{0}: (7, {}), {2}: (8, {}), {3}: (9, {}), {4}: (10, {}), {5... | custom-call | flops 1000 | bytes 1000 | tf_op jit(solution)/shard_map/pallas_call | solution.py:163
  492.8 19.8 %shard_map.282 = (bf16[2,4,128,2048]{3,2,1,0:T(8,128)(2,1)}, bf16[4,144,2048]{2,1,0:T(8,128)(2,1)}, bf16[2560,2048]{1,0:T(8,128)(2,1)}, bf16[2560,2048]{1,0:T(8,...) custom-call(s32[2]{0:T(128)} %pad_add_fusion.1.order_ref, ...), custom_call_target="tpu_custom_call", output_to_operand_aliasing={{0}: (7, {}), {2}: (8, {}), {3}: (9, {}), {4}: (10, {}), {5... | custom-call | flops 1000 | bytes 1000 | tf_op jit(solution)/shard_map/pallas_call | solution.py:163
  512.6 6.8 collective-permute-done.51.refs_0_
  521.9 20.1 %shard_map.284 = (bf16[2,4,128,2048]{3,2,1,0:T(8,128)(2,1)}, bf16[4,144,2048]{2,1,0:T(8,128)(2,1)}, bf16[2560,2048]{1,0:T(8,128)(2,1)}, bf16[2560,2048]{1,0:T(8,...) custom-call(s32[2]{0:T(128)} %pad_add_fusion.1.order_ref, ...), custom_call_target="tpu_custom_call", output_to_operand_aliasing={{0}: (7, {}), {2}: (8, {}), {3}: (9, {}), {4}: (10, {}), {5... | custom-call | flops 1000 | bytes 1000 | tf_op jit(solution)/shard_map/pallas_call | solution.py:163
  542.0 7.0 collective-permute-done.49.refs_0_
  557.5 7.9 collective-permute-start.53
  566.3 19.9 %shard_map.286 = (bf16[2,4,128,2048]{3,2,1,0:T(8,128)(2,1)}, bf16[4,144,2048]{2,1,0:T(8,128)(2,1)}, bf16[2560,2048]{1,0:T(8,128)(2,1)}, bf16[2560,2048]{1,0:T(8,...) custom-call(s32[2]{0:T(128)} %pad_add_fusion.1.order_ref, ...), custom_call_target="tpu_custom_call", output_to_operand_aliasing={{0}: (7, {}), {2}: (8, {}), {3}: (9, {}), {4}: (10, {}), {5... | custom-call | flops 1000 | bytes 1000 | tf_op jit(solution)/shard_map/pallas_call | solution.py:163
  590.0 7.9 collective-permute-start.56
  597.9 17.1 %shard_map.288.refs_5_ = bf16[1024,2048]{1,0:T(8,128)(2,1)} custom-call(bf16[2560,1024]{1,0:T(8,128)(2,1)} %get-tuple-element.392.left_ref, bf16[2560,2048]{1,0:T(8,128)(2,1)} %get-tuple-element.393.right_ref, bf16[144,2048]{1,0:T(8,128)(2,1)} %get-tuple-element.389.refs_0_), custom_call_target="tpu_custom_call" | custom-call | flops 1000 | bytes 1000 | tf_op jit(solution)/shard_map/pallas_call | solution.py:210
  616.2 5.4 add_convert_fusion
  632.8 16.2 %shard_map.290.refs_5_ = bf16[2048,1024]{1,0:T(8,128)(2,1)} custom-call(bf16[2560,2048]{1,0:T(8,128)(2,1)} %get-tuple-element.402.left_ref, bf16[2560,1024]{1,0:T(8,128)(2,1)} %get-tuple-element.403.right_ref, bf16[144,2048]{1,0:T(8,128)(2,1)} %get-tuple-element.395.refs_0_), custom_call_target="tpu_custom_call" | custom-call | flops 1000 | bytes 1000 | tf_op jit(solution)/shard_map/pallas_call | solution.py:210
  660.6 7.3 collective-permute-start.68
  679.9 16.1 %shard_map.292.refs_6_ = bf16[2048,1024]{1,0:T(8,128)(2,1)} custom-call(bf16[2560,2048]{1,0:T(8,128)(2,1)} %get-tuple-element.402.left_ref, bf16[2560,1024]{1,0:T(8,128)(2,1)} %get-tuple-element.409.right_ref, bf16[144,2048]{1,0:T(8,128)(2,1)} %get-tuple-element.406.refs_0_), custom_call_target="tpu_custom_call" | custom-call | flops 1000 | bytes 1000 | tf_op jit(solution)/shard_map/pallas_call | solution.py:210
  723.0 11.2 %shard_map.295 = (bf16[512,1536]{1,0:T(8,128)(2,1)S(1)}, f32[2,128]{1,0:T(2,128)S(1)}) custom-call(f32[512,1536]{1,0:T(8,128)S(1)} %copy-done.9, bf16[512,512]{1,0:T(8,128)(2,1)S(1)} %copy-done.48, f32[512,128]{1,0:T(8,128)S(1)} %copy-done.37, f32[512,128]{1,0:T(8,128)S(1)} %pad_maximum_fusion.21.sin_ref, f32[2,128]{1,0:T(2,128)S(1)} %reshape.727.gain_ref, ...), custom_call_target="tpu_custom_call" | custom-call | flops 1000 | bytes 1000 | tf_op jit(solution)/shard_map/pallas_call | solution.py:425
  742.5 7.9 fusion.12.refs_2_
  750.4 5.2 collective-permute-done.78.refs_0_
  761.9 9.8 collective-permute-start.72
  776.3 11.2 %shard_map.299 = (bf16[512,1536]{1,0:T(8,128)(2,1)S(1)}, f32[2,128]{1,0:T(2,128)S(1)}) custom-call(f32[512,1536]{1,0:T(8,128)S(1)} %copy-done.7, bf16[512,512]{1,0:T(8,128)(2,1)S(1)} %convolution_convert_fusion.2.do_ref, f32[512,128]{1,0:T(8,128)S(1)} %copy-done.39, f32[512,128]{1,0:T(8,128)S(1)} %copy-done.31, f32[2,128]{1,0:T(2,128)S(1)} %reshape.727.gain_ref, ...), custom_call_target="tpu_custom_call" | custom-call | flops 1000 | bytes 1000 | tf_op jit(solution)/shard_map/pallas_call | solution.py:425
  793.4 8.8 fusion.5
  808.7 9.2 collective-permute-done.81.refs_3_
  818.7 5.5 fusion.20
  829.8 5.1 collective-permute-start.85
  838.0 6.1 shard_map.301
  847.5 6.6 shard_map.302
  854.8 7.0 collective-permute-done.85.refs_3_
  881.7 11.0 %collective-permute-start.90 = (bf16[4,64,1664]{2,1,0:T(8,128)(2,1)}, bf16[4,64,1664]{2,1,0:T(8,128)(2,1)}, u32[]{:S(2)}, u32[]{:S(2)}) collective-permute-start(bf16[4,64,1664]{2,1,0:T(8,128)(2,1)} %fusion.31), channel_id=1, source_target_pairs={{0,1},{3,2},{4,5},{7,6},{8,9},{11,10},{12,13},{15,14},{16,17},{19,... | collective-permute-start | bytes 2555912 | tf_op jit(solution)/shard_map/ppermute | solution.py:504
  920.9 7.8 collective-permute-done.94.refs_2_
  958.0 10.4 %all-to-all-done.1.payload_ref = bf16[4,64,1664]{2,1,0:T(8,128)(2,1)S(1)} async-done(((bf16[4,64,1664]{2,1,0:T(8,128)(2,1)}), bf16[4,64,1664]{2,1,0:T(8,128)(2,1)S(1)}, u32[]{:S(2)}, u32[]{:S(2)}) %all-to-all-start.1) | async-done | bytes 852000 | tf_op jit(solution)/shard_map/all_to_all | solution.py:1031
  (861 shorter events, 414.0 us)
Async XLA Ops:
  8.5 37.5 %collective-permute-start.3 = (bf16[2,128,2048]{2,1,0:T(8,128)(2,1)S(1)}, bf16[2,128,2048]{2,1,0:T(8,128)(2,1)}, u32[]{:S(2)}, u32[]{:S(2)}) collective-permute-start(bf16[2,128,2048]{2,1,0:T(8,128)(2,1)S(1)} %bitcast.482), channel_id=1, source_target_pairs={{0,1},{1,0},{2,3},{3,2},{4,5},{5,4},{6,7},{7,6},{8,9},{9,8},{10,11... | collective-permute-start | bytes 3145736 | tf_op jit(solution)/shard_map/ppermute | solution.py:435
  11.6 36.1 %collective-permute-start.4 = (bf16[2,128,2048]{2,1,0:T(8,128)(2,1)S(1)}, bf16[2,128,2048]{2,1,0:T(8,128)(2,1)}, u32[]{:S(2)}, u32[]{:S(2)}) collective-permute-start(bf16[2,128,2048]{2,1,0:T(8,128)(2,1)S(1)} %bitcast.483), channel_id=1, source_target_pairs={{1,2},{2,1},{5,6},{6,5},{9,10},{10,9},{13,14},{14,13},{17,18},{18,... | collective-permute-start | bytes 3145736 | tf_op jit(solution)/shard_map/ppermute | solution.py:575
  23.8 187.2 %all-gather.2.cloned.1.call-start = ((), (), s32[]{:S(2)}) async-start(), calls=%async_computation.5 | async-start | bytes 6291456 | tf_op jit(solution)/shard_map/all_gather | solution.py:793
  47.7 34.2 %collective-permute-start.9 = (bf16[2,128,2048]{2,1,0:T(8,128)(2,1)}, bf16[2,128,2048]{2,1,0:T(8,128)(2,1)}, u32[]{:S(2)}, u32[]{:S(2)}) collective-permute-start(bf16[2,128,2048]{2,1,0:T(8,128)(2,1)} %bitcast.7), channel_id=1, source_target_pairs={{0,4},{4,0},{8,12},{12,8},{1,5},{5,1},{9,13},{13,9},{2,6},{6,2},{1... | collective-permute-start | bytes 3145736 | tf_op jit(solution)/shard_map/ppermute | solution.py:435
  99.6 31.7 %collective-permute-start.11 = (bf16[4,64,2176]{2,1,0:T(8,128)(2,1)}, bf16[4,64,2176]{2,1,0:T(8,128)(2,1)S(1)}, u32[]{:S(2)}, u32[]{:S(2)}) collective-permute-start(bf16[4,64,2176]{2,1,0:T(8,128)(2,1)} %get-tuple-element.241.refs_4_), channel_id=1, source_target_pairs={{1,0},{2,3},{5,4},{6,7},{9,8},{10,11},{13,12},{14,15},{17,16},{18,... | collective-permute-start | bytes 3342344 | tf_op jit(solution)/shard_map/ppermute | solution.py:476
  112.5 42.9 %collective-permute-start.16 = (bf16[2,128,2048]{2,1,0:T(8,128)(2,1)}, bf16[2,128,2048]{2,1,0:T(8,128)(2,1)}, u32[]{:S(2)}, u32[]{:S(2)}) collective-permute-start(bf16[2,128,2048]{2,1,0:T(8,128)(2,1)} %get-tuple-element.243), channel_id=1, source_target_pairs={{1,2},{2,1},{5,6},{6,5},{9,10},{10,9},{13,14},{14,13},{17,18},{18,... | collective-permute-start | bytes 3145736 | tf_op jit(solution)/shard_map/ppermute | solution.py:581
  136.5 35.2 %collective-permute-start.15 = (bf16[4,64,2176]{2,1,0:T(8,128)(2,1)}, bf16[4,64,2176]{2,1,0:T(8,128)(2,1)S(1)}, u32[]{:S(2)}, u32[]{:S(2)}) collective-permute-start(bf16[4,64,2176]{2,1,0:T(8,128)(2,1)} %get-tuple-element.548), channel_id=1, source_target_pairs={{0,16},{16,0},{1,17},{17,1},{2,18},{18,2},{3,19},{19,3},{4,20},{20... | collective-permute-start | bytes 3342344 | tf_op jit(solution)/shard_map/ppermute | solution.py:435
  139.6 596.0 %reduce-scatter.4.cloned.1.call-start = ((), (), s32[]{:S(2)}) async-start(), calls=%async_computation.6 | async-start | bytes 6291456 | tf_op jit(solution)/shard_map/reduce_scatter | solution.py:696
  203.5 57.4 %collective-permute-start.25 = (bf16[1024,1024]{1,0:T(8,128)(2,1)}, bf16[1024,1024]{1,0:T(8,128)(2,1)}, u32[]{:S(2)}, u32[]{:S(2)}) collective-permute-start(bf16[1024,1024]{1,0:T(8,128)(2,1)} %shard_map.261.refs_5_), channel_id=1, source_target_pairs={{0,16},{16,0},{1,17},{17,1},{2,18},{18,2},{3,19},{19,3},{4,20},{20... | collective-permute-start | bytes 6291464 | tf_op jit(solution)/shard_map/ppermute | solution.py:435
  206.0 56.4 %collective-permute-start.23 = (bf16[2,128,2048]{2,1,0:T(8,128)(2,1)}, bf16[2,128,2048]{2,1,0:T(8,128)(2,1)}, u32[]{:S(2)}, u32[]{:S(2)}) collective-permute-start(bf16[2,128,2048]{2,1,0:T(8,128)(2,1)} %get-tuple-element.251), channel_id=1, source_target_pairs={{1,0},{2,3},{5,4},{6,7},{9,8},{10,11},{13,12},{14,15},{17,16},{18,... | collective-permute-start | bytes 3145736 | tf_op jit(solution)/shard_map/ppermute | solution.py:585
  209.9 52.5 %collective-permute-start.24 = (bf16[2,128,2048]{2,1,0:T(8,128)(2,1)}, bf16[2,128,2048]{2,1,0:T(8,128)(2,1)}, u32[]{:S(2)}, u32[]{:S(2)}) collective-permute-start(bf16[2,128,2048]{2,1,0:T(8,128)(2,1)} %broadcast_select_fusion.7), channel_id=1, source_target_pairs={{0,8},{4,12},{8,0},{12,4},{1,9},{5,13},{9,1},{13,5},{2,10},{6,14},... | collective-permute-start | bytes 3145736 | tf_op jit(solution)/shard_map/ppermute | solution.py:435
  213.3 32.4 %collective-permute-start.19 = (bf16[128,2048]{1,0:T(8,128)(2,1)S(1)}, bf16[128,2048]{1,0:T(8,128)(2,1)S(1)}, u32[]{:S(2)}, u32[]{:S(2)}) collective-permute-start(bf16[128,2048]{1,0:T(8,128)(2,1)S(1)} %fusion.65), channel_id=1, source_target_pairs={{0,8},{4,12},{8,0},{12,4},{1,9},{5,13},{9,1},{13,5},{2,10},{6,14},... | collective-permute-start | bytes 1572872 | tf_op jit(solution)/shard_map/ppermute | solution.py:435
  232.2 30.3 %collective-permute-start.20 = (bf16[2,128,2048]{2,1,0:T(8,128)(2,1)}, bf16[2,128,2048]{2,1,0:T(8,128)(2,1)}, u32[]{:S(2)}, u32[]{:S(2)}) collective-permute-start(bf16[2,128,2048]{2,1,0:T(8,128)(2,1)} %bitcast.55), channel_id=1, source_target_pairs={{0,4},{4,0},{8,12},{12,8},{1,5},{5,1},{9,13},{13,9},{2,6},{6,2},{1... | collective-permute-start | bytes 3145736 | tf_op jit(solution)/shard_map/ppermute | solution.py:435
  278.2 42.7 %collective-permute-start.30 = (bf16[4,2,128,2048]{3,2,1,0:T(8,128)(2,1)}, bf16[4,2,128,2048]{3,2,1,0:T(8,128)(2,1)}, u32[]{:S(2)}, u32[]{:S(2)}) collective-permute-start(bf16[4,2,128,2048]{3,2,1,0:T(8,128)(2,1)} %pad_maximum_fusion.1.up_ref), channel_id=1, source_target_pairs={{0,4},{4,0},{8,12},{12,8},{1,5},{5,1},{9,13},{13,9},{2,6},{6,2},{1... | collective-permute-start | bytes 12582920 | tf_op jit(solution)/shard_map/ppermute | solution.py:435
  283.9 37.1 %collective-permute-start.29 = (bf16[2,128,2048]{2,1,0:T(8,128)(2,1)}, bf16[2,128,2048]{2,1,0:T(8,128)(2,1)}, u32[]{:S(2)}, u32[]{:S(2)}) collective-permute-start(bf16[2,128,2048]{2,1,0:T(8,128)(2,1)} %copy-done.110), channel_id=1, source_target_pairs={{0,8},{4,12},{8,0},{12,4},{1,9},{5,13},{9,1},{13,5},{2,10},{6,14},... | collective-permute-start | bytes 3145736 | tf_op jit(solution)/shard_map/ppermute | solution.py:435
  285.2 57.3 %collective-permute-start.36 = (bf16[512,2048]{1,0:T(8,128)(2,1)}, bf16[512,2048]{1,0:T(8,128)(2,1)}, u32[]{:S(2)}, u32[]{:S(2)}) collective-permute-start(bf16[512,2048]{1,0:T(8,128)(2,1)} %shard_map.271), channel_id=1, source_target_pairs={{0,16},{16,0},{1,17},{17,1},{2,18},{18,2},{3,19},{19,3},{4,20},{20... | collective-permute-start | bytes 6291464 | tf_op jit(solution)/shard_map/ppermute | solution.py:435
  290.0 31.0 %collective-permute-start.31 = (bf16[128,2048]{1,0:T(8,128)(2,1)}, bf16[128,2048]{1,0:T(8,128)(2,1)}, u32[]{:S(2)}, u32[]{:S(2)}) collective-permute-start(bf16[128,2048]{1,0:T(8,128)(2,1)} %fusion.64), channel_id=1, source_target_pairs={{0,8},{4,12},{8,0},{12,4},{1,9},{5,13},{9,1},{13,5},{2,10},{6,14},... | collective-permute-start | bytes 1572872 | tf_op jit(solution)/shard_map/ppermute | solution.py:435
  325.4 43.5 %collective-permute-start.33 = (bf16[4,2,128,2048]{3,2,1,0:T(8,128)(2,1)}, bf16[4,2,128,2048]{3,2,1,0:T(8,128)(2,1)}, u32[]{:S(2)}, u32[]{:S(2)}) collective-permute-start(bf16[4,2,128,2048]{3,2,1,0:T(8,128)(2,1)} %pad_maximum_fusion.3.up_ref), channel_id=1, source_target_pairs={{0,4},{4,0},{8,12},{12,8},{1,5},{5,1},{9,13},{13,9},{2,6},{6,2},{1... | collective-permute-start | bytes 12582920 | tf_op jit(solution)/shard_map/ppermute | solution.py:435
  328.3 40.6 %collective-permute-start.32 = (bf16[4,144,2048]{2,1,0:T(8,128)(2,1)}, bf16[4,144,2048]{2,1,0:T(8,128)(2,1)}, u32[]{:S(2)}, u32[]{:S(2)}) collective-permute-start(bf16[4,144,2048]{2,1,0:T(8,128)(2,1)} %pad_maximum_fusion.5.norm_ref), channel_id=1, source_target_pairs={{0,4},{4,0},{8,12},{12,8},{1,5},{5,1},{9,13},{13,9},{2,6},{6,2},{1... | collective-permute-start | bytes 7077896 | tf_op jit(solution)/shard_map/ppermute | solution.py:435
  328.8 67.0 %collective-permute-start.37 = (bf16[4,144,2048]{2,1,0:T(8,128)(2,1)}, bf16[4,144,2048]{2,1,0:T(8,128)(2,1)}, u32[]{:S(2)}, u32[]{:S(2)}) collective-permute-start(bf16[4,144,2048]{2,1,0:T(8,128)(2,1)} %pad_maximum_fusion.5.norm_ref), channel_id=1, source_target_pairs={{0,8},{4,12},{8,0},{12,4},{1,9},{5,13},{9,1},{13,5},{2,10},{6,14},... | collective-permute-start | bytes 7077896 | tf_op jit(solution)/shard_map/ppermute | solution.py:435
  336.5 31.5 %collective-permute-start.34 = (bf16[144,2048]{1,0:T(8,128)(2,1)}, bf16[144,2048]{1,0:T(8,128)(2,1)S(1)}, u32[]{:S(2)}, u32[]{:S(2)}) collective-permute-start(bf16[144,2048]{1,0:T(8,128)(2,1)} %get-tuple-element.593), channel_id=1, source_target_pairs={{0,1},{1,0},{2,3},{3,2},{4,5},{5,4},{6,7},{7,6},{8,9},{9,8},{10,11... | collective-permute-start | bytes 1769480 | tf_op jit(solution)/shard_map/ppermute | solution.py:435
  371.7 35.8 %collective-permute-start.41 = (bf16[144,2048]{1,0:T(8,128)(2,1)}, bf16[144,2048]{1,0:T(8,128)(2,1)S(1)}, u32[]{:S(2)}, u32[]{:S(2)}) collective-permute-start(bf16[144,2048]{1,0:T(8,128)(2,1)} %get-tuple-element.274), channel_id=1, source_target_pairs={{0,8},{4,12},{8,0},{12,4},{1,9},{5,13},{9,1},{13,5},{2,10},{6,14},... | collective-permute-start | bytes 1769480 | tf_op jit(solution)/shard_map/ppermute | solution.py:435
  492.8 49.2 %collective-permute-start.50 = (bf16[4,144,2048]{2,1,0:T(8,128)(2,1)}, bf16[4,144,2048]{2,1,0:T(8,128)(2,1)}, u32[]{:S(2)}, u32[]{:S(2)}) collective-permute-start(bf16[4,144,2048]{2,1,0:T(8,128)(2,1)} %get-tuple-element.341), channel_id=1, source_target_pairs={{0,4},{4,0},{8,12},{12,8},{1,5},{5,1},{9,13},{13,9},{2,6},{6,2},{1... | collective-permute-start | bytes 7077896 | tf_op jit(solution)/shard_map/ppermute | solution.py:435
  520.4 28.6 %collective-permute-start.52 = (bf16[4,144,2048]{2,1,0:T(8,128)(2,1)}, bf16[4,144,2048]{2,1,0:T(8,128)(2,1)}, u32[]{:S(2)}, u32[]{:S(2)}) collective-permute-start(bf16[4,144,2048]{2,1,0:T(8,128)(2,1)} %get-tuple-element.356), channel_id=1, source_target_pairs={{0,4},{4,0},{8,12},{12,8},{1,5},{5,1},{9,13},{13,9},{2,6},{6,2},{1... | collective-permute-start | bytes 7077896 | tf_op jit(solution)/shard_map/ppermute | solution.py:435
  520.4 28.6 %collective-permute-start.49 = (bf16[2,144,2048]{2,1,0:T(8,128)(2,1)}, bf16[2,144,2048]{2,1,0:T(8,128)(2,1)S(1)}, u32[]{:S(2)}, u32[]{:S(2)}) collective-permute-start(bf16[2,144,2048]{2,1,0:T(8,128)(2,1)} %get-tuple-element.577), channel_id=1, source_target_pairs={{0,8},{4,12},{8,0},{12,4},{1,9},{5,13},{9,1},{13,5},{2,10},{6,14},... | collective-permute-start | bytes 3538952 | tf_op jit(solution)/shard_map/ppermute | solution.py:435
  521.6 93.4 %collective-permute-start.59 = (bf16[2,4,128,2048]{3,2,1,0:T(8,128)(2,1)}, bf16[2,4,128,2048]{3,2,1,0:T(8,128)(2,1)}, u32[]{:S(2)}, u32[]{:S(2)}) collective-permute-start(bf16[2,4,128,2048]{3,2,1,0:T(8,128)(2,1)} %get-tuple-element.391), channel_id=1, source_target_pairs={{0,4},{4,0},{8,12},{12,8},{1,5},{5,1},{9,13},{13,9},{2,6},{6,2},{1... | collective-permute-start | bytes 12582920 | tf_op jit(solution)/shard_map/ppermute | solution.py:435
  550.0 65.1 %collective-permute-start.58 = (bf16[4,144,2048]{2,1,0:T(8,128)(2,1)}, bf16[4,144,2048]{2,1,0:T(8,128)(2,1)}, u32[]{:S(2)}, u32[]{:S(2)}) collective-permute-start(bf16[4,144,2048]{2,1,0:T(8,128)(2,1)} %get-tuple-element.390), channel_id=1, source_target_pairs={{0,4},{4,0},{8,12},{12,8},{1,5},{5,1},{9,13},{13,9},{2,6},{6,2},{1... | collective-permute-start | bytes 7077896 | tf_op jit(solution)/shard_map/ppermute | solution.py:435
  554.8 31.5 %collective-permute-start.54 = (bf16[2,144,2048]{2,1,0:T(8,128)(2,1)S(1)}, bf16[2,144,2048]{2,1,0:T(8,128)(2,1)S(1)}, u32[]{:S(2)}, u32[]{:S(2)}) collective-permute-start(bf16[2,144,2048]{2,1,0:T(8,128)(2,1)S(1)} %get-tuple-element.576), channel_id=1, source_target_pairs={{0,8},{4,12},{8,0},{12,4},{1,9},{5,13},{9,1},{13,5},{2,10},{6,14},... | collective-permute-start | bytes 3538952 | tf_op jit(solution)/shard_map/ppermute | solution.py:435
  557.5 28.7 %collective-permute-start.53 = (bf16[144,2048]{1,0:T(8,128)(2,1)S(1)}, bf16[144,2048]{1,0:T(8,128)(2,1)S(1)}, u32[]{:S(2)}, u32[]{:S(2)}) collective-permute-start(bf16[144,2048]{1,0:T(8,128)(2,1)S(1)} %bitcast_convert_fusion.2), channel_id=1, source_target_pairs={{0,1},{3,2},{4,5},{7,6},{8,9},{11,10},{12,13},{15,14},{16,17},{19,... | collective-permute-start | bytes 1769480 | tf_op jit(solution)/shard_map/ppermute | solution.py:608
  565.4 49.5 %collective-permute-start.57 = (bf16[2,144,2048]{2,1,0:T(8,128)(2,1)}, bf16[2,144,2048]{2,1,0:T(8,128)(2,1)}, u32[]{:S(2)}, u32[]{:S(2)}) collective-permute-start(bf16[2,144,2048]{2,1,0:T(8,128)(2,1)} %get-tuple-element.575), channel_id=1, source_target_pairs={{0,8},{4,12},{8,0},{12,4},{1,9},{5,13},{9,1},{13,5},{2,10},{6,14},... | collective-permute-start | bytes 3538952 | tf_op jit(solution)/shard_map/ppermute | solution.py:435
  616.0 201.9 %reduce-scatter.6.cloned.1.call-start = ((), (), s32[]{:S(2)}) async-start(), calls=%async_computation.7 | async-start | bytes 6291456 | tf_op jit(solution)/shard_map/reduce_scatter | solution.py:696
  616.1 37.4 %collective-permute-start.64 = (bf16[2,4,128,2048]{3,2,1,0:T(8,128)(2,1)}, bf16[2,4,128,2048]{3,2,1,0:T(8,128)(2,1)}, u32[]{:S(2)}, u32[]{:S(2)}) collective-permute-start(bf16[2,4,128,2048]{3,2,1,0:T(8,128)(2,1)} %get-tuple-element.401), channel_id=1, source_target_pairs={{0,4},{4,0},{8,12},{12,8},{1,5},{5,1},{9,13},{13,9},{2,6},{6,2},{1... | collective-permute-start | bytes 12582920 | tf_op jit(solution)/shard_map/ppermute | solution.py:435
  623.4 30.1 %collective-permute-start.63 = (bf16[2,1,128,2048]{3,2,1,0:T(8,128)(2,1)S(1)}, bf16[2,1,128,2048]{3,2,1,0:T(8,128)(2,1)S(1)}, u32[]{:S(2)}, u32[]{:S(2)}) collective-permute-start(bf16[2,1,128,2048]{3,2,1,0:T(8,128)(2,1)S(1)} %get-tuple-element.564), channel_id=1, source_target_pairs={{0,8},{4,12},{8,0},{12,4},{1,9},{5,13},{9,1},{13,5},{2,10},{6,14},... | collective-permute-start | bytes 3145736 | tf_op jit(solution)/shard_map/ppermute | solution.py:435
  654.7 245.1 %reduce-scatter.8.cloned.1.call-start = ((), (), s32[]{:S(2)}) async-start(), calls=%async_computation.8 | async-start | bytes 6291456 | tf_op jit(solution)/shard_map/reduce_scatter | solution.py:696
  659.0 39.1 %collective-permute-start.67 = (bf16[144,2048]{1,0:T(8,128)(2,1)}, bf16[144,2048]{1,0:T(8,128)(2,1)}, u32[]{:S(2)}, u32[]{:S(2)}) collective-permute-start(bf16[144,2048]{1,0:T(8,128)(2,1)} %fusion.38), channel_id=1, source_target_pairs={{1,2},{2,1},{5,6},{6,5},{9,10},{10,9},{13,14},{14,13},{17,18},{18,... | collective-permute-start | bytes 1769480 | tf_op jit(solution)/shard_map/ppermute | solution.py:628
  660.6 37.5 %collective-permute-start.68 = (bf16[144,2048]{1,0:T(8,128)(2,1)}, bf16[144,2048]{1,0:T(8,128)(2,1)}, u32[]{:S(2)}, u32[]{:S(2)}) collective-permute-start(bf16[144,2048]{1,0:T(8,128)(2,1)} %fusion.38), channel_id=1, source_target_pairs={{0,1},{3,2},{4,5},{7,6},{8,9},{11,10},{12,13},{15,14},{16,17},{19,... | collective-permute-start | bytes 1769480 | tf_op jit(solution)/shard_map/ppermute | solution.py:629
  671.0 31.0 %collective-permute-start.70 = (bf16[2,128,2048]{2,1,0:T(8,128)(2,1)}, bf16[2,128,2048]{2,1,0:T(8,128)(2,1)}, u32[]{:S(2)}, u32[]{:S(2)}) collective-permute-start(bf16[2,128,2048]{2,1,0:T(8,128)(2,1)} %bitcast_convert_fusion), channel_id=1, source_target_pairs={{0,1},{3,2},{4,5},{7,6},{8,9},{11,10},{12,13},{15,14},{16,17},{19,... | collective-permute-start | bytes 3145736 | tf_op jit(solution)/shard_map/ppermute | solution.py:608
  696.0 39.5 %collective-permute-start.77 = (bf16[2,1,128,2048]{3,2,1,0:T(8,128)(2,1)}, bf16[2,1,128,2048]{3,2,1,0:T(8,128)(2,1)}, u32[]{:S(2)}, u32[]{:S(2)}) collective-permute-start(bf16[2,1,128,2048]{3,2,1,0:T(8,128)(2,1)} %get-tuple-element.561), channel_id=1, source_target_pairs={{0,8},{4,12},{8,0},{12,4},{1,9},{5,13},{9,1},{13,5},{2,10},{6,14},... | collective-permute-start | bytes 3145736 | tf_op jit(solution)/shard_map/ppermute | solution.py:435
  697.3 111.4 %collective-permute-start.73 = (bf16[2,1,128,2048]{3,2,1,0:T(8,128)(2,1)}, bf16[2,1,128,2048]{3,2,1,0:T(8,128)(2,1)}, u32[]{:S(2)}, u32[]{:S(2)}) collective-permute-start(bf16[2,1,128,2048]{3,2,1,0:T(8,128)(2,1)} %get-tuple-element.562), channel_id=1, source_target_pairs={{0,8},{4,12},{8,0},{12,4},{1,9},{5,13},{9,1},{13,5},{2,10},{6,14},... | collective-permute-start | bytes 3145736 | tf_op jit(solution)/shard_map/ppermute | solution.py:435
  706.2 29.3 %collective-permute-start.75 = (bf16[144,2048]{1,0:T(8,128)(2,1)}, bf16[144,2048]{1,0:T(8,128)(2,1)}, u32[]{:S(2)}, u32[]{:S(2)}) collective-permute-start(bf16[144,2048]{1,0:T(8,128)(2,1)} %get-tuple-element.554), channel_id=1, source_target_pairs={{1,2},{2,1},{5,6},{6,5},{9,10},{10,9},{13,14},{14,13},{17,18},{18,... | collective-permute-start | bytes 1769480 | tf_op jit(solution)/shard_map/ppermute | solution.py:634
  761.2 47.5 %collective-permute-start.71 = (bf16[2,128,2048]{2,1,0:T(8,128)(2,1)}, bf16[2,128,2048]{2,1,0:T(8,128)(2,1)S(1)}, u32[]{:S(2)}, u32[]{:S(2)}) collective-permute-start(bf16[2,128,2048]{2,1,0:T(8,128)(2,1)} %fusion.22), channel_id=1, source_target_pairs={{1,2},{2,1},{5,6},{6,5},{9,10},{10,9},{13,14},{14,13},{17,18},{18,... | collective-permute-start | bytes 3145736 | tf_op jit(solution)/shard_map/ppermute | solution.py:628
  761.9 46.8 %collective-permute-start.72 = (bf16[2,128,2048]{2,1,0:T(8,128)(2,1)}, bf16[2,128,2048]{2,1,0:T(8,128)(2,1)}, u32[]{:S(2)}, u32[]{:S(2)}) collective-permute-start(bf16[2,128,2048]{2,1,0:T(8,128)(2,1)} %fusion.22), channel_id=1, source_target_pairs={{0,1},{3,2},{4,5},{7,6},{8,9},{11,10},{12,13},{15,14},{16,17},{19,... | collective-permute-start | bytes 3145736 | tf_op jit(solution)/shard_map/ppermute | solution.py:629
  824.3 37.6 %collective-permute-start.82 = (bf16[2,128,2048]{2,1,0:T(8,128)(2,1)S(1)}, bf16[2,128,2048]{2,1,0:T(8,128)(2,1)}, u32[]{:S(2)}, u32[]{:S(2)}) collective-permute-start(bf16[2,128,2048]{2,1,0:T(8,128)(2,1)S(1)} %get-tuple-element.552), channel_id=1, source_target_pairs={{1,2},{2,1},{5,6},{6,5},{9,10},{10,9},{13,14},{14,13},{17,18},{18,... | collective-permute-start | bytes 3145736 | tf_op jit(solution)/shard_map/ppermute | solution.py:634
  825.9 35.9 %collective-permute-start.83 = (bf16[2,128,2048]{2,1,0:T(8,128)(2,1)S(1)}, bf16[2,128,2048]{2,1,0:T(8,128)(2,1)}, u32[]{:S(2)}, u32[]{:S(2)}) collective-permute-start(bf16[2,128,2048]{2,1,0:T(8,128)(2,1)S(1)} %get-tuple-element.551), channel_id=1, source_target_pairs={{0,1},{1,0},{2,3},{3,2},{4,5},{5,4},{6,7},{7,6},{8,9},{9,8},{10,11... | collective-permute-start | bytes 3145736 | tf_op jit(solution)/shard_map/ppermute | solution.py:435
  829.8 32.0 %collective-permute-start.85 = (bf16[2,64,2048]{2,1,0:T(8,128)(2,1)S(1)}, bf16[2,64,2048]{2,1,0:T(8,128)(2,1)S(1)}, u32[]{:S(2)}, u32[]{:S(2)}) collective-permute-start(bf16[2,64,2048]{2,1,0:T(8,128)(2,1)S(1)} %add_convert_fusion.8), channel_id=1, source_target_pairs={{0,1},{3,2},{4,5},{7,6},{8,9},{11,10},{12,13},{15,14},{16,17},{19,... | collective-permute-start | bytes 1572872 | tf_op jit(solution)/shard_map/ppermute | solution.py:490
  836.5 72.0 %collective-permute-start.91 = (bf16[2,2,128,2048]{3,2,1,0:T(8,128)(2,1)}, bf16[2,2,128,2048]{3,2,1,0:T(8,128)(2,1)}, u32[]{:S(2)}, u32[]{:S(2)}) collective-permute-start(bf16[2,2,128,2048]{3,2,1,0:T(8,128)(2,1)} %fusion.19), channel_id=1, source_target_pairs={{0,4},{4,0},{8,12},{12,8},{1,5},{5,1},{9,13},{13,9},{2,6},{6,2},{1... | collective-permute-start | bytes 6291464 | tf_op jit(solution)/shard_map/ppermute | solution.py:435
  870.3 38.2 %collective-permute-start.86 = (bf16[4,64,1664]{2,1,0:T(8,128)(2,1)}, bf16[4,64,1664]{2,1,0:T(8,128)(2,1)}, u32[]{:S(2)}, u32[]{:S(2)}) collective-permute-start(bf16[4,64,1664]{2,1,0:T(8,128)(2,1)} %get-tuple-element.572.refs_2_), channel_id=1, source_target_pairs={{0,16},{16,0},{1,17},{17,1},{2,18},{18,2},{3,19},{19,3},{4,20},{20... | collective-permute-start | bytes 2555912 | tf_op jit(solution)/shard_map/ppermute | solution.py:435
  895.9 49.9 %collective-permute-start.96 = (bf16[4,64,1664]{2,1,0:T(8,128)(2,1)S(1)}, bf16[4,64,1664]{2,1,0:T(8,128)(2,1)}, u32[]{:S(2)}, u32[]{:S(2)}) collective-permute-start(bf16[4,64,1664]{2,1,0:T(8,128)(2,1)S(1)} %get-tuple-element.574.refs_0_), channel_id=1, source_target_pairs={{0,16},{16,0},{1,17},{17,1},{2,18},{18,2},{3,19},{19,3},{4,20},{20... | collective-permute-start | bytes 2555912 | tf_op jit(solution)/shard_map/ppermute | solution.py:435
  (282 other events, 2544.8 us)
Sparse Core Ops, SparseCore 0:
  139.7 64.8 all-gather.1
  616.2 51.9 reduce-scatter.3
  671.1 54.3 reduce-scatter.5
  727.6 54.2 reduce-scatter.7

commit v3 on v2

--- a/solution.py
+++ b/solution.py
@@ -31,8 +31,11 @@
 
 def expert_kernel(
     capacity, tile_f, tile_d, tokens, extra, order_ref, norm_ref, up_ref,
-    wg_hbm, wu_hbm, wd_hbm, *refs
+    *refs
 ):
+    counts, extra = extra
+    sources = [refs[sum(counts[:i]) : sum(counts[: i + 1])] for i in range(3)]
+    refs = refs[sum(counts) :]
     shared_ref, back_ref, rows_ref, dy_ref, h_ref, dhg_ref, dhu_ref = refs[extra : extra + 7]
     ru_ref, gate_rows_ref, sums_ref, slot_ref, wg_ref, wu_ref, wd_ref, arrived = refs[extra + 7 :]
     group, width = norm_ref.shape[0], norm_ref.shape[2]
@@ -44,11 +47,19 @@
 
     def copies(j):
         at = pl.ds(j * tile_f, tile_f)
-        return [
-            pltpu.make_async_copy(wg_hbm.at[:, at], wg_ref.at[:, at], arrived.at[j, 0]),
-            pltpu.make_async_copy(wu_hbm.at[:, at], wu_ref.at[:, at], arrived.at[j, 1]),
-            pltpu.make_async_copy(wd_hbm.at[at, :], wd_ref.at[at, :], arrived.at[j, 2]),
-        ]
+        found = []
+        for i, whole in enumerate((wg_ref, wu_ref)):
+            for half, source in enumerate(sources[i]):
+                size = source.shape[0]
+                first = ((order_ref[2] + half) % 2) * size if len(sources[i]) > 1 else 0
+                to = whole.at[pl.ds(pl.multiple_of(first, size), size), at]
+                found.append((source.at[:, at], to, arrived.at[j, 2 * i + half]))
+        for half, source in enumerate(sources[2] if j == 0 else ()):
+            size = source.shape[0]
+            first = ((order_ref[2] + half) % 2) * size if len(sources[2]) > 1 else 0
+            to = wd_ref.at[pl.ds(pl.multiple_of(first, size), size), :]
+            found.append((source, to, arrived.at[j, 4 + half]))
+        return [pltpu.make_async_copy(*each) for each in found]
 
     def chosen(b):
         slots = lax.broadcasted_iota(jnp.int32, (capacity, tokens), 0).astype(F32)
@@ -137,9 +148,10 @@
 
 
 def expert_call(order, norm, up, tokens, weights, kept, part, parts, shared, capacity, deps, tile_f=512, tile_d=512):
-    wg, wu, wd = weights
     group, width = norm.shape[0], norm.shape[2]
-    hidden = wg.shape[1]
+    hidden = weights[0][0].shape[1]
+    counts = [len(parts) for parts in weights]
+    flat = [part for parts in weights for part in parts]
     rows = group * capacity
     first_steps = hidden // tile_f
     tiles = width // tile_d
@@ -161,17 +173,15 @@
     sizes = (width, width, hidden, hidden, hidden)
     struct = jax.ShapeDtypeStruct
     results = pl.pallas_call(
-        functools.partial(expert_kernel, capacity, tile_f, tile_d, tokens, extra),
+        functools.partial(expert_kernel, capacity, tile_f, tile_d, tokens, (counts, extra)),
         grid_spec=pltpu.PrefetchScalarGridSpec(
             num_scalar_prefetch=1,
             grid=(first_steps + tiles,),
             in_specs=[
                 fixed(norm.shape),
                 pl.BlockSpec((group, 1, tokens, width), lambda i, o: (0, micro, 0, 0)),
-                anywhere,
-                anywhere,
-                anywhere,
             ]
+            + [anywhere] * len(flat)
             + [anywhere] * extra,
             out_specs=[
                 pl.BlockSpec((1, group, tokens, tile_d), lambda i, o: (micro, 0, 0, late(i, o))),
@@ -183,19 +193,19 @@
                 pltpu.VMEM((rows, 1), F32),
                 pltpu.VMEM((rows, 1), F32),
                 pltpu.VMEM((group, tokens), F32),
-                pltpu.VMEM(wg.shape, BF16),
-                pltpu.VMEM(wu.shape, BF16),
-                pltpu.VMEM(wd.shape, BF16),
-                pltpu.SemaphoreType.DMA((first_steps, 3)),
+                pltpu.VMEM((width, hidden), BF16),
+                pltpu.VMEM((width, hidden), BF16),
+                pltpu.VMEM((hidden, width), BF16),
+                pltpu.SemaphoreType.DMA((first_steps, 6)),
             ],
         ),
         out_shape=[struct((2, group, tokens, width), BF16), struct((group, tokens + TAIL, width), BF16)]
         + [struct((parts * rows, size), BF16) for size in sizes],
-        input_output_aliases={6 + len(deps) + i: i for i in range(len(shared_in))}
-        | {6 + len(deps) + len(shared_in) + i: 2 + i for i in range(len(kept_in))},
+        input_output_aliases={3 + len(flat) + len(deps) + i: i for i in range(len(shared_in))}
+        | {3 + len(flat) + len(deps) + len(shared_in) + i: 2 + i for i in range(len(kept_in))},
         compiler_params=pltpu.CompilerParams(vmem_limit_bytes=58 * 2**20),
         cost_estimate=QUICK,
-    )(order, norm, up, wg, wu, wd, *deps, *shared_in, *kept_in)
+    )(order, norm, up, *flat, *deps, *shared_in, *kept_in)
     return results[0], results[1], results[2:]
 
 
@@ -687,11 +697,6 @@
     return lax.dynamic_slice(whole, start, (1, whole.shape[1], 1) + whole.shape[3:])[0, :, 0]
 
 
-def join_rows(own, moved):
-    first = lax.axis_index("dp") == 0
-    return jnp.concatenate([jnp.where(first, own, moved), jnp.where(first, moved, own)])
-
-
 def sum_rows(whole):
     return lax.psum_scatter(whole, "dp", scatter_dimension=0, tiled=True)
 
@@ -790,7 +795,7 @@
     token = turn([spread, upstream_flow], token, *copies)
     up_moved = [swap(copies[1], "dp", 1)] if two else []
     experts = [
-        lax.all_gather(own, "dp", axis=0, tiled=True) for own in copies[: 1 if two else 3]
+        [lax.all_gather(own, "dp", axis=0, tiled=True)] for own in (copies[::2] if two else copies)
     ]
     shape = (dp_size, 4, 4) + payload.shape[1:]
     if two:
@@ -844,7 +849,7 @@
         out_rows = out_rows.reshape(per_ctx, -1)
     sum_a, sum_b = [], []
     flow_a = Flow(scatter_ctx_steps(out_terms_of(0), sum_a))
-    token = turn([flow_a], experts[0])
+    token = turn([flow_a], experts[0][0])
     done = attention(1, token, [])
     token = turn([flow_a], done)
     flow_b = Flow(scatter_ctx_steps(out_terms_of(1), sum_b))
@@ -871,19 +876,17 @@
     gather_a = Flow(gather_steps(route(0, sum_a[0]), groups[0], (3, 3, 3, 3)))
     token, up_moved = turn([flow_b, gather_a, upstream_flow], values=up_moved + [token])
     if two:
-        last_moved = [swap(meet([copies[2]], token)[0], "dp", 1)]
-        experts.append(join_rows(expert_up[0], up_moved[0]))
+        experts.insert(1, [expert_up[0], up_moved[0]])
     token = turn([gather_a])
-    token = turn([gather_a, upstream_flow, flow_b], experts[0], experts[1])
-    if two:
-        experts.append(join_rows(expert_down[0], last_moved[0]))
+    token = turn([gather_a, upstream_flow, flow_b], experts[0][0], experts[2][0])
     second_payload = route(1, sum_b[0])
-    gather_b = Flow(gather_steps(second_payload, groups[1], (1, 1, 2, 3)))
+    gather_b = Flow(gather_steps(second_payload, groups[1], (2, 2, 3, 3)))
 
     shared, kept, calls = [None] * 4, None, 0
     back = [[None] * 4 for _ in micros]
     expert_index = place * 4 + line
-    order = jnp.stack([expert_index, expert_index * tokens // 512]).astype(jnp.int32)
+    order = jnp.stack([expert_index, expert_index * tokens // 512, lax.axis_index("dp")])
+    order = order.astype(jnp.int32)
 
     def expert(m, k, token, flows):
         nonlocal kept, calls

time: 994 us -> 981 us (0.987)
  other arithmetic: 159 us -> 143 us
    ppermute x64 -> x63, waiting for transfers between devices: 155 us -> 142 us  [swap(): lax.ppermute(value, axis, [(i, i ^ bit) for i in range(lax.axis_size(axis...]
    all_gather x1 -> x2, waiting for transfers between devices: 0.01 us -> 11.6 us  [body(): lax.all_gather(own, 'dp', axis=0, tiled=True)]
    unnamed x451 -> x423, local copies, waits for them, and re-layouts: 56.4 us -> 50.9 us
    ppermute x64 -> x63, starting transfers between devices: 75.4 us -> 70 us  [swap(): lax.ppermute(value, axis, [(i, i ^ bit) for i in range(lax.axis_size(axis...]
  transfers between devices with their start and end apart: 106 -> 106, of which waited for: 27 -> 28; matrix products, arithmetic and copies ran while one was open for 24% -> 22% of each run, Pallas kernels for 27% -> 28%
where the time goes in v3:
time: 981 us; the launch traced here: 969 us
  Pallas kernels  275 us (28%)
  waiting for transfers between devices  222 us (23%)
  starting transfers between devices  167 us (17%)
  other arithmetic  143 us (15%)
  local copies, waits for them, and re-layouts  94.6 us (10%)
  matrix products  51.3 us (5%)
  between operations  17.4 us (2%)
    pallas_call x8, Pallas kernels, expert_call(): pl.pallas_call(functools.partial(expert_kernel, capacity, tile_f, tile_d,...  165 us
    ppermute x63, waiting for transfers between devices, swap(): lax.ppermute(value, axis, [(i, i ^ bit) for i in range(lax.axis_size(axis...  142 us
    ppermute x63, starting transfers between devices, swap(): lax.ppermute(value, axis, [(i, i ^ bit) for i in range(lax.axis_size(axis...  70 us
    unnamed x423, local copies, waits for them, and re-layouts  50.9 us
    pallas_call x3, Pallas kernels, product_call(): pl.pallas_call(product_kernel, grid=(columns // wide, rows // tile), in_s...  49.3 us
    dot_general x6, matrix products, dot_t(): lax.dot_general(a, b, (((1,), (1,)), ((), ())), preferred_element_type=F32)  28.2 us
    ppermute x3, starting transfers between devices, scatter_steps(): lax.ppermute(second, 'expert', INWARD)  24.1 us
    pallas_call x2, Pallas kernels, attention_backward_call(): pl.pallas_call(functools.partial(backward_kernel, dh), grid=(heads,), in_...  22.4 us
  transfers between devices with their start and end apart: 106, of which 28 were waited for; matrix products, arithmetic and copies ran while one was open for 22% of the time, Pallas kernels for 28%

profile of v3, /device:TPU:0, one launch (start us, length us, event | category | flops | bytes accessed | tf_op | source)
XLA Modules:
  0.0 969.1 jit_solution(11287135556599481582)
XLA Ops:
  24.0 12.1 %all-to-all-done = bf16[4,64,1664]{2,1,0:T(8,128)(2,1)S(1)} async-done(((bf16[4,64,1664]{2,1,0:T(8,128)(2,1)}), bf16[4,64,1664]{2,1,0:T(8,128)(2,1)S(1)}, u32[]{:S(2)}, u32[]{:S(2)}) %all-to-all-start) | async-done | bytes 852000 | tf_op jit(solution)/shard_map/all_to_all | solution.py:783
  47.2 19.2 %collective-permute-done.refs_0_ = bf16[4,64,2176]{2,1,0:T(8,128)(2,1)} collective-permute-done((bf16[4,64,2176]{2,1,0:T(8,128)(2,1)S(1)}, bf16[4,64,2176]{2,1,0:T(8,128)(2,1)}, u32[]{:S(2)}, u32[]{:S(2)}) %collective-permute-start) | collective-permute-done | bytes 1114144 | tf_op jit(solution)/shard_map/ppermute | solution.py:445
  81.8 14.8 %collective-permute-done.10.refs_5_ = bf16[2,128,2048]{2,1,0:T(8,128)(2,1)S(1)} collective-permute-done((bf16[2,128,2048]{2,1,0:T(8,128)(2,1)}, bf16[2,128,2048]{2,1,0:T(8,128)(2,1)S(1)}, u32[]{:S(2)}, u32[]{:S(2)}) %collective-permute-start.10) | collective-permute-done | bytes 1048608 | tf_op jit(solution)/shard_map/ppermute | solution.py:445
  110.6 17.5 %collective-permute-done.14.refs_3_ = bf16[2,128,2048]{2,1,0:T(8,128)(2,1)S(1)} collective-permute-done((bf16[2,128,2048]{2,1,0:T(8,128)(2,1)}, bf16[2,128,2048]{2,1,0:T(8,128)(2,1)S(1)}, u32[]{:S(2)}, u32[]{:S(2)}) %collective-permute-start.14) | collective-permute-done | bytes 1048608 | tf_op jit(solution)/shard_map/ppermute | solution.py:445
  154.7 15.4 %collective-permute-done.15.refs_0_ = bf16[4,64,2176]{2,1,0:T(8,128)(2,1)} collective-permute-done((bf16[4,64,2176]{2,1,0:T(8,128)(2,1)}, bf16[4,64,2176]{2,1,0:T(8,128)(2,1)}, u32[]{:S(2)}, u32[]{:S(2)}) %collective-permute-start.15) | collective-permute-done | bytes 1114144 | tf_op jit(solution)/shard_map/ppermute | solution.py:445
  178.9 6.3 fusion.16.joined_ref
  185.2 8.5 shard_map.264
  211.3 6.3 fusion.14.joined_ref
  217.7 8.5 shard_map.266.refs_1_
  229.2 14.5 %collective-permute-done.19.refs_0_ = bf16[128,2048]{1,0:T(8,128)(2,1)} collective-permute-done((bf16[128,2048]{1,0:T(8,128)(2,1)S(1)}, bf16[128,2048]{1,0:T(8,128)(2,1)}, u32[]{:S(2)}, u32[]{:S(2)}) %collective-permute-start.19) | collective-permute-done | bytes 524320 | tf_op jit(solution)/shard_map/ppermute | solution.py:445
  251.0 6.2 collective-permute-start.21
  258.8 11.5 %collective-permute-done.21.refs_1_ = bf16[144,2048]{1,0:T(8,128)(2,1)S(1)} collective-permute-done((bf16[144,2048]{1,0:T(8,128)(2,1)}, bf16[144,2048]{1,0:T(8,128)(2,1)S(1)}, u32[]{:S(2)}, u32[]{:S(2)}) %collective-permute-start.21) | collective-permute-done | bytes 589856 | tf_op jit(solution)/shard_map/ppermute | solution.py:445
  280.6 17.1 %collective-permute-done.27.refs_1_ = bf16[144,2048]{1,0:T(8,128)(2,1)} collective-permute-done((bf16[144,2048]{1,0:T(8,128)(2,1)}, bf16[144,2048]{1,0:T(8,128)(2,1)}, u32[]{:S(2)}, u32[]{:S(2)}) %collective-permute-start.27) | collective-permute-done | bytes 589856 | tf_op jit(solution)/shard_map/ppermute | solution.py:558
  302.4 11.6 %all-gather.5.cloned.1.call-done.refs_5_.refs_3_ = bf16[1024,2048]{1,0:T(8,128)(2,1)} async-done(((bf16[512,2048]{1,0:T(8,128)(2,1)}), bf16[1024,2048]{1,0:T(8,128)(2,1)}) %all-gather.5.cloned.1.call-update) | async-done | bytes 4194320 | tf_op jit(solution)/shard_map/all_gather | solution.py:798
  340.0 20.5 %shard_map.271 = (bf16[2,4,128,2048]{3,2,1,0:T(8,128)(2,1)}, bf16[4,144,2048]{2,1,0:T(8,128)(2,1)}, bf16[2560,2048]{1,0:T(8,128)(2,1)}, bf16[2560,2048]{1,0:T(8,...) custom-call(s32[3]{0:T(128)} %pad_add_fusion.1.order_ref, ...), custom_call_target="tpu_custom_call" | custom-call | flops 1000 | bytes 1000 | tf_op jit(solution)/shard_map/pallas_call | solution.py:175
  363.4 20.6 %shard_map.273 = (bf16[2,4,128,2048]{3,2,1,0:T(8,128)(2,1)}, bf16[4,144,2048]{2,1,0:T(8,128)(2,1)}, bf16[2560,2048]{1,0:T(8,128)(2,1)}, bf16[2560,2048]{1,0:T(8,...) custom-call(s32[3]{0:T(128)} %pad_add_fusion.1.order_ref, ...), custom_call_target="tpu_custom_call", output_to_operand_aliasing={{2}: (8, {}), {3}: (9, {}), {4}: (10, {}), {5}: (11, {}), {... | custom-call | flops 1000 | bytes 1000 | tf_op jit(solution)/shard_map/pallas_call | solution.py:175
  389.3 20.7 %shard_map.275 = (bf16[2,4,128,2048]{3,2,1,0:T(8,128)(2,1)}, bf16[4,144,2048]{2,1,0:T(8,128)(2,1)}, bf16[2560,2048]{1,0:T(8,128)(2,1)}, bf16[2560,2048]{1,0:T(8,...) custom-call(s32[3]{0:T(128)} %pad_add_fusion.1.order_ref, ...), custom_call_target="tpu_custom_call", output_to_operand_aliasing={{2}: (8, {}), {3}: (9, {}), {4}: (10, {}), {5}: (11, {}), {... | custom-call | flops 1000 | bytes 1000 | tf_op jit(solution)/shard_map/pallas_call | solution.py:175
  421.7 20.5 %shard_map.277 = (bf16[2,4,128,2048]{3,2,1,0:T(8,128)(2,1)}, bf16[4,144,2048]{2,1,0:T(8,128)(2,1)}, bf16[2560,2048]{1,0:T(8,128)(2,1)}, bf16[2560,2048]{1,0:T(8,...) custom-call(s32[3]{0:T(128)} %pad_add_fusion.1.order_ref, ...), custom_call_target="tpu_custom_call", output_to_operand_aliasing={{2}: (8, {}), {3}: (9, {}), {4}: (10, {}), {5}: (11, {}), {... | custom-call | flops 1000 | bytes 1000 | tf_op jit(solution)/shard_map/pallas_call | solution.py:175
  442.3 5.8 collective-permute-done.45.refs_2_
  453.7 20.7 %shard_map.279 = (bf16[2,4,128,2048]{3,2,1,0:T(8,128)(2,1)}, bf16[4,144,2048]{2,1,0:T(8,128)(2,1)}, bf16[2560,2048]{1,0:T(8,128)(2,1)}, bf16[2560,2048]{1,0:T(8,...) custom-call(s32[3]{0:T(128)} %pad_add_fusion.1.order_ref, ...), custom_call_target="tpu_custom_call", output_to_operand_aliasing={{0}: (8, {}), {2}: (9, {}), {3}: (10, {}), {4}: (11, {}), {... | custom-call | flops 1000 | bytes 1000 | tf_op jit(solution)/shard_map/pallas_call | solution.py:175
  481.4 20.6 %shard_map.281 = (bf16[2,4,128,2048]{3,2,1,0:T(8,128)(2,1)}, bf16[4,144,2048]{2,1,0:T(8,128)(2,1)}, bf16[2560,2048]{1,0:T(8,128)(2,1)}, bf16[2560,2048]{1,0:T(8,...) custom-call(s32[3]{0:T(128)} %pad_add_fusion.1.order_ref, ...), custom_call_target="tpu_custom_call", output_to_operand_aliasing={{0}: (8, {}), {2}: (9, {}), {3}: (10, {}), {4}: (11, {}), {... | custom-call | flops 1000 | bytes 1000 | tf_op jit(solution)/shard_map/pallas_call | solution.py:175
  502.0 6.1 collective-permute-done.50.refs_0_
  510.2 20.7 %shard_map.283 = (bf16[2,4,128,2048]{3,2,1,0:T(8,128)(2,1)}, bf16[4,144,2048]{2,1,0:T(8,128)(2,1)}, bf16[2560,2048]{1,0:T(8,128)(2,1)}, bf16[2560,2048]{1,0:T(8,...) custom-call(s32[3]{0:T(128)} %pad_add_fusion.1.order_ref, ...), custom_call_target="tpu_custom_call", output_to_operand_aliasing={{0}: (8, {}), {2}: (9, {}), {3}: (10, {}), {4}: (11, {}), {... | custom-call | flops 1000 | bytes 1000 | tf_op jit(solution)/shard_map/pallas_call | solution.py:175
  531.0 6.8 collective-permute-done.48.refs_0_
  546.0 7.2 collective-permute-start.52
  554.2 20.5 %shard_map.285 = (bf16[2,4,128,2048]{3,2,1,0:T(8,128)(2,1)}, bf16[4,144,2048]{2,1,0:T(8,128)(2,1)}, bf16[2560,2048]{1,0:T(8,128)(2,1)}, bf16[2560,2048]{1,0:T(8,...) custom-call(s32[3]{0:T(128)} %pad_add_fusion.1.order_ref, ...), custom_call_target="tpu_custom_call", output_to_operand_aliasing={{0}: (8, {}), {2}: (9, {}), {3}: (10, {}), {4}: (11, {}), {... | custom-call | flops 1000 | bytes 1000 | tf_op jit(solution)/shard_map/pallas_call | solution.py:175
  577.9 7.1 collective-permute-start.55
  585.0 17.0 %shard_map.287.refs_5_ = bf16[1024,2048]{1,0:T(8,128)(2,1)} custom-call(bf16[2560,1024]{1,0:T(8,128)(2,1)} %get-tuple-element.392.left_ref, bf16[2560,2048]{1,0:T(8,128)(2,1)} %get-tuple-element.393.right_ref, bf16[144,2048]{1,0:T(8,128)(2,1)} %get-tuple-element.389.refs_0_), custom_call_target="tpu_custom_call" | custom-call | flops 1000 | bytes 1000 | tf_op jit(solution)/shard_map/pallas_call | solution.py:220
  602.2 5.6 add_convert_fusion
  618.8 16.2 %shard_map.289.refs_5_ = bf16[2048,1024]{1,0:T(8,128)(2,1)} custom-call(bf16[2560,2048]{1,0:T(8,128)(2,1)} %get-tuple-element.402.left_ref, bf16[2560,1024]{1,0:T(8,128)(2,1)} %get-tuple-element.403.right_ref, bf16[144,2048]{1,0:T(8,128)(2,1)} %get-tuple-element.395.refs_0_), custom_call_target="tpu_custom_call" | custom-call | flops 1000 | bytes 1000 | tf_op jit(solution)/shard_map/pallas_call | solution.py:220
  646.0 7.1 collective-permute-start.67
  665.5 16.1 %shard_map.291.refs_6_ = bf16[2048,1024]{1,0:T(8,128)(2,1)} custom-call(bf16[2560,2048]{1,0:T(8,128)(2,1)} %get-tuple-element.402.left_ref, bf16[2560,1024]{1,0:T(8,128)(2,1)} %get-tuple-element.409.right_ref, bf16[144,2048]{1,0:T(8,128)(2,1)} %get-tuple-element.406.refs_0_), custom_call_target="tpu_custom_call" | custom-call | flops 1000 | bytes 1000 | tf_op jit(solution)/shard_map/pallas_call | solution.py:220
  707.9 11.2 %shard_map.294 = (bf16[512,1536]{1,0:T(8,128)(2,1)S(1)}, f32[2,128]{1,0:T(2,128)S(1)}) custom-call(f32[512,1536]{1,0:T(8,128)S(1)} %copy-done.9, bf16[512,512]{1,0:T(8,128)(2,1)S(1)} %copy-done.45, f32[512,128]{1,0:T(8,128)S(1)} %copy-done.33, f32[512,128]{1,0:T(8,128)S(1)} %copy-done.25, f32[2,128]{1,0:T(2,128)S(1)} %copy-done.53, s32[512,1]{1,0:T(8,128)S(1)} %copy-done.31, ...), custom_call_target="tpu_custom_call" | custom-call | flops 1000 | bytes 1000 | tf_op jit(solution)/shard_map/pallas_call | solution.py:435
  727.3 8.0 fusion.12.refs_2_
  735.3 5.9 collective-permute-done.77.refs_0_
  747.5 9.9 %collective-permute-start.71 = (bf16[2,128,2048]{2,1,0:T(8,128)(2,1)}, bf16[2,128,2048]{2,1,0:T(8,128)(2,1)}, u32[]{:S(2)}, u32[]{:S(2)}) collective-permute-start(bf16[2,128,2048]{2,1,0:T(8,128)(2,1)} %fusion.22), channel_id=1, source_target_pairs={{0,1},{3,2},{4,5},{7,6},{8,9},{11,10},{12,13},{15,14},{16,17},{19,... | collective-permute-start | bytes 3145736 | tf_op jit(solution)/shard_map/ppermute | solution.py:639
  762.9 11.2 %shard_map.298 = (bf16[512,1536]{1,0:T(8,128)(2,1)S(1)}, f32[2,128]{1,0:T(2,128)S(1)}) custom-call(f32[512,1536]{1,0:T(8,128)S(1)} %copy-done.7, bf16[512,512]{1,0:T(8,128)(2,1)S(1)} %convolution_convert_fusion.2.do_ref, f32[512,128]{1,0:T(8,128)S(1)} %copy-done.35, f32[512,128]{1,0:T(8,128)S(1)} %copy-done.27, f32[2,128]{1,0:T(2,128)S(1)} %copy-done.53, ...), custom_call_target="tpu_custom_call" | custom-call | flops 1000 | bytes 1000 | tf_op jit(solution)/shard_map/pallas_call | solution.py:435
  779.9 8.8 fusion.5
  795.4 8.4 collective-permute-done.80.refs_3_
  804.6 5.4 fusion.20
  815.5 5.2 collective-permute-start.84
  823.7 6.1 shard_map.300
  833.2 6.6 shard_map.301
  840.5 7.1 collective-permute-done.84.refs_3_
  856.2 5.9 collective-permute-done.86.refs_0_
  866.6 11.8 %collective-permute-start.89 = (bf16[4,64,1664]{2,1,0:T(8,128)(2,1)}, bf16[4,64,1664]{2,1,0:T(8,128)(2,1)}, u32[]{:S(2)}, u32[]{:S(2)}) collective-permute-start(bf16[4,64,1664]{2,1,0:T(8,128)(2,1)} %fusion.31), channel_id=1, source_target_pairs={{0,1},{3,2},{4,5},{7,6},{8,9},{11,10},{12,13},{15,14},{16,17},{19,... | collective-permute-start | bytes 2555912 | tf_op jit(solution)/shard_map/ppermute | solution.py:514
  906.4 8.0 collective-permute-done.93.refs_2_
  945.0 9.5 all-to-all-done.1.payload_ref
  (829 shorter events, 393.3 us)
Async XLA Ops:
  8.5 37.5 %collective-permute-start.3 = (bf16[2,128,2048]{2,1,0:T(8,128)(2,1)S(1)}, bf16[2,128,2048]{2,1,0:T(8,128)(2,1)}, u32[]{:S(2)}, u32[]{:S(2)}) collective-permute-start(bf16[2,128,2048]{2,1,0:T(8,128)(2,1)S(1)} %bitcast.487), channel_id=1, source_target_pairs={{0,1},{1,0},{2,3},{3,2},{4,5},{5,4},{6,7},{7,6},{8,9},{9,8},{10,11... | collective-permute-start | bytes 3145736 | tf_op jit(solution)/shard_map/ppermute | solution.py:445
  11.6 35.5 %collective-permute-start.4 = (bf16[2,128,2048]{2,1,0:T(8,128)(2,1)S(1)}, bf16[2,128,2048]{2,1,0:T(8,128)(2,1)}, u32[]{:S(2)}, u32[]{:S(2)}) collective-permute-start(bf16[2,128,2048]{2,1,0:T(8,128)(2,1)S(1)} %bitcast.488), channel_id=1, source_target_pairs={{1,2},{2,1},{5,6},{6,5},{9,10},{10,9},{13,14},{14,13},{17,18},{18,... | collective-permute-start | bytes 3145736 | tf_op jit(solution)/shard_map/ppermute | solution.py:585
  23.8 184.1 %all-gather.3.cloned.1.call-start = ((), (), s32[]{:S(2)}) async-start(), calls=%async_computation.5 | async-start | bytes 6291456 | tf_op jit(solution)/shard_map/all_gather | solution.py:798
  38.3 28.0 %collective-permute-start = (bf16[4,64,2176]{2,1,0:T(8,128)(2,1)S(1)}, bf16[4,64,2176]{2,1,0:T(8,128)(2,1)}, u32[]{:S(2)}, u32[]{:S(2)}) collective-permute-start(bf16[4,64,2176]{2,1,0:T(8,128)(2,1)S(1)} %pad_maximum_fusion.8.refs_0_), channel_id=1, source_target_pairs={{0,1},{1,0},{2,3},{3,2},{4,5},{5,4},{6,7},{7,6},{8,9},{9,8},{10,11... | collective-permute-start | bytes 3342344 | tf_op jit(solution)/shard_map/ppermute | solution.py:445
  47.1 34.7 %collective-permute-start.9 = (bf16[2,128,2048]{2,1,0:T(8,128)(2,1)}, bf16[2,128,2048]{2,1,0:T(8,128)(2,1)}, u32[]{:S(2)}, u32[]{:S(2)}) collective-permute-start(bf16[2,128,2048]{2,1,0:T(8,128)(2,1)} %bitcast.7), channel_id=1, source_target_pairs={{0,4},{4,0},{8,12},{12,8},{1,5},{5,1},{9,13},{13,9},{2,6},{6,2},{1... | collective-permute-start | bytes 3145736 | tf_op jit(solution)/shard_map/ppermute | solution.py:445
  100.5 29.9 %collective-permute-start.11 = (bf16[4,64,2176]{2,1,0:T(8,128)(2,1)}, bf16[4,64,2176]{2,1,0:T(8,128)(2,1)S(1)}, u32[]{:S(2)}, u32[]{:S(2)}) collective-permute-start(bf16[4,64,2176]{2,1,0:T(8,128)(2,1)} %get-tuple-element.241.refs_4_), channel_id=1, source_target_pairs={{1,0},{2,3},{5,4},{6,7},{9,8},{10,11},{13,12},{14,15},{17,16},{18,... | collective-permute-start | bytes 3342344 | tf_op jit(solution)/shard_map/ppermute | solution.py:486
  108.9 45.8 %collective-permute-start.16 = (bf16[2,128,2048]{2,1,0:T(8,128)(2,1)}, bf16[2,128,2048]{2,1,0:T(8,128)(2,1)}, u32[]{:S(2)}, u32[]{:S(2)}) collective-permute-start(bf16[2,128,2048]{2,1,0:T(8,128)(2,1)} %get-tuple-element.243), channel_id=1, source_target_pairs={{1,2},{2,1},{5,6},{6,5},{9,10},{10,9},{13,14},{14,13},{17,18},{18,... | collective-permute-start | bytes 3145736 | tf_op jit(solution)/shard_map/ppermute | solution.py:591
  134.6 35.5 %collective-permute-start.15 = (bf16[4,64,2176]{2,1,0:T(8,128)(2,1)}, bf16[4,64,2176]{2,1,0:T(8,128)(2,1)}, u32[]{:S(2)}, u32[]{:S(2)}) collective-permute-start(bf16[4,64,2176]{2,1,0:T(8,128)(2,1)} %get-tuple-element.548), channel_id=1, source_target_pairs={{0,16},{16,0},{1,17},{17,1},{2,18},{18,2},{3,19},{19,3},{4,20},{20... | collective-permute-start | bytes 3342344 | tf_op jit(solution)/shard_map/ppermute | solution.py:445
  138.0 176.0 %all-gather.5.cloned.1.call-start = ((), (), s32[]{:S(2)}) async-start(), calls=%async_computation.6 | async-start | bytes 6291456 | tf_op jit(solution)/shard_map/all_gather | solution.py:798
  200.5 56.7 %collective-permute-start.25 = (bf16[1024,1024]{1,0:T(8,128)(2,1)}, bf16[1024,1024]{1,0:T(8,128)(2,1)}, u32[]{:S(2)}, u32[]{:S(2)}) collective-permute-start(bf16[1024,1024]{1,0:T(8,128)(2,1)} %shard_map.261.refs_5_), channel_id=1, source_target_pairs={{0,16},{16,0},{1,17},{17,1},{2,18},{18,2},{3,19},{19,3},{4,20},{20... | collective-permute-start | bytes 6291464 | tf_op jit(solution)/shard_map/ppermute | solution.py:445
  203.1 55.7 %collective-permute-start.23 = (bf16[2,128,2048]{2,1,0:T(8,128)(2,1)}, bf16[2,128,2048]{2,1,0:T(8,128)(2,1)}, u32[]{:S(2)}, u32[]{:S(2)}) collective-permute-start(bf16[2,128,2048]{2,1,0:T(8,128)(2,1)} %get-tuple-element.251), channel_id=1, source_target_pairs={{1,0},{2,3},{5,4},{6,7},{9,8},{10,11},{13,12},{14,15},{17,16},{18,... | collective-permute-start | bytes 3145736 | tf_op jit(solution)/shard_map/ppermute | solution.py:595
  206.9 51.8 %collective-permute-start.24 = (bf16[2,128,2048]{2,1,0:T(8,128)(2,1)}, bf16[2,128,2048]{2,1,0:T(8,128)(2,1)}, u32[]{:S(2)}, u32[]{:S(2)}) collective-permute-start(bf16[2,128,2048]{2,1,0:T(8,128)(2,1)} %broadcast_select_fusion.3), channel_id=1, source_target_pairs={{0,8},{4,12},{8,0},{12,4},{1,9},{5,13},{9,1},{13,5},{2,10},{6,14},... | collective-permute-start | bytes 3145736 | tf_op jit(solution)/shard_map/ppermute | solution.py:445
  210.3 33.4 %collective-permute-start.19 = (bf16[128,2048]{1,0:T(8,128)(2,1)S(1)}, bf16[128,2048]{1,0:T(8,128)(2,1)}, u32[]{:S(2)}, u32[]{:S(2)}) collective-permute-start(bf16[128,2048]{1,0:T(8,128)(2,1)S(1)} %fusion.65), channel_id=1, source_target_pairs={{0,8},{4,12},{8,0},{12,4},{1,9},{5,13},{9,1},{13,5},{2,10},{6,14},... | collective-permute-start | bytes 1572872 | tf_op jit(solution)/shard_map/ppermute | solution.py:445
  229.2 29.6 %collective-permute-start.20 = (bf16[2,128,2048]{2,1,0:T(8,128)(2,1)}, bf16[2,128,2048]{2,1,0:T(8,128)(2,1)S(1)}, u32[]{:S(2)}, u32[]{:S(2)}) collective-permute-start(bf16[2,128,2048]{2,1,0:T(8,128)(2,1)} %bitcast.55), channel_id=1, source_target_pairs={{0,4},{4,0},{8,12},{12,8},{1,5},{5,1},{9,13},{13,9},{2,6},{6,2},{1... | collective-permute-start | bytes 3145736 | tf_op jit(solution)/shard_map/ppermute | solution.py:445
  258.7 462.1 %reduce-scatter.4.cloned.1.call-start = ((), (), s32[]{:S(2)}) async-start(), calls=%async_computation.7 | async-start | bytes 6291456 | tf_op jit(solution)/shard_map/reduce_scatter | solution.py:701
  277.2 39.2 %collective-permute-start.30 = (bf16[4,2,128,2048]{3,2,1,0:T(8,128)(2,1)}, bf16[4,2,128,2048]{3,2,1,0:T(8,128)(2,1)}, u32[]{:S(2)}, u32[]{:S(2)}) collective-permute-start(bf16[4,2,128,2048]{3,2,1,0:T(8,128)(2,1)} %pad_maximum_fusion.1.up_ref), channel_id=1, source_target_pairs={{0,4},{4,0},{8,12},{12,8},{1,5},{5,1},{9,13},{13,9},{2,6},{6,2},{1... | collective-permute-start | bytes 12582920 | tf_op jit(solution)/shard_map/ppermute | solution.py:445
  279.2 37.2 %collective-permute-start.29 = (bf16[2,128,2048]{2,1,0:T(8,128)(2,1)}, bf16[2,128,2048]{2,1,0:T(8,128)(2,1)S(1)}, u32[]{:S(2)}, u32[]{:S(2)}) collective-permute-start(bf16[2,128,2048]{2,1,0:T(8,128)(2,1)} %broadcast_select_fusion.2), channel_id=1, source_target_pairs={{0,8},{4,12},{8,0},{12,4},{1,9},{5,13},{9,1},{13,5},{2,10},{6,14},... | collective-permute-start | bytes 3145736 | tf_op jit(solution)/shard_map/ppermute | solution.py:445
  321.4 39.2 %collective-permute-start.33 = (bf16[4,2,128,2048]{3,2,1,0:T(8,128)(2,1)}, bf16[4,2,128,2048]{3,2,1,0:T(8,128)(2,1)}, u32[]{:S(2)}, u32[]{:S(2)}) collective-permute-start(bf16[4,2,128,2048]{3,2,1,0:T(8,128)(2,1)} %pad_maximum_fusion.2.up_ref), channel_id=1, source_target_pairs={{0,4},{4,0},{8,12},{12,8},{1,5},{5,1},{9,13},{13,9},{2,6},{6,2},{1... | collective-permute-start | bytes 12582920 | tf_op jit(solution)/shard_map/ppermute | solution.py:445
  324.5 36.1 %collective-permute-start.32 = (bf16[4,144,2048]{2,1,0:T(8,128)(2,1)}, bf16[4,144,2048]{2,1,0:T(8,128)(2,1)}, u32[]{:S(2)}, u32[]{:S(2)}) collective-permute-start(bf16[4,144,2048]{2,1,0:T(8,128)(2,1)} %pad_maximum_fusion.3.norm_ref), channel_id=1, source_target_pairs={{0,4},{4,0},{8,12},{12,8},{1,5},{5,1},{9,13},{13,9},{2,6},{6,2},{1... | collective-permute-start | bytes 7077896 | tf_op jit(solution)/shard_map/ppermute | solution.py:445
  324.9 59.1 %collective-permute-start.36 = (bf16[4,144,2048]{2,1,0:T(8,128)(2,1)}, bf16[4,144,2048]{2,1,0:T(8,128)(2,1)S(1)}, u32[]{:S(2)}, u32[]{:S(2)}) collective-permute-start(bf16[4,144,2048]{2,1,0:T(8,128)(2,1)} %pad_maximum_fusion.3.norm_ref), channel_id=1, source_target_pairs={{0,8},{4,12},{8,0},{12,4},{1,9},{5,13},{9,1},{13,5},{2,10},{6,14},... | collective-permute-start | bytes 7077896 | tf_op jit(solution)/shard_map/ppermute | solution.py:445
  385.6 28.6 %collective-permute-start.39 = (bf16[4,144,2048]{2,1,0:T(8,128)(2,1)}, bf16[4,144,2048]{2,1,0:T(8,128)(2,1)S(1)}, u32[]{:S(2)}, u32[]{:S(2)}) collective-permute-start(bf16[4,144,2048]{2,1,0:T(8,128)(2,1)} %get-tuple-element.290.norm_ref.refs_4_), channel_id=1, source_target_pairs={{0,4},{4,0},{8,12},{12,8},{1,5},{5,1},{9,13},{13,9},{2,6},{6,2},{1... | collective-permute-start | bytes 7077896 | tf_op jit(solution)/shard_map/ppermute | solution.py:445
  419.5 28.6 %collective-permute-start.43 = (bf16[4,144,2048]{2,1,0:T(8,128)(2,1)S(1)}, bf16[4,144,2048]{2,1,0:T(8,128)(2,1)S(1)}, u32[]{:S(2)}, u32[]{:S(2)}) collective-permute-start(bf16[4,144,2048]{2,1,0:T(8,128)(2,1)S(1)} %pad_maximum_fusion.4.norm_ref), channel_id=1, source_target_pairs={{0,4},{4,0},{8,12},{12,8},{1,5},{5,1},{9,13},{13,9},{2,6},{6,2},{1... | collective-permute-start | bytes 7077896 | tf_op jit(solution)/shard_map/ppermute | solution.py:445
  481.4 49.5 %collective-permute-start.49 = (bf16[4,144,2048]{2,1,0:T(8,128)(2,1)}, bf16[4,144,2048]{2,1,0:T(8,128)(2,1)S(1)}, u32[]{:S(2)}, u32[]{:S(2)}) collective-permute-start(bf16[4,144,2048]{2,1,0:T(8,128)(2,1)} %get-tuple-element.341), channel_id=1, source_target_pairs={{0,4},{4,0},{8,12},{12,8},{1,5},{5,1},{9,13},{13,9},{2,6},{6,2},{1... | collective-permute-start | bytes 7077896 | tf_op jit(solution)/shard_map/ppermute | solution.py:445
  509.2 28.6 %collective-permute-start.51 = (bf16[4,144,2048]{2,1,0:T(8,128)(2,1)}, bf16[4,144,2048]{2,1,0:T(8,128)(2,1)}, u32[]{:S(2)}, u32[]{:S(2)}) collective-permute-start(bf16[4,144,2048]{2,1,0:T(8,128)(2,1)} %get-tuple-element.356), channel_id=1, source_target_pairs={{0,4},{4,0},{8,12},{12,8},{1,5},{5,1},{9,13},{13,9},{2,6},{6,2},{1... | collective-permute-start | bytes 7077896 | tf_op jit(solution)/shard_map/ppermute | solution.py:445
  509.2 28.6 %collective-permute-start.48 = (bf16[2,144,2048]{2,1,0:T(8,128)(2,1)}, bf16[2,144,2048]{2,1,0:T(8,128)(2,1)S(1)}, u32[]{:S(2)}, u32[]{:S(2)}) collective-permute-start(bf16[2,144,2048]{2,1,0:T(8,128)(2,1)} %get-tuple-element.573), channel_id=1, source_target_pairs={{0,8},{4,12},{8,0},{12,4},{1,9},{5,13},{9,1},{13,5},{2,10},{6,14},... | collective-permute-start | bytes 3538952 | tf_op jit(solution)/shard_map/ppermute | solution.py:445
  510.0 92.1 %collective-permute-start.58 = (bf16[2,4,128,2048]{3,2,1,0:T(8,128)(2,1)}, bf16[2,4,128,2048]{3,2,1,0:T(8,128)(2,1)}, u32[]{:S(2)}, u32[]{:S(2)}) collective-permute-start(bf16[2,4,128,2048]{3,2,1,0:T(8,128)(2,1)} %get-tuple-element.391), channel_id=1, source_target_pairs={{0,4},{4,0},{8,12},{12,8},{1,5},{5,1},{9,13},{13,9},{2,6},{6,2},{1... | collective-permute-start | bytes 12582920 | tf_op jit(solution)/shard_map/ppermute | solution.py:445
  538.8 63.3 %collective-permute-start.57 = (bf16[4,144,2048]{2,1,0:T(8,128)(2,1)}, bf16[4,144,2048]{2,1,0:T(8,128)(2,1)}, u32[]{:S(2)}, u32[]{:S(2)}) collective-permute-start(bf16[4,144,2048]{2,1,0:T(8,128)(2,1)} %get-tuple-element.390), channel_id=1, source_target_pairs={{0,4},{4,0},{8,12},{12,8},{1,5},{5,1},{9,13},{13,9},{2,6},{6,2},{1... | collective-permute-start | bytes 7077896 | tf_op jit(solution)/shard_map/ppermute | solution.py:445
  543.6 31.2 %collective-permute-start.53 = (bf16[2,144,2048]{2,1,0:T(8,128)(2,1)S(1)}, bf16[2,144,2048]{2,1,0:T(8,128)(2,1)}, u32[]{:S(2)}, u32[]{:S(2)}) collective-permute-start(bf16[2,144,2048]{2,1,0:T(8,128)(2,1)S(1)} %get-tuple-element.572), channel_id=1, source_target_pairs={{0,8},{4,12},{8,0},{12,4},{1,9},{5,13},{9,1},{13,5},{2,10},{6,14},... | collective-permute-start | bytes 3538952 | tf_op jit(solution)/shard_map/ppermute | solution.py:445
  546.0 28.7 %collective-permute-start.52 = (bf16[144,2048]{1,0:T(8,128)(2,1)S(1)}, bf16[144,2048]{1,0:T(8,128)(2,1)}, u32[]{:S(2)}, u32[]{:S(2)}) collective-permute-start(bf16[144,2048]{1,0:T(8,128)(2,1)S(1)} %bitcast_convert_fusion.2), channel_id=1, source_target_pairs={{0,1},{3,2},{4,5},{7,6},{8,9},{11,10},{12,13},{15,14},{16,17},{19,... | collective-permute-start | bytes 1769480 | tf_op jit(solution)/shard_map/ppermute | solution.py:618
  553.2 48.8 %collective-permute-start.56 = (bf16[2,144,2048]{2,1,0:T(8,128)(2,1)}, bf16[2,144,2048]{2,1,0:T(8,128)(2,1)}, u32[]{:S(2)}, u32[]{:S(2)}) collective-permute-start(bf16[2,144,2048]{2,1,0:T(8,128)(2,1)} %get-tuple-element.571), channel_id=1, source_target_pairs={{0,8},{4,12},{8,0},{12,4},{1,9},{5,13},{9,1},{13,5},{2,10},{6,14},... | collective-permute-start | bytes 3538952 | tf_op jit(solution)/shard_map/ppermute | solution.py:445
  602.1 201.7 %reduce-scatter.6.cloned.1.call-start = ((), (), s32[]{:S(2)}) async-start(), calls=%async_computation.8 | async-start | bytes 6291456 | tf_op jit(solution)/shard_map/reduce_scatter | solution.py:701
  602.1 37.3 %collective-permute-start.63 = (bf16[2,4,128,2048]{3,2,1,0:T(8,128)(2,1)}, bf16[2,4,128,2048]{3,2,1,0:T(8,128)(2,1)}, u32[]{:S(2)}, u32[]{:S(2)}) collective-permute-start(bf16[2,4,128,2048]{3,2,1,0:T(8,128)(2,1)} %get-tuple-element.401), channel_id=1, source_target_pairs={{0,4},{4,0},{8,12},{12,8},{1,5},{5,1},{9,13},{13,9},{2,6},{6,2},{1... | collective-permute-start | bytes 12582920 | tf_op jit(solution)/shard_map/ppermute | solution.py:445
  609.6 29.8 %collective-permute-start.62 = (bf16[2,1,128,2048]{3,2,1,0:T(8,128)(2,1)S(1)}, bf16[2,1,128,2048]{3,2,1,0:T(8,128)(2,1)}, u32[]{:S(2)}, u32[]{:S(2)}) collective-permute-start(bf16[2,1,128,2048]{3,2,1,0:T(8,128)(2,1)S(1)} %get-tuple-element.564), channel_id=1, source_target_pairs={{0,8},{4,12},{8,0},{12,4},{1,9},{5,13},{9,1},{13,5},{2,10},{6,14},... | collective-permute-start | bytes 3145736 | tf_op jit(solution)/shard_map/ppermute | solution.py:445
  640.3 245.2 %reduce-scatter.8.cloned.1.call-start = ((), (), s32[]{:S(2)}) async-start(), calls=%async_computation.9 | async-start | bytes 6291456 | tf_op jit(solution)/shard_map/reduce_scatter | solution.py:701
  644.4 39.4 %collective-permute-start.66 = (bf16[144,2048]{1,0:T(8,128)(2,1)}, bf16[144,2048]{1,0:T(8,128)(2,1)}, u32[]{:S(2)}, u32[]{:S(2)}) collective-permute-start(bf16[144,2048]{1,0:T(8,128)(2,1)} %fusion.38), channel_id=1, source_target_pairs={{1,2},{2,1},{5,6},{6,5},{9,10},{10,9},{13,14},{14,13},{17,18},{18,... | collective-permute-start | bytes 1769480 | tf_op jit(solution)/shard_map/ppermute | solution.py:638
  646.0 37.7 %collective-permute-start.67 = (bf16[144,2048]{1,0:T(8,128)(2,1)}, bf16[144,2048]{1,0:T(8,128)(2,1)}, u32[]{:S(2)}, u32[]{:S(2)}) collective-permute-start(bf16[144,2048]{1,0:T(8,128)(2,1)} %fusion.38), channel_id=1, source_target_pairs={{0,1},{3,2},{4,5},{7,6},{8,9},{11,10},{12,13},{15,14},{16,17},{19,... | collective-permute-start | bytes 1769480 | tf_op jit(solution)/shard_map/ppermute | solution.py:639
  656.6 30.5 %collective-permute-start.69 = (bf16[2,128,2048]{2,1,0:T(8,128)(2,1)}, bf16[2,128,2048]{2,1,0:T(8,128)(2,1)}, u32[]{:S(2)}, u32[]{:S(2)}) collective-permute-start(bf16[2,128,2048]{2,1,0:T(8,128)(2,1)} %bitcast_convert_fusion), channel_id=1, source_target_pairs={{0,1},{3,2},{4,5},{7,6},{8,9},{11,10},{12,13},{15,14},{16,17},{19,... | collective-permute-start | bytes 3145736 | tf_op jit(solution)/shard_map/ppermute | solution.py:618
  681.6 39.1 %collective-permute-start.76 = (bf16[2,1,128,2048]{3,2,1,0:T(8,128)(2,1)}, bf16[2,1,128,2048]{3,2,1,0:T(8,128)(2,1)}, u32[]{:S(2)}, u32[]{:S(2)}) collective-permute-start(bf16[2,1,128,2048]{3,2,1,0:T(8,128)(2,1)} %get-tuple-element.561), channel_id=1, source_target_pairs={{0,8},{4,12},{8,0},{12,4},{1,9},{5,13},{9,1},{13,5},{2,10},{6,14},... | collective-permute-start | bytes 3145736 | tf_op jit(solution)/shard_map/ppermute | solution.py:445
  683.4 112.0 %collective-permute-start.72 = (bf16[2,1,128,2048]{3,2,1,0:T(8,128)(2,1)}, bf16[2,1,128,2048]{3,2,1,0:T(8,128)(2,1)}, u32[]{:S(2)}, u32[]{:S(2)}) collective-permute-start(bf16[2,1,128,2048]{3,2,1,0:T(8,128)(2,1)} %get-tuple-element.562), channel_id=1, source_target_pairs={{0,8},{4,12},{8,0},{12,4},{1,9},{5,13},{9,1},{13,5},{2,10},{6,14},... | collective-permute-start | bytes 3145736 | tf_op jit(solution)/shard_map/ppermute | solution.py:445
  691.3 29.5 %collective-permute-start.74 = (bf16[144,2048]{1,0:T(8,128)(2,1)}, bf16[144,2048]{1,0:T(8,128)(2,1)}, u32[]{:S(2)}, u32[]{:S(2)}) collective-permute-start(bf16[144,2048]{1,0:T(8,128)(2,1)} %get-tuple-element.554), channel_id=1, source_target_pairs={{1,2},{2,1},{5,6},{6,5},{9,10},{10,9},{13,14},{14,13},{17,18},{18,... | collective-permute-start | bytes 1769480 | tf_op jit(solution)/shard_map/ppermute | solution.py:644
  746.8 48.6 %collective-permute-start.70 = (bf16[2,128,2048]{2,1,0:T(8,128)(2,1)}, bf16[2,128,2048]{2,1,0:T(8,128)(2,1)S(1)}, u32[]{:S(2)}, u32[]{:S(2)}) collective-permute-start(bf16[2,128,2048]{2,1,0:T(8,128)(2,1)} %fusion.22), channel_id=1, source_target_pairs={{1,2},{2,1},{5,6},{6,5},{9,10},{10,9},{13,14},{14,13},{17,18},{18,... | collective-permute-start | bytes 3145736 | tf_op jit(solution)/shard_map/ppermute | solution.py:638
  747.5 47.9 %collective-permute-start.71 = (bf16[2,128,2048]{2,1,0:T(8,128)(2,1)}, bf16[2,128,2048]{2,1,0:T(8,128)(2,1)}, u32[]{:S(2)}, u32[]{:S(2)}) collective-permute-start(bf16[2,128,2048]{2,1,0:T(8,128)(2,1)} %fusion.22), channel_id=1, source_target_pairs={{0,1},{3,2},{4,5},{7,6},{8,9},{11,10},{12,13},{15,14},{16,17},{19,... | collective-permute-start | bytes 3145736 | tf_op jit(solution)/shard_map/ppermute | solution.py:639
  810.0 37.7 %collective-permute-start.81 = (bf16[2,128,2048]{2,1,0:T(8,128)(2,1)S(1)}, bf16[2,128,2048]{2,1,0:T(8,128)(2,1)}, u32[]{:S(2)}, u32[]{:S(2)}) collective-permute-start(bf16[2,128,2048]{2,1,0:T(8,128)(2,1)S(1)} %get-tuple-element.552), channel_id=1, source_target_pairs={{1,2},{2,1},{5,6},{6,5},{9,10},{10,9},{13,14},{14,13},{17,18},{18,... | collective-permute-start | bytes 3145736 | tf_op jit(solution)/shard_map/ppermute | solution.py:644
  811.6 36.1 %collective-permute-start.82 = (bf16[2,128,2048]{2,1,0:T(8,128)(2,1)S(1)}, bf16[2,128,2048]{2,1,0:T(8,128)(2,1)}, u32[]{:S(2)}, u32[]{:S(2)}) collective-permute-start(bf16[2,128,2048]{2,1,0:T(8,128)(2,1)S(1)} %get-tuple-element.551), channel_id=1, source_target_pairs={{0,1},{1,0},{2,3},{3,2},{4,5},{5,4},{6,7},{7,6},{8,9},{9,8},{10,11... | collective-permute-start | bytes 3145736 | tf_op jit(solution)/shard_map/ppermute | solution.py:445
  815.5 32.2 %collective-permute-start.84 = (bf16[2,64,2048]{2,1,0:T(8,128)(2,1)S(1)}, bf16[2,64,2048]{2,1,0:T(8,128)(2,1)S(1)}, u32[]{:S(2)}, u32[]{:S(2)}) collective-permute-start(bf16[2,64,2048]{2,1,0:T(8,128)(2,1)S(1)} %add_convert_fusion.8), channel_id=1, source_target_pairs={{0,1},{3,2},{4,5},{7,6},{8,9},{11,10},{12,13},{15,14},{16,17},{19,... | collective-permute-start | bytes 1572872 | tf_op jit(solution)/shard_map/ppermute | solution.py:500
  822.3 72.0 %collective-permute-start.90 = (bf16[2,2,128,2048]{3,2,1,0:T(8,128)(2,1)}, bf16[2,2,128,2048]{3,2,1,0:T(8,128)(2,1)}, u32[]{:S(2)}, u32[]{:S(2)}) collective-permute-start(bf16[2,2,128,2048]{3,2,1,0:T(8,128)(2,1)} %fusion.19), channel_id=1, source_target_pairs={{0,4},{4,0},{8,12},{12,8},{1,5},{5,1},{9,13},{13,9},{2,6},{6,2},{1... | collective-permute-start | bytes 6291464 | tf_op jit(solution)/shard_map/ppermute | solution.py:445
  854.7 39.6 %collective-permute-start.85 = (bf16[4,64,1664]{2,1,0:T(8,128)(2,1)}, bf16[4,64,1664]{2,1,0:T(8,128)(2,1)}, u32[]{:S(2)}, u32[]{:S(2)}) collective-permute-start(bf16[4,64,1664]{2,1,0:T(8,128)(2,1)} %get-tuple-element.568.refs_2_), channel_id=1, source_target_pairs={{0,16},{16,0},{1,17},{17,1},{2,18},{18,2},{3,19},{19,3},{4,20},{20... | collective-permute-start | bytes 2555912 | tf_op jit(solution)/shard_map/ppermute | solution.py:445
  881.6 50.0 %collective-permute-start.95 = (bf16[4,64,1664]{2,1,0:T(8,128)(2,1)S(1)}, bf16[4,64,1664]{2,1,0:T(8,128)(2,1)}, u32[]{:S(2)}, u32[]{:S(2)}) collective-permute-start(bf16[4,64,1664]{2,1,0:T(8,128)(2,1)S(1)} %get-tuple-element.570.refs_0_), channel_id=1, source_target_pairs={{0,16},{16,0},{1,17},{17,1},{2,18},{18,2},{3,19},{19,3},{4,20},{20... | collective-permute-start | bytes 2555912 | tf_op jit(solution)/shard_map/ppermute | solution.py:445
  (268 other events, 3089.2 us)
Sparse Core Ops, SparseCore 0:
  138.1 64.5 all-gather.2
  258.8 55.1 all-gather.4
  602.2 51.5 reduce-scatter.3
  656.6 54.3 reduce-scatter.5
  713.1 54.3 reduce-scatter.7

commit v4 on v3

--- a/solution.py
+++ b/solution.py
@@ -592,7 +592,8 @@
         lax.ppermute(third_mid, "expert", OUTWARD),
     ]
     second = jnp.where(middle, second_mid, second_end)
-    third_end, y2 = yield [lax.ppermute(second_mid, "expert", OUTWARD), swap(second, "ctx", 2)]
+    (third_end,) = yield [lax.ppermute(second_mid, "expert", OUTWARD)]
+    (y2,) = yield [swap(second, "ctx", 2)]
     third = jnp.where(middle, third_mid, third_end)
     groups[0] = jnp.stack([own, pair, second, third])
     y3, groups[1] = yield [swap(third, "ctx", 2), swap(groups[0], "ctx", 1)]
@@ -851,7 +852,7 @@
     flow_a = Flow(scatter_ctx_steps(out_terms_of(0), sum_a))
     token = turn([flow_a], experts[0][0])
     done = attention(1, token, [])
-    token = turn([flow_a], done)
+    token = turn([flow_a, upstream_flow], done)
     flow_b = Flow(scatter_ctx_steps(out_terms_of(1), sum_b))
 
     normed_two, unit_two, scale_two, gates_own, residuals = [], [], [], [], []

time: 981 us -> 990 us (level)
    ppermute x2, waiting for transfers between devices: 17.1 us -> 31.4 us  [gather_steps(): lax.ppermute(third_mid, 'expert', OUTWARD)]
    unnamed x423 -> x429, local copies, waits for them, and re-layouts: 50.9 us -> 49.6 us
where the time goes in v4:
time: 990 us; the launch traced here: 979 us
  Pallas kernels  275 us (28%)
  waiting for transfers between devices  223 us (23%)
  starting transfers between devices  175 us (18%)
  other arithmetic  143 us (14%)
  local copies, waits for them, and re-layouts  93.4 us (9%)
  matrix products  51.5 us (5%)
  between operations  17.4 us (2%)
    pallas_call x8, Pallas kernels, expert_call(): pl.pallas_call(functools.partial(expert_kernel, capacity, tile_f, tile_d,...  165 us
    ppermute x63, waiting for transfers between devices, swap(): lax.ppermute(value, axis, [(i, i ^ bit) for i in range(lax.axis_size(axis...  134 us
    ppermute x63, starting transfers between devices, swap(): lax.ppermute(value, axis, [(i, i ^ bit) for i in range(lax.axis_size(axis...  78.3 us
    unnamed x429, local copies, waits for them, and re-layouts  49.6 us
    pallas_call x3, Pallas kernels, product_call(): pl.pallas_call(product_kernel, grid=(columns // wide, rows // tile), in_s...  49.2 us
    ppermute x2, waiting for transfers between devices, gather_steps(): lax.ppermute(third_mid, 'expert', OUTWARD)  31.4 us
    dot_general x6, matrix products, dot_t(): lax.dot_general(a, b, (((1,), (1,)), ((), ())), preferred_element_type=F32)  28.4 us
    ppermute x3, starting transfers between devices, scatter_steps(): lax.ppermute(second, 'expert', INWARD)  24.8 us
  transfers between devices with their start and end apart: 106, of which 28 were waited for; matrix products, arithmetic and copies ran while one was open for 22% of the time, Pallas kernels for 28%

profile of v4, /device:TPU:0, one launch (start us, length us, event | category | flops | bytes accessed | tf_op | source)
XLA Modules:
  0.0 978.5 jit_solution(3121546344357479224)
XLA Ops:
  24.0 12.1 %all-to-all-done = bf16[4,64,1664]{2,1,0:T(8,128)(2,1)S(1)} async-done(((bf16[4,64,1664]{2,1,0:T(8,128)(2,1)}), bf16[4,64,1664]{2,1,0:T(8,128)(2,1)S(1)}, u32[]{:S(2)}, u32[]{:S(2)}) %all-to-all-start) | async-done | bytes 852000 | tf_op jit(solution)/shard_map/all_to_all | solution.py:784
  47.2 19.2 %collective-permute-done.refs_0_ = bf16[4,64,2176]{2,1,0:T(8,128)(2,1)} collective-permute-done((bf16[4,64,2176]{2,1,0:T(8,128)(2,1)S(1)}, bf16[4,64,2176]{2,1,0:T(8,128)(2,1)}, u32[]{:S(2)}, u32[]{:S(2)}) %collective-permute-start) | collective-permute-done | bytes 1114144 | tf_op jit(solution)/shard_map/ppermute | solution.py:445
  81.8 14.9 %collective-permute-done.10.refs_5_ = bf16[2,128,2048]{2,1,0:T(8,128)(2,1)S(1)} collective-permute-done((bf16[2,128,2048]{2,1,0:T(8,128)(2,1)}, bf16[2,128,2048]{2,1,0:T(8,128)(2,1)S(1)}, u32[]{:S(2)}, u32[]{:S(2)}) %collective-permute-start.10) | collective-permute-done | bytes 1048608 | tf_op jit(solution)/shard_map/ppermute | solution.py:445
  110.6 17.5 %collective-permute-done.14.refs_3_ = bf16[2,128,2048]{2,1,0:T(8,128)(2,1)S(1)} collective-permute-done((bf16[2,128,2048]{2,1,0:T(8,128)(2,1)}, bf16[2,128,2048]{2,1,0:T(8,128)(2,1)S(1)}, u32[]{:S(2)}, u32[]{:S(2)}) %collective-permute-start.14) | collective-permute-done | bytes 1048608 | tf_op jit(solution)/shard_map/ppermute | solution.py:445
  169.6 6.3 fusion.16.joined_ref
  175.9 8.5 shard_map.264
  200.2 9.4 all-gather.3.cloned.1.call-done.refs_1_.refs_4_.refs_0_
  212.9 6.3 fusion.14.joined_ref
  219.2 8.5 shard_map.266.refs_2_
  247.2 7.5 collective-permute-start.22
  254.6 15.5 %collective-permute-done.25.refs_4_ = bf16[1024,1024]{1,0:T(8,128)(2,1)} collective-permute-done((bf16[1024,1024]{1,0:T(8,128)(2,1)}, bf16[1024,1024]{1,0:T(8,128)(2,1)}, u32[]{:S(2)}, u32[]{:S(2)}) %collective-permute-start.25) | collective-permute-done | bytes 2097184 | tf_op jit(solution)/shard_map/ppermute | solution.py:445
  276.3 31.4 %collective-permute-done.27.refs_1_ = bf16[144,2048]{1,0:T(8,128)(2,1)S(1)} collective-permute-done((bf16[144,2048]{1,0:T(8,128)(2,1)}, bf16[144,2048]{1,0:T(8,128)(2,1)S(1)}, u32[]{:S(2)}, u32[]{:S(2)}) %collective-permute-start.27) | collective-permute-done | bytes 589856 | tf_op jit(solution)/shard_map/ppermute | solution.py:558
  313.7 10.3 %collective-permute-done.31.refs_3_ = bf16[128,2048]{1,0:T(8,128)(2,1)S(1)} collective-permute-done((bf16[128,2048]{1,0:T(8,128)(2,1)}, bf16[128,2048]{1,0:T(8,128)(2,1)S(1)}, u32[]{:S(2)}, u32[]{:S(2)}) %collective-permute-start.31) | collective-permute-done | bytes 524320 | tf_op jit(solution)/shard_map/ppermute | solution.py:445
  339.8 7.3 collective-permute-start.34
  349.5 20.6 %shard_map.271 = (bf16[2,4,128,2048]{3,2,1,0:T(8,128)(2,1)}, bf16[4,144,2048]{2,1,0:T(8,128)(2,1)}, bf16[2560,2048]{1,0:T(8,128)(2,1)}, bf16[2560,2048]{1,0:T(8,...) custom-call(s32[3]{0:T(128)} %pad_add_fusion.1.order_ref, ...), custom_call_target="tpu_custom_call" | custom-call | flops 1000 | bytes 1000 | tf_op jit(solution)/shard_map/pallas_call | solution.py:175
  373.0 20.5 %shard_map.273 = (bf16[2,4,128,2048]{3,2,1,0:T(8,128)(2,1)}, bf16[4,144,2048]{2,1,0:T(8,128)(2,1)}, bf16[2560,2048]{1,0:T(8,128)(2,1)}, bf16[2560,2048]{1,0:T(8,...) custom-call(s32[3]{0:T(128)} %pad_add_fusion.1.order_ref, ...), custom_call_target="tpu_custom_call", output_to_operand_aliasing={{2}: (8, {}), {3}: (9, {}), {4}: (10, {}), {5}: (11, {}), {... | custom-call | flops 1000 | bytes 1000 | tf_op jit(solution)/shard_map/pallas_call | solution.py:175
  398.8 20.7 %shard_map.275 = (bf16[2,4,128,2048]{3,2,1,0:T(8,128)(2,1)}, bf16[4,144,2048]{2,1,0:T(8,128)(2,1)}, bf16[2560,2048]{1,0:T(8,128)(2,1)}, bf16[2560,2048]{1,0:T(8,...) custom-call(s32[3]{0:T(128)} %pad_add_fusion.1.order_ref, ...), custom_call_target="tpu_custom_call", output_to_operand_aliasing={{2}: (8, {}), {3}: (9, {}), {4}: (10, {}), {5}: (11, {}), {... | custom-call | flops 1000 | bytes 1000 | tf_op jit(solution)/shard_map/pallas_call | solution.py:175
  431.2 20.6 %shard_map.277 = (bf16[2,4,128,2048]{3,2,1,0:T(8,128)(2,1)}, bf16[4,144,2048]{2,1,0:T(8,128)(2,1)}, bf16[2560,2048]{1,0:T(8,128)(2,1)}, bf16[2560,2048]{1,0:T(8,...) custom-call(s32[3]{0:T(128)} %pad_add_fusion.1.order_ref, ...), custom_call_target="tpu_custom_call", output_to_operand_aliasing={{2}: (8, {}), {3}: (9, {}), {4}: (10, {}), {5}: (11, {}), {... | custom-call | flops 1000 | bytes 1000 | tf_op jit(solution)/shard_map/pallas_call | solution.py:175
  451.8 5.8 collective-permute-done.45.refs_2_
  463.3 20.7 %shard_map.279 = (bf16[2,4,128,2048]{3,2,1,0:T(8,128)(2,1)}, bf16[4,144,2048]{2,1,0:T(8,128)(2,1)}, bf16[2560,2048]{1,0:T(8,128)(2,1)}, bf16[2560,2048]{1,0:T(8,...) custom-call(s32[3]{0:T(128)} %pad_add_fusion.1.order_ref, ...), custom_call_target="tpu_custom_call", output_to_operand_aliasing={{0}: (8, {}), {2}: (9, {}), {3}: (10, {}), {4}: (11, {}), {... | custom-call | flops 1000 | bytes 1000 | tf_op jit(solution)/shard_map/pallas_call | solution.py:175
  490.6 20.6 %shard_map.281 = (bf16[2,4,128,2048]{3,2,1,0:T(8,128)(2,1)}, bf16[4,144,2048]{2,1,0:T(8,128)(2,1)}, bf16[2560,2048]{1,0:T(8,128)(2,1)}, bf16[2560,2048]{1,0:T(8,...) custom-call(s32[3]{0:T(128)} %pad_add_fusion.1.order_ref, ...), custom_call_target="tpu_custom_call", output_to_operand_aliasing={{0}: (8, {}), {2}: (9, {}), {3}: (10, {}), {4}: (11, {}), {... | custom-call | flops 1000 | bytes 1000 | tf_op jit(solution)/shard_map/pallas_call | solution.py:175
  511.1 6.5 collective-permute-done.50.refs_0_
  519.3 20.7 %shard_map.283 = (bf16[2,4,128,2048]{3,2,1,0:T(8,128)(2,1)}, bf16[4,144,2048]{2,1,0:T(8,128)(2,1)}, bf16[2560,2048]{1,0:T(8,128)(2,1)}, bf16[2560,2048]{1,0:T(8,...) custom-call(s32[3]{0:T(128)} %pad_add_fusion.1.order_ref, ...), custom_call_target="tpu_custom_call", output_to_operand_aliasing={{0}: (8, {}), {2}: (9, {}), {3}: (10, {}), {4}: (11, {}), {... | custom-call | flops 1000 | bytes 1000 | tf_op jit(solution)/shard_map/pallas_call | solution.py:175
  540.0 7.2 collective-permute-done.48.refs_0_
  555.5 7.2 collective-permute-start.52
  563.6 20.6 %shard_map.285 = (bf16[2,4,128,2048]{3,2,1,0:T(8,128)(2,1)}, bf16[4,144,2048]{2,1,0:T(8,128)(2,1)}, bf16[2560,2048]{1,0:T(8,128)(2,1)}, bf16[2560,2048]{1,0:T(8,...) custom-call(s32[3]{0:T(128)} %pad_add_fusion.1.order_ref, ...), custom_call_target="tpu_custom_call", output_to_operand_aliasing={{0}: (8, {}), {2}: (9, {}), {3}: (10, {}), {4}: (11, {}), {... | custom-call | flops 1000 | bytes 1000 | tf_op jit(solution)/shard_map/pallas_call | solution.py:175
  587.3 7.0 collective-permute-start.55
  594.3 17.0 %shard_map.287.refs_5_ = bf16[1024,2048]{1,0:T(8,128)(2,1)} custom-call(bf16[2560,1024]{1,0:T(8,128)(2,1)} %get-tuple-element.394.left_ref, bf16[2560,2048]{1,0:T(8,128)(2,1)} %get-tuple-element.395.right_ref, bf16[144,2048]{1,0:T(8,128)(2,1)} %get-tuple-element.391.refs_0_), custom_call_target="tpu_custom_call" | custom-call | flops 1000 | bytes 1000 | tf_op jit(solution)/shard_map/pallas_call | solution.py:220
  611.6 5.4 add_convert_fusion
  628.1 16.1 %shard_map.289.refs_5_ = bf16[2048,1024]{1,0:T(8,128)(2,1)} custom-call(bf16[2560,2048]{1,0:T(8,128)(2,1)} %get-tuple-element.404.left_ref, bf16[2560,1024]{1,0:T(8,128)(2,1)} %get-tuple-element.405.right_ref, bf16[144,2048]{1,0:T(8,128)(2,1)} %get-tuple-element.397.refs_0_), custom_call_target="tpu_custom_call" | custom-call | flops 1000 | bytes 1000 | tf_op jit(solution)/shard_map/pallas_call | solution.py:220
  655.1 7.4 collective-permute-start.67
  674.2 16.1 %shard_map.291.refs_6_ = bf16[2048,1024]{1,0:T(8,128)(2,1)} custom-call(bf16[2560,2048]{1,0:T(8,128)(2,1)} %get-tuple-element.404.left_ref, bf16[2560,1024]{1,0:T(8,128)(2,1)} %get-tuple-element.411.right_ref, bf16[144,2048]{1,0:T(8,128)(2,1)} %get-tuple-element.408.refs_0_), custom_call_target="tpu_custom_call" | custom-call | flops 1000 | bytes 1000 | tf_op jit(solution)/shard_map/pallas_call | solution.py:220
  717.0 11.2 %shard_map.294 = (bf16[512,1536]{1,0:T(8,128)(2,1)S(1)}, f32[2,128]{1,0:T(2,128)S(1)}) custom-call(f32[512,1536]{1,0:T(8,128)S(1)} %copy-done.9, bf16[512,512]{1,0:T(8,128)(2,1)S(1)} %copy-done.45, f32[512,128]{1,0:T(8,128)S(1)} %copy-done.33, f32[512,128]{1,0:T(8,128)S(1)} %copy-done.25, f32[2,128]{1,0:T(2,128)S(1)} %copy-done.53, s32[512,1]{1,0:T(8,128)S(1)} %copy-done.31, ...), custom_call_target="tpu_custom_call" | custom-call | flops 1000 | bytes 1000 | tf_op jit(solution)/shard_map/pallas_call | solution.py:435
  736.4 7.9 fusion.12.refs_2_
  744.4 5.5 collective-permute-done.77.refs_0_
  756.1 10.4 %collective-permute-start.71 = (bf16[2,128,2048]{2,1,0:T(8,128)(2,1)}, bf16[2,128,2048]{2,1,0:T(8,128)(2,1)}, u32[]{:S(2)}, u32[]{:S(2)}) collective-permute-start(bf16[2,128,2048]{2,1,0:T(8,128)(2,1)} %fusion.22), channel_id=1, source_target_pairs={{0,1},{3,2},{4,5},{7,6},{8,9},{11,10},{12,13},{15,14},{16,17},{19,... | collective-permute-start | bytes 3145736 | tf_op jit(solution)/shard_map/ppermute | solution.py:640
  772.0 11.2 %shard_map.298 = (bf16[512,1536]{1,0:T(8,128)(2,1)S(1)}, f32[2,128]{1,0:T(2,128)S(1)}) custom-call(f32[512,1536]{1,0:T(8,128)S(1)} %copy-done.7, bf16[512,512]{1,0:T(8,128)(2,1)S(1)} %convolution_convert_fusion.2.do_ref, f32[512,128]{1,0:T(8,128)S(1)} %copy-done.35, f32[512,128]{1,0:T(8,128)S(1)} %copy-done.27, f32[2,128]{1,0:T(2,128)S(1)} %copy-done.53, ...), custom_call_target="tpu_custom_call" | custom-call | flops 1000 | bytes 1000 | tf_op jit(solution)/shard_map/pallas_call | solution.py:435
  787.7 9.1 fusion.5
  803.5 8.3 collective-permute-done.80.refs_3_
  812.6 5.4 fusion.20
  831.7 6.1 shard_map.300
  841.2 6.7 shard_map.301
  849.8 5.8 collective-permute-done.84.refs_3_
  864.2 6.0 collective-permute-done.86.refs_0_
  875.8 10.5 %collective-permute-start.89 = (bf16[4,64,1664]{2,1,0:T(8,128)(2,1)}, bf16[4,64,1664]{2,1,0:T(8,128)(2,1)}, u32[]{:S(2)}, u32[]{:S(2)}) collective-permute-start(bf16[4,64,1664]{2,1,0:T(8,128)(2,1)} %fusion.31), channel_id=1, source_target_pairs={{0,1},{3,2},{4,5},{7,6},{8,9},{11,10},{12,13},{15,14},{16,17},{19,... | collective-permute-start | bytes 2555912 | tf_op jit(solution)/shard_map/ppermute | solution.py:514
  916.2 7.2 collective-permute-done.93.refs_2_
  927.9 5.0 collective-permute-start.97
  954.4 9.5 all-to-all-done.1.payload_ref
  (835 shorter events, 400.2 us)
Async XLA Ops:
  8.5 37.5 %collective-permute-start.3 = (bf16[2,128,2048]{2,1,0:T(8,128)(2,1)S(1)}, bf16[2,128,2048]{2,1,0:T(8,128)(2,1)}, u32[]{:S(2)}, u32[]{:S(2)}) collective-permute-start(bf16[2,128,2048]{2,1,0:T(8,128)(2,1)S(1)} %bitcast.487), channel_id=1, source_target_pairs={{0,1},{1,0},{2,3},{3,2},{4,5},{5,4},{6,7},{7,6},{8,9},{9,8},{10,11... | collective-permute-start | bytes 3145736 | tf_op jit(solution)/shard_map/ppermute | solution.py:445
  11.6 35.5 %collective-permute-start.4 = (bf16[2,128,2048]{2,1,0:T(8,128)(2,1)S(1)}, bf16[2,128,2048]{2,1,0:T(8,128)(2,1)}, u32[]{:S(2)}, u32[]{:S(2)}) collective-permute-start(bf16[2,128,2048]{2,1,0:T(8,128)(2,1)S(1)} %bitcast.488), channel_id=1, source_target_pairs={{1,2},{2,1},{5,6},{6,5},{9,10},{10,9},{13,14},{14,13},{17,18},{18,... | collective-permute-start | bytes 3145736 | tf_op jit(solution)/shard_map/ppermute | solution.py:585
  23.8 185.8 %all-gather.3.cloned.1.call-start = ((), (), s32[]{:S(2)}) async-start(), calls=%async_computation.5 | async-start | bytes 6291456 | tf_op jit(solution)/shard_map/all_gather | solution.py:799
  47.1 34.7 %collective-permute-start.9 = (bf16[2,128,2048]{2,1,0:T(8,128)(2,1)}, bf16[2,128,2048]{2,1,0:T(8,128)(2,1)}, u32[]{:S(2)}, u32[]{:S(2)}) collective-permute-start(bf16[2,128,2048]{2,1,0:T(8,128)(2,1)} %bitcast.7), channel_id=1, source_target_pairs={{0,4},{4,0},{8,12},{12,8},{1,5},{5,1},{9,13},{13,9},{2,6},{6,2},{1... | collective-permute-start | bytes 3145736 | tf_op jit(solution)/shard_map/ppermute | solution.py:445
  100.5 30.4 %collective-permute-start.11 = (bf16[4,64,2176]{2,1,0:T(8,128)(2,1)}, bf16[4,64,2176]{2,1,0:T(8,128)(2,1)S(1)}, u32[]{:S(2)}, u32[]{:S(2)}) collective-permute-start(bf16[4,64,2176]{2,1,0:T(8,128)(2,1)} %get-tuple-element.242.refs_4_), channel_id=1, source_target_pairs={{1,0},{2,3},{5,4},{6,7},{9,8},{10,11},{13,12},{14,15},{17,16},{18,... | collective-permute-start | bytes 3342344 | tf_op jit(solution)/shard_map/ppermute | solution.py:486
  108.9 47.7 %collective-permute-start.16 = (bf16[2,128,2048]{2,1,0:T(8,128)(2,1)}, bf16[2,128,2048]{2,1,0:T(8,128)(2,1)}, u32[]{:S(2)}, u32[]{:S(2)}) collective-permute-start(bf16[2,128,2048]{2,1,0:T(8,128)(2,1)} %get-tuple-element.244), channel_id=1, source_target_pairs={{1,2},{2,1},{5,6},{6,5},{9,10},{10,9},{13,14},{14,13},{17,18},{18,... | collective-permute-start | bytes 3145736 | tf_op jit(solution)/shard_map/ppermute | solution.py:591
  128.1 28.5 %collective-permute-start.17 = (bf16[2,128,2048]{2,1,0:T(8,128)(2,1)}, bf16[2,128,2048]{2,1,0:T(8,128)(2,1)}, u32[]{:S(2)}, u32[]{:S(2)}) collective-permute-start(bf16[2,128,2048]{2,1,0:T(8,128)(2,1)} %get-tuple-element.250), channel_id=1, source_target_pairs={{1,0},{2,3},{5,4},{6,7},{9,8},{10,11},{13,12},{14,15},{17,16},{18,... | collective-permute-start | bytes 3145736 | tf_op jit(solution)/shard_map/ppermute | solution.py:592
  145.2 168.4 %all-gather.5.cloned.1.call-start = ((), (), s32[]{:S(2)}) async-start(), calls=%async_computation.6 | async-start | bytes 6291456 | tf_op jit(solution)/shard_map/all_gather | solution.py:799
  192.5 77.6 %collective-permute-start.25 = (bf16[1024,1024]{1,0:T(8,128)(2,1)}, bf16[1024,1024]{1,0:T(8,128)(2,1)}, u32[]{:S(2)}, u32[]{:S(2)}) collective-permute-start(bf16[1024,1024]{1,0:T(8,128)(2,1)} %shard_map.261.refs_5_), channel_id=1, source_target_pairs={{0,16},{16,0},{1,17},{17,1},{2,18},{18,2},{3,19},{19,3},{4,20},{20... | collective-permute-start | bytes 6291464 | tf_op jit(solution)/shard_map/ppermute | solution.py:445
  195.1 534.8 %reduce-scatter.4.cloned.1.call-start = ((), (), s32[]{:S(2)}) async-start(), calls=%async_computation.7 | async-start | bytes 6291456 | tf_op jit(solution)/shard_map/reduce_scatter | solution.py:702
  195.2 35.6 %collective-permute-start.20 = (bf16[2,128,2048]{2,1,0:T(8,128)(2,1)}, bf16[2,128,2048]{2,1,0:T(8,128)(2,1)}, u32[]{:S(2)}, u32[]{:S(2)}) collective-permute-start(bf16[2,128,2048]{2,1,0:T(8,128)(2,1)} %get-tuple-element.252), channel_id=1, source_target_pairs={{1,0},{2,3},{5,4},{6,7},{9,8},{10,11},{13,12},{14,15},{17,16},{18,... | collective-permute-start | bytes 3145736 | tf_op jit(solution)/shard_map/ppermute | solution.py:595
  199.0 72.6 %collective-permute-start.24 = (bf16[2,128,2048]{2,1,0:T(8,128)(2,1)}, bf16[2,128,2048]{2,1,0:T(8,128)(2,1)}, u32[]{:S(2)}, u32[]{:S(2)}) collective-permute-start(bf16[2,128,2048]{2,1,0:T(8,128)(2,1)} %broadcast_select_fusion.3), channel_id=1, source_target_pairs={{0,8},{4,12},{8,0},{12,4},{1,9},{5,13},{9,1},{13,5},{2,10},{6,14},... | collective-permute-start | bytes 3145736 | tf_op jit(solution)/shard_map/ppermute | solution.py:445
  230.7 40.9 %collective-permute-start.21 = (bf16[2,128,2048]{2,1,0:T(8,128)(2,1)}, bf16[2,128,2048]{2,1,0:T(8,128)(2,1)S(1)}, u32[]{:S(2)}, u32[]{:S(2)}) collective-permute-start(bf16[2,128,2048]{2,1,0:T(8,128)(2,1)} %bitcast.55), channel_id=1, source_target_pairs={{0,4},{4,0},{8,12},{12,8},{1,5},{5,1},{9,13},{13,9},{2,6},{6,2},{1... | collective-permute-start | bytes 3145736 | tf_op jit(solution)/shard_map/ppermute | solution.py:445
  243.5 80.5 %collective-permute-start.30 = (bf16[4,2,128,2048]{3,2,1,0:T(8,128)(2,1)}, bf16[4,2,128,2048]{3,2,1,0:T(8,128)(2,1)}, u32[]{:S(2)}, u32[]{:S(2)}) collective-permute-start(bf16[4,2,128,2048]{3,2,1,0:T(8,128)(2,1)} %pad_maximum_fusion.1.up_ref), channel_id=1, source_target_pairs={{0,4},{4,0},{8,12},{12,8},{1,5},{5,1},{9,13},{13,9},{2,6},{6,2},{1... | collective-permute-start | bytes 12582920 | tf_op jit(solution)/shard_map/ppermute | solution.py:445
  273.5 34.3 %collective-permute-start.27 = (bf16[144,2048]{1,0:T(8,128)(2,1)}, bf16[144,2048]{1,0:T(8,128)(2,1)S(1)}, u32[]{:S(2)}, u32[]{:S(2)}) collective-permute-start(bf16[144,2048]{1,0:T(8,128)(2,1)} %get-tuple-element.256), channel_id=1, source_target_pairs={{1,0},{2,3},{5,4},{6,7},{9,8},{10,11},{13,12},{14,15},{17,16},{18,... | collective-permute-start | bytes 1769480 | tf_op jit(solution)/shard_map/ppermute | solution.py:558
  274.8 38.9 %collective-permute-start.29 = (bf16[2,128,2048]{2,1,0:T(8,128)(2,1)}, bf16[2,128,2048]{2,1,0:T(8,128)(2,1)S(1)}, u32[]{:S(2)}, u32[]{:S(2)}) collective-permute-start(bf16[2,128,2048]{2,1,0:T(8,128)(2,1)} %copy-done.107), channel_id=1, source_target_pairs={{0,8},{4,12},{8,0},{12,4},{1,9},{5,13},{9,1},{13,5},{2,10},{6,14},... | collective-permute-start | bytes 3145736 | tf_op jit(solution)/shard_map/ppermute | solution.py:445
  328.9 41.3 %collective-permute-start.33 = (bf16[4,2,128,2048]{3,2,1,0:T(8,128)(2,1)}, bf16[4,2,128,2048]{3,2,1,0:T(8,128)(2,1)}, u32[]{:S(2)}, u32[]{:S(2)}) collective-permute-start(bf16[4,2,128,2048]{3,2,1,0:T(8,128)(2,1)} %pad_maximum_fusion.2.up_ref), channel_id=1, source_target_pairs={{0,4},{4,0},{8,12},{12,8},{1,5},{5,1},{9,13},{13,9},{2,6},{6,2},{1... | collective-permute-start | bytes 12582920 | tf_op jit(solution)/shard_map/ppermute | solution.py:445
  331.8 38.3 %collective-permute-start.32 = (bf16[4,144,2048]{2,1,0:T(8,128)(2,1)}, bf16[4,144,2048]{2,1,0:T(8,128)(2,1)}, u32[]{:S(2)}, u32[]{:S(2)}) collective-permute-start(bf16[4,144,2048]{2,1,0:T(8,128)(2,1)} %pad_maximum_fusion.3.norm_ref), channel_id=1, source_target_pairs={{0,4},{4,0},{8,12},{12,8},{1,5},{5,1},{9,13},{13,9},{2,6},{6,2},{1... | collective-permute-start | bytes 7077896 | tf_op jit(solution)/shard_map/ppermute | solution.py:445
  331.8 61.7 %collective-permute-start.36 = (bf16[4,144,2048]{2,1,0:T(8,128)(2,1)}, bf16[4,144,2048]{2,1,0:T(8,128)(2,1)S(1)}, u32[]{:S(2)}, u32[]{:S(2)}) collective-permute-start(bf16[4,144,2048]{2,1,0:T(8,128)(2,1)} %pad_maximum_fusion.3.norm_ref), channel_id=1, source_target_pairs={{0,8},{4,12},{8,0},{12,4},{1,9},{5,13},{9,1},{13,5},{2,10},{6,14},... | collective-permute-start | bytes 7077896 | tf_op jit(solution)/shard_map/ppermute | solution.py:445
  339.8 30.3 %collective-permute-start.34 = (bf16[144,2048]{1,0:T(8,128)(2,1)}, bf16[144,2048]{1,0:T(8,128)(2,1)S(1)}, u32[]{:S(2)}, u32[]{:S(2)}) collective-permute-start(bf16[144,2048]{1,0:T(8,128)(2,1)} %get-tuple-element.591), channel_id=1, source_target_pairs={{0,1},{1,0},{2,3},{3,2},{4,5},{5,4},{6,7},{7,6},{8,9},{9,8},{10,11... | collective-permute-start | bytes 1769480 | tf_op jit(solution)/shard_map/ppermute | solution.py:445
  395.1 28.6 %collective-permute-start.39 = (bf16[4,144,2048]{2,1,0:T(8,128)(2,1)}, bf16[4,144,2048]{2,1,0:T(8,128)(2,1)S(1)}, u32[]{:S(2)}, u32[]{:S(2)}) collective-permute-start(bf16[4,144,2048]{2,1,0:T(8,128)(2,1)} %get-tuple-element.292.norm_ref.refs_4_), channel_id=1, source_target_pairs={{0,4},{4,0},{8,12},{12,8},{1,5},{5,1},{9,13},{13,9},{2,6},{6,2},{1... | collective-permute-start | bytes 7077896 | tf_op jit(solution)/shard_map/ppermute | solution.py:445
  429.0 28.6 %collective-permute-start.43 = (bf16[4,144,2048]{2,1,0:T(8,128)(2,1)S(1)}, bf16[4,144,2048]{2,1,0:T(8,128)(2,1)S(1)}, u32[]{:S(2)}, u32[]{:S(2)}) collective-permute-start(bf16[4,144,2048]{2,1,0:T(8,128)(2,1)S(1)} %pad_maximum_fusion.4.norm_ref), channel_id=1, source_target_pairs={{0,4},{4,0},{8,12},{12,8},{1,5},{5,1},{9,13},{13,9},{2,6},{6,2},{1... | collective-permute-start | bytes 7077896 | tf_op jit(solution)/shard_map/ppermute | solution.py:445
  490.6 49.5 %collective-permute-start.49 = (bf16[4,144,2048]{2,1,0:T(8,128)(2,1)}, bf16[4,144,2048]{2,1,0:T(8,128)(2,1)S(1)}, u32[]{:S(2)}, u32[]{:S(2)}) collective-permute-start(bf16[4,144,2048]{2,1,0:T(8,128)(2,1)} %get-tuple-element.343), channel_id=1, source_target_pairs={{0,4},{4,0},{8,12},{12,8},{1,5},{5,1},{9,13},{13,9},{2,6},{6,2},{1... | collective-permute-start | bytes 7077896 | tf_op jit(solution)/shard_map/ppermute | solution.py:445
  518.6 28.6 %collective-permute-start.51 = (bf16[4,144,2048]{2,1,0:T(8,128)(2,1)}, bf16[4,144,2048]{2,1,0:T(8,128)(2,1)}, u32[]{:S(2)}, u32[]{:S(2)}) collective-permute-start(bf16[4,144,2048]{2,1,0:T(8,128)(2,1)} %get-tuple-element.358), channel_id=1, source_target_pairs={{0,4},{4,0},{8,12},{12,8},{1,5},{5,1},{9,13},{13,9},{2,6},{6,2},{1... | collective-permute-start | bytes 7077896 | tf_op jit(solution)/shard_map/ppermute | solution.py:445
  518.6 28.6 %collective-permute-start.48 = (bf16[2,144,2048]{2,1,0:T(8,128)(2,1)}, bf16[2,144,2048]{2,1,0:T(8,128)(2,1)S(1)}, u32[]{:S(2)}, u32[]{:S(2)}) collective-permute-start(bf16[2,144,2048]{2,1,0:T(8,128)(2,1)} %get-tuple-element.575), channel_id=1, source_target_pairs={{0,8},{4,12},{8,0},{12,4},{1,9},{5,13},{9,1},{13,5},{2,10},{6,14},... | collective-permute-start | bytes 3538952 | tf_op jit(solution)/shard_map/ppermute | solution.py:445
  519.1 92.3 %collective-permute-start.58 = (bf16[2,4,128,2048]{3,2,1,0:T(8,128)(2,1)}, bf16[2,4,128,2048]{3,2,1,0:T(8,128)(2,1)}, u32[]{:S(2)}, u32[]{:S(2)}) collective-permute-start(bf16[2,4,128,2048]{3,2,1,0:T(8,128)(2,1)} %get-tuple-element.393), channel_id=1, source_target_pairs={{0,4},{4,0},{8,12},{12,8},{1,5},{5,1},{9,13},{13,9},{2,6},{6,2},{1... | collective-permute-start | bytes 12582920 | tf_op jit(solution)/shard_map/ppermute | solution.py:445
  548.3 63.1 %collective-permute-start.57 = (bf16[4,144,2048]{2,1,0:T(8,128)(2,1)}, bf16[4,144,2048]{2,1,0:T(8,128)(2,1)}, u32[]{:S(2)}, u32[]{:S(2)}) collective-permute-start(bf16[4,144,2048]{2,1,0:T(8,128)(2,1)} %get-tuple-element.392), channel_id=1, source_target_pairs={{0,4},{4,0},{8,12},{12,8},{1,5},{5,1},{9,13},{13,9},{2,6},{6,2},{1... | collective-permute-start | bytes 7077896 | tf_op jit(solution)/shard_map/ppermute | solution.py:445
  553.0 31.2 %collective-permute-start.53 = (bf16[2,144,2048]{2,1,0:T(8,128)(2,1)S(1)}, bf16[2,144,2048]{2,1,0:T(8,128)(2,1)}, u32[]{:S(2)}, u32[]{:S(2)}) collective-permute-start(bf16[2,144,2048]{2,1,0:T(8,128)(2,1)S(1)} %get-tuple-element.574), channel_id=1, source_target_pairs={{0,8},{4,12},{8,0},{12,4},{1,9},{5,13},{9,1},{13,5},{2,10},{6,14},... | collective-permute-start | bytes 3538952 | tf_op jit(solution)/shard_map/ppermute | solution.py:445
  555.5 28.7 %collective-permute-start.52 = (bf16[144,2048]{1,0:T(8,128)(2,1)S(1)}, bf16[144,2048]{1,0:T(8,128)(2,1)}, u32[]{:S(2)}, u32[]{:S(2)}) collective-permute-start(bf16[144,2048]{1,0:T(8,128)(2,1)S(1)} %bitcast_convert_fusion.2), channel_id=1, source_target_pairs={{0,1},{3,2},{4,5},{7,6},{8,9},{11,10},{12,13},{15,14},{16,17},{19,... | collective-permute-start | bytes 1769480 | tf_op jit(solution)/shard_map/ppermute | solution.py:619
  562.7 48.6 %collective-permute-start.56 = (bf16[2,144,2048]{2,1,0:T(8,128)(2,1)}, bf16[2,144,2048]{2,1,0:T(8,128)(2,1)}, u32[]{:S(2)}, u32[]{:S(2)}) collective-permute-start(bf16[2,144,2048]{2,1,0:T(8,128)(2,1)} %get-tuple-element.573), channel_id=1, source_target_pairs={{0,8},{4,12},{8,0},{12,4},{1,9},{5,13},{9,1},{13,5},{2,10},{6,14},... | collective-permute-start | bytes 3538952 | tf_op jit(solution)/shard_map/ppermute | solution.py:445
  611.4 200.4 %reduce-scatter.6.cloned.1.call-start = ((), (), s32[]{:S(2)}) async-start(), calls=%async_computation.8 | async-start | bytes 6291456 | tf_op jit(solution)/shard_map/reduce_scatter | solution.py:702
  611.5 37.0 %collective-permute-start.63 = (bf16[2,4,128,2048]{3,2,1,0:T(8,128)(2,1)}, bf16[2,4,128,2048]{3,2,1,0:T(8,128)(2,1)}, u32[]{:S(2)}, u32[]{:S(2)}) collective-permute-start(bf16[2,4,128,2048]{3,2,1,0:T(8,128)(2,1)} %get-tuple-element.403), channel_id=1, source_target_pairs={{0,4},{4,0},{8,12},{12,8},{1,5},{5,1},{9,13},{13,9},{2,6},{6,2},{1... | collective-permute-start | bytes 12582920 | tf_op jit(solution)/shard_map/ppermute | solution.py:445
  618.7 29.7 %collective-permute-start.62 = (bf16[2,1,128,2048]{3,2,1,0:T(8,128)(2,1)S(1)}, bf16[2,1,128,2048]{3,2,1,0:T(8,128)(2,1)}, u32[]{:S(2)}, u32[]{:S(2)}) collective-permute-start(bf16[2,1,128,2048]{3,2,1,0:T(8,128)(2,1)S(1)} %get-tuple-element.566), channel_id=1, source_target_pairs={{0,8},{4,12},{8,0},{12,4},{1,9},{5,13},{9,1},{13,5},{2,10},{6,14},... | collective-permute-start | bytes 3145736 | tf_op jit(solution)/shard_map/ppermute | solution.py:445
  649.3 244.1 %reduce-scatter.8.cloned.1.call-start = ((), (), s32[]{:S(2)}) async-start(), calls=%async_computation.9 | async-start | bytes 6291456 | tf_op jit(solution)/shard_map/reduce_scatter | solution.py:702
  653.4 38.9 %collective-permute-start.66 = (bf16[144,2048]{1,0:T(8,128)(2,1)}, bf16[144,2048]{1,0:T(8,128)(2,1)}, u32[]{:S(2)}, u32[]{:S(2)}) collective-permute-start(bf16[144,2048]{1,0:T(8,128)(2,1)} %fusion.38), channel_id=1, source_target_pairs={{1,2},{2,1},{5,6},{6,5},{9,10},{10,9},{13,14},{14,13},{17,18},{18,... | collective-permute-start | bytes 1769480 | tf_op jit(solution)/shard_map/ppermute | solution.py:639
  655.1 37.3 %collective-permute-start.67 = (bf16[144,2048]{1,0:T(8,128)(2,1)}, bf16[144,2048]{1,0:T(8,128)(2,1)}, u32[]{:S(2)}, u32[]{:S(2)}) collective-permute-start(bf16[144,2048]{1,0:T(8,128)(2,1)} %fusion.38), channel_id=1, source_target_pairs={{0,1},{3,2},{4,5},{7,6},{8,9},{11,10},{12,13},{15,14},{16,17},{19,... | collective-permute-start | bytes 1769480 | tf_op jit(solution)/shard_map/ppermute | solution.py:640
  666.0 30.1 %collective-permute-start.69 = (bf16[2,128,2048]{2,1,0:T(8,128)(2,1)}, bf16[2,128,2048]{2,1,0:T(8,128)(2,1)}, u32[]{:S(2)}, u32[]{:S(2)}) collective-permute-start(bf16[2,128,2048]{2,1,0:T(8,128)(2,1)} %bitcast_convert_fusion), channel_id=1, source_target_pairs={{0,1},{3,2},{4,5},{7,6},{8,9},{11,10},{12,13},{15,14},{16,17},{19,... | collective-permute-start | bytes 3145736 | tf_op jit(solution)/shard_map/ppermute | solution.py:619
  690.3 39.7 %collective-permute-start.76 = (bf16[2,1,128,2048]{3,2,1,0:T(8,128)(2,1)}, bf16[2,1,128,2048]{3,2,1,0:T(8,128)(2,1)}, u32[]{:S(2)}, u32[]{:S(2)}) collective-permute-start(bf16[2,1,128,2048]{3,2,1,0:T(8,128)(2,1)} %get-tuple-element.563), channel_id=1, source_target_pairs={{0,8},{4,12},{8,0},{12,4},{1,9},{5,13},{9,1},{13,5},{2,10},{6,14},... | collective-permute-start | bytes 3145736 | tf_op jit(solution)/shard_map/ppermute | solution.py:445
  691.9 111.6 %collective-permute-start.72 = (bf16[2,1,128,2048]{3,2,1,0:T(8,128)(2,1)}, bf16[2,1,128,2048]{3,2,1,0:T(8,128)(2,1)}, u32[]{:S(2)}, u32[]{:S(2)}) collective-permute-start(bf16[2,1,128,2048]{3,2,1,0:T(8,128)(2,1)} %get-tuple-element.564), channel_id=1, source_target_pairs={{0,8},{4,12},{8,0},{12,4},{1,9},{5,13},{9,1},{13,5},{2,10},{6,14},... | collective-permute-start | bytes 3145736 | tf_op jit(solution)/shard_map/ppermute | solution.py:445
  700.0 30.0 %collective-permute-start.74 = (bf16[144,2048]{1,0:T(8,128)(2,1)}, bf16[144,2048]{1,0:T(8,128)(2,1)}, u32[]{:S(2)}, u32[]{:S(2)}) collective-permute-start(bf16[144,2048]{1,0:T(8,128)(2,1)} %get-tuple-element.556), channel_id=1, source_target_pairs={{1,2},{2,1},{5,6},{6,5},{9,10},{10,9},{13,14},{14,13},{17,18},{18,... | collective-permute-start | bytes 1769480 | tf_op jit(solution)/shard_map/ppermute | solution.py:645
  755.4 48.1 %collective-permute-start.70 = (bf16[2,128,2048]{2,1,0:T(8,128)(2,1)}, bf16[2,128,2048]{2,1,0:T(8,128)(2,1)S(1)}, u32[]{:S(2)}, u32[]{:S(2)}) collective-permute-start(bf16[2,128,2048]{2,1,0:T(8,128)(2,1)} %fusion.22), channel_id=1, source_target_pairs={{1,2},{2,1},{5,6},{6,5},{9,10},{10,9},{13,14},{14,13},{17,18},{18,... | collective-permute-start | bytes 3145736 | tf_op jit(solution)/shard_map/ppermute | solution.py:639
  756.1 47.4 %collective-permute-start.71 = (bf16[2,128,2048]{2,1,0:T(8,128)(2,1)}, bf16[2,128,2048]{2,1,0:T(8,128)(2,1)}, u32[]{:S(2)}, u32[]{:S(2)}) collective-permute-start(bf16[2,128,2048]{2,1,0:T(8,128)(2,1)} %fusion.22), channel_id=1, source_target_pairs={{0,1},{3,2},{4,5},{7,6},{8,9},{11,10},{12,13},{15,14},{16,17},{19,... | collective-permute-start | bytes 3145736 | tf_op jit(solution)/shard_map/ppermute | solution.py:640
  818.0 37.6 %collective-permute-start.81 = (bf16[2,128,2048]{2,1,0:T(8,128)(2,1)S(1)}, bf16[2,128,2048]{2,1,0:T(8,128)(2,1)}, u32[]{:S(2)}, u32[]{:S(2)}) collective-permute-start(bf16[2,128,2048]{2,1,0:T(8,128)(2,1)S(1)} %get-tuple-element.554), channel_id=1, source_target_pairs={{1,2},{2,1},{5,6},{6,5},{9,10},{10,9},{13,14},{14,13},{17,18},{18,... | collective-permute-start | bytes 3145736 | tf_op jit(solution)/shard_map/ppermute | solution.py:645
  819.6 36.0 %collective-permute-start.82 = (bf16[2,128,2048]{2,1,0:T(8,128)(2,1)S(1)}, bf16[2,128,2048]{2,1,0:T(8,128)(2,1)}, u32[]{:S(2)}, u32[]{:S(2)}) collective-permute-start(bf16[2,128,2048]{2,1,0:T(8,128)(2,1)S(1)} %get-tuple-element.553), channel_id=1, source_target_pairs={{0,1},{1,0},{2,3},{3,2},{4,5},{5,4},{6,7},{7,6},{8,9},{9,8},{10,11... | collective-permute-start | bytes 3145736 | tf_op jit(solution)/shard_map/ppermute | solution.py:445
  823.6 32.0 %collective-permute-start.84 = (bf16[2,64,2048]{2,1,0:T(8,128)(2,1)S(1)}, bf16[2,64,2048]{2,1,0:T(8,128)(2,1)S(1)}, u32[]{:S(2)}, u32[]{:S(2)}) collective-permute-start(bf16[2,64,2048]{2,1,0:T(8,128)(2,1)S(1)} %add_convert_fusion.8), channel_id=1, source_target_pairs={{0,1},{3,2},{4,5},{7,6},{8,9},{11,10},{12,13},{15,14},{16,17},{19,... | collective-permute-start | bytes 1572872 | tf_op jit(solution)/shard_map/ppermute | solution.py:500
  830.3 72.0 %collective-permute-start.90 = (bf16[2,2,128,2048]{3,2,1,0:T(8,128)(2,1)}, bf16[2,2,128,2048]{3,2,1,0:T(8,128)(2,1)}, u32[]{:S(2)}, u32[]{:S(2)}) collective-permute-start(bf16[2,2,128,2048]{3,2,1,0:T(8,128)(2,1)} %fusion.19), channel_id=1, source_target_pairs={{0,4},{4,0},{8,12},{12,8},{1,5},{5,1},{9,13},{13,9},{2,6},{6,2},{1... | collective-permute-start | bytes 6291464 | tf_op jit(solution)/shard_map/ppermute | solution.py:445
  863.9 38.3 %collective-permute-start.85 = (bf16[4,64,1664]{2,1,0:T(8,128)(2,1)}, bf16[4,64,1664]{2,1,0:T(8,128)(2,1)}, u32[]{:S(2)}, u32[]{:S(2)}) collective-permute-start(bf16[4,64,1664]{2,1,0:T(8,128)(2,1)} %get-tuple-element.570.refs_2_), channel_id=1, source_target_pairs={{0,16},{16,0},{1,17},{17,1},{2,18},{18,2},{3,19},{19,3},{4,20},{20... | collective-permute-start | bytes 2555912 | tf_op jit(solution)/shard_map/ppermute | solution.py:445
  890.8 49.9 %collective-permute-start.95 = (bf16[4,64,1664]{2,1,0:T(8,128)(2,1)S(1)}, bf16[4,64,1664]{2,1,0:T(8,128)(2,1)}, u32[]{:S(2)}, u32[]{:S(2)}) collective-permute-start(bf16[4,64,1664]{2,1,0:T(8,128)(2,1)S(1)} %get-tuple-element.572.refs_0_), channel_id=1, source_target_pairs={{0,16},{16,0},{1,17},{17,1},{2,18},{18,2},{3,19},{19,3},{4,20},{20... | collective-permute-start | bytes 2555912 | tf_op jit(solution)/shard_map/ppermute | solution.py:445
  (271 other events, 3117.2 us)
Sparse Core Ops, SparseCore 0:
  145.4 64.1 all-gather.2
  211.1 81.9 all-gather.4
  611.6 52.6 reduce-scatter.3
  667.0 54.3 reduce-scatter.5
  723.5 54.2 reduce-scatter.7
